TPU v7x, 512 devices: a whole 4x8x8 slice. The times are simulated.
512 devices in a mesh: slab: 128 (over z, y, core), coil: 4 (over x).
Axes of the slice: x: 4, y: 8, z: 8, core: 2. Of those that a mesh axis runs over, the one named last changes fastest.
Arguments:
- iterate: float32 [2, 4, 4, 384, 384], P(None, 'coil', None, 'slab'), may hold values from -6 to 6
- residual: float32 [2, 4, 4, 384, 384], P(None, 'coil', None, 'slab'), may hold values from -50 to 50
- direction: float32 [2, 4, 4, 384, 384], P(None, 'coil', None, 'slab'), may hold values from -50 to 50
- sensitivity: bfloat16 [2, 32, 4, 384, 384], P(None, 'coil', None, 'slab'), may hold values from -0.75 to 0.75
- sampling: int32 [4, 384, 384], replicated, may hold values from 0 to 1
- edge_weight: int32 [4, 4, 384, 384], P('coil', None, 'slab'), may hold values from 1 to 4
Outputs:
- new_iterate: float32 [2, 4, 4, 384, 384], P(None, 'coil', None, 'slab')
- new_residual: float32 [2, 4, 4, 384, 384], P(None, 'coil', None, 'slab')
- new_direction: float32 [2, 4, 4, 384, 384], P(None, 'coil', None, 'slab')
- new_norm: float32 [], replicated
All inputs are finite; a program needn't handle non-finite values.
Results may differ from a plain program's by a relative error of at most 0.0013.
Values sent between devices are 32-bit elements; how exact they have to be, the bound alone decides.
No kernel may reach another device: no remote copies, remote signals or barrier semaphores. Data moves between devices by JAX's collectives and lax.ppermute only.
A program may use at most 64 MiB of HBM per device.

v0:
```python
import functools
import math

import jax
import jax.numpy as jnp
import ml_dtypes
import numpy as np
from jax import lax
from jax.experimental import pallas as pl
from jax.experimental.pallas import tpu as pltpu
from jax.sharding import Mesh
from jax.sharding import PartitionSpec as P

smooth_scale = 0.05
slab_axes = ("z", "y", "core")
f32 = jnp.float32
bf16 = jnp.bfloat16

first_rows = 18
second_rows = 20


def dft_tables(length):
    counter = np.arange(length, dtype=np.int64)
    phases = (counter[:, None] * counter[None, :]) % length
    angles = phases.astype(np.float32) * np.float32(2.0 * math.pi / length)
    unit_norm = np.float32(1.0 / math.sqrt(length))
    wide = angles.astype(np.float64)
    cos = np.cos(wide).astype(np.float32) * unit_norm
    sin = np.sin(wide).astype(np.float32) * unit_norm
    return cos.astype(ml_dtypes.bfloat16), sin.astype(ml_dtypes.bfloat16)


def split(values):
    upper = values.astype(bf16)
    return upper, (values - upper.astype(f32)).astype(bf16)


def mm(a, b, contract):
    return lax.dot_general(a, b, (contract, ((), ())), preferred_element_type=f32)


def sens_rows(sens_ref, part, row, coils):
    pieces = [sens_ref[part, c, row].astype(f32) for c in range(coils)]
    return jnp.concatenate(pieces, axis=0)


def images_kernel(sens_ref, field_ref, table_ref, out_ref):
    coils, rows = sens_ref.shape[1], sens_ref.shape[2]
    frames = field_ref.shape[0]
    table = table_ref[...]
    table = jnp.concatenate([table, table], axis=1)
    half = table.shape[0] // 2
    for r in range(rows):
        s_re = sens_rows(sens_ref, 0, r, coils)
        s_im = sens_rows(sens_ref, 1, r, coils)
        real, imag = [], []
        for f in range(frames):
            d_re = jnp.concatenate([field_ref[f, 0, r]] * coils, axis=0)
            d_im = jnp.concatenate([field_ref[f, 1, r]] * coils, axis=0)
            real.append(s_re * d_re - s_im * d_im)
            imag.append(s_re * d_im + s_im * d_re)
        upper, lower = split(jnp.concatenate(real + imag, axis=0))
        got = mm(table, jnp.concatenate([upper, lower], axis=1), ((1,), (1,)))
        re = got[:half, :128] + got[half:, 128:]
        im = got[:half, 128:] - got[half:, :128]
        for j in range(half // 128):
            at = (j * rows + r) * 2
            out_ref[pl.ds(at, 128, stride=first_rows), :] = re[j * 128 : (j + 1) * 128]
            out_ref[pl.ds(at + 1, 128, stride=first_rows), :] = im[j * 128 : (j + 1) * 128]


def mask_kernel(place_ref, sampling_ref, out_ref):
    frames, full, cols = sampling_ref.shape
    groups = cols // 128
    lane = lax.broadcasted_iota(jnp.int32, (cols, cols), 1)
    freq = lax.broadcasted_iota(jnp.int32, (cols, cols), 0)
    wanted = (lane // 128) * 128 + place_ref[0]
    total = jnp.zeros((full, cols), f32)
    for f in range(frames):
        mine = (freq == wanted) & ((lane % 128) // (128 // frames) == f)
        chosen = jnp.where(mine, 1.0, 0.0).astype(bf16)
        total += mm(sampling_ref[f].astype(f32).astype(bf16), chosen, ((1,), (0,)))
    for j in range(groups):
        out_ref[j] = total[:, j * 128 : (j + 1) * 128]


def lanes(values):
    row = jnp.sum(values, axis=0, keepdims=True)
    return row[:, :128] + row[:, 128:256] + row[:, 256:384]


def smooth_kernel(place_ref, field_ref, before_ref, after_ref, residual_ref, out_ref, stats_ref):
    slab, slabs, frame, frames = (place_ref[i] for i in range(4))
    rows = residual_ref.shape[1]
    zdim, cols = residual_ref.shape[2:]
    nearer = jnp.maximum(frame - 1, 0)
    later = jnp.minimum(frame + 1, frames - 1)
    has_prev_frame = jnp.where(frame > 0, 1.0, 0.0)
    has_next_frame = jnp.where(frame < frames - 1, 1.0, 0.0)
    has_prev_row = jnp.where(slab > 0, 1.0, 0.0)
    has_next_row = jnp.where(slab < slabs - 1, 1.0, 0.0)
    zero_col = jnp.zeros((zdim, 1), f32)
    zero_slice = jnp.zeros((1, cols), f32)
    dots = jnp.zeros((1, 128), f32)
    norm = jnp.zeros((1, 128), f32)
    for r in range(rows):
        weight = field_ref[frame, 2, r]
        old_weight = field_ref[nearer, 2, r] * has_prev_frame
        now_weight = weight * has_next_frame
        for p in range(2):
            v = field_ref[frame, p, r]
            term = old_weight * (v - field_ref[nearer, p, r])
            term -= now_weight * (field_ref[later, p, r] - v)
            if r > 0:
                term += field_ref[frame, 2, r - 1] * (v - field_ref[frame, p, r - 1])
            else:
                term += before_ref[2] * has_prev_row * (v - before_ref[p])
            if r < rows - 1:
                term -= weight * (field_ref[frame, p, r + 1] - v)
            else:
                term -= weight * has_next_row * (after_ref[p] - v)
            flux = weight[:-1] * (v[1:] - v[:-1])
            term += jnp.concatenate([zero_slice, flux], axis=0)
            term -= jnp.concatenate([flux, zero_slice], axis=0)
            flux = weight[:, :-1] * (v[:, 1:] - v[:, :-1])
            term += jnp.concatenate([zero_col, flux], axis=1)
            term -= jnp.concatenate([flux, zero_col], axis=1)
            term = smooth_scale * term
            out_ref[p, r] = term
            dots += lanes(v * term)
            norm += lanes(residual_ref[p, r] * residual_ref[p, r])
    stats_ref[0:1, :] = dots
    stats_ref[1:2, :] = norm


def middle_kernel(in_ref, mask_ref, stats_ref, forward_ref, inverse_ref, out_ref):
    groups = mask_ref.shape[0]
    rows = 3
    forward = forward_ref[...]
    forward = jnp.concatenate([forward, forward], axis=1)
    inverse = inverse_ref[...]
    inverse = jnp.concatenate([inverse, inverse], axis=1)
    half = forward.shape[0] // 2
    energy = jnp.zeros((1, 128), f32)
    for j in range(groups):
        parts = []
        for r in range(rows):
            at = (j * rows + r) * 2
            re = in_ref[pl.ds(at, 128, stride=first_rows), :]
            im = in_ref[pl.ds(at + 1, 128, stride=first_rows), :]
            parts.append(jnp.concatenate([re, im], axis=1))
        upper, lower = split(jnp.concatenate(parts, axis=0))
        got = mm(forward, jnp.concatenate([upper, lower], axis=0), ((1,), (0,)))
        mask = mask_ref[j]
        re = (got[:half, :128] + got[half:, 128:]) * mask
        im = (got[:half, 128:] - got[half:, :128]) * mask
        energy += jnp.sum(re * re + im * im, axis=0, keepdims=True)
        upper, lower = split(jnp.concatenate([re, im], axis=1))
        got = mm(inverse, jnp.concatenate([upper, lower], axis=0), ((1,), (0,)))
        re = got[:half, :128] - got[half:, 128:]
        im = got[:half, 128:] + got[half:, :128]
        for r in range(rows):
            at = (r * groups + j) * 2
            out_ref[pl.ds(at, 128, stride=second_rows), :] = re[r * 128 : (r + 1) * 128]
            out_ref[pl.ds(at + 1, 128, stride=second_rows), :] = im[r * 128 : (r + 1) * 128]
    energy = energy + stats_ref[0:1, :]
    out_ref[pl.ds(first_rows, 128, stride=second_rows), :] = jnp.broadcast_to(energy, (128, 128))
    out_ref[pl.ds(first_rows + 1, 128, stride=second_rows), :] = jnp.broadcast_to(
        stats_ref[1:2, :], (128, 128)
    )


def combine_kernel(in_ref, sens_ref, table_ref, out_ref):
    coils, rows, zdim, cols = sens_ref.shape[1:]
    frames = out_ref.shape[0]
    table = table_ref[...]
    table = jnp.concatenate([table, table], axis=0)
    groups = cols // 128
    span = coils * zdim
    for r in range(rows):
        real, imag = [], []
        for j in range(groups):
            at = (r * groups + j) * 2
            real.append(in_ref[pl.ds(at, 128, stride=second_rows), :].T)
            imag.append(in_ref[pl.ds(at + 1, 128, stride=second_rows), :].T)
        both = jnp.concatenate(
            [jnp.concatenate(real, axis=1), jnp.concatenate(imag, axis=1)], axis=0
        )
        upper, lower = split(both)
        got = mm(jnp.concatenate([upper, lower], axis=1), table, ((1,), (0,)))
        re = got[:128, :cols] - got[128:, cols:]
        im = got[128:, :cols] + got[:128, cols:]
        s_re = sens_rows(sens_ref, 0, r, coils)
        s_im = sens_rows(sens_ref, 1, r, coils)
        for f in range(frames):
            b_re = re[f * span : (f + 1) * span]
            b_im = im[f * span : (f + 1) * span]
            for p, t in enumerate((s_re * b_re + s_im * b_im, s_re * b_im - s_im * b_re)):
                eight = t[0:8]
                for g in range(1, span // 8):
                    eight = eight + t[g * 8 : (g + 1) * 8]
                out_ref[f, p * rows + r] = eight[0:zdim] + eight[zdim : 2 * zdim]
    energy = jnp.sum(in_ref[pl.ds(first_rows, 128, stride=second_rows), :], axis=0, keepdims=True)
    norm = jnp.sum(in_ref[pl.ds(first_rows + 1, 128, stride=second_rows), :], axis=0, keepdims=True)
    filler = jnp.zeros((1, cols - 256), f32)
    line = jnp.concatenate([energy, norm, filler], axis=1)
    plane = jnp.concatenate([line, jnp.zeros((zdim - 1, cols), f32)], axis=0)
    for f in range(frames):
        out_ref[f, 2 * rows] = plane


def step_kernel(
    sums_ref, smooth_ref, iterate_ref, residual_ref, direction_ref, new_iterate_ref, new_residual_ref, norms_ref, old_ref
):
    planes = residual_ref.shape[0]
    sources = sums_ref.shape[0]
    line = sums_ref[0, planes][0:1]
    for i in range(1, sources):
        line = line + sums_ref[i, planes][0:1]
    curvature = jnp.sum(line[:, :128], axis=1, keepdims=True)
    old_norm = jnp.sum(line[:, 128:256], axis=1, keepdims=True)
    step = old_norm / curvature
    norm = jnp.zeros((1, 128), f32)
    for i in range(planes):
        applied = smooth_ref[i]
        for k in range(sources):
            applied = applied + sums_ref[k, i]
        new_iterate_ref[i] = iterate_ref[i] + step * direction_ref[i]
        fresh = residual_ref[i] - step * applied
        new_residual_ref[i] = fresh
        norm = norm + lanes(fresh * fresh)
    norms_ref[...] = jnp.broadcast_to(norm[None], norms_ref.shape)
    old_ref[...] = jnp.broadcast_to(old_norm, old_ref.shape)


def finish_kernel(norms_ref, old_ref, new_residual_ref, direction_ref, new_direction_ref, norm_ref):
    row = jnp.sum(norms_ref[...], axis=0)
    new_norm = jnp.sum(row, axis=1, keepdims=True)
    ratio = new_norm / old_ref[0:1, 0:1]
    for i in range(direction_ref.shape[0]):
        new_direction_ref[i] = new_residual_ref[i] + ratio * direction_ref[i]
    norm_ref[...] = jnp.broadcast_to(new_norm, norm_ref.shape)


vmem = pl.BlockSpec(memory_space=pltpu.VMEM)
smem = pl.BlockSpec(memory_space=pltpu.SMEM)


def call(kernel, ins, outs, name, scalars=0):
    shapes = [jax.ShapeDtypeStruct(s, f32) for s in outs]
    return pl.pallas_call(
        kernel,
        out_shape=shapes,
        in_specs=[smem] * scalars + [vmem] * (len(ins) - scalars),
        out_specs=[vmem] * len(outs),
        compiler_params=pltpu.CompilerParams(vmem_limit_bytes=40 * 1024 * 1024),
        name=name,
    )(*ins)


def swap(values, axis):
    pairs = values.reshape(values.shape[0] // 2, 2, 128)
    return lax.all_to_all(pairs, axis, 0, 0, tiled=True).reshape(values.shape)


def body(iterate, residual, direction, sensitivity, sampling, edge_weight):
    slabs = lax.axis_size(slab_axes)
    frames = lax.axis_size("coil")
    slab = lax.axis_index(slab_axes)
    frame = lax.axis_index("coil")
    rows, zdim, cols = direction.shape[3], direction.shape[2], direction.shape[4]

    sens = jnp.swapaxes(sensitivity, 2, 3)
    d = jnp.swapaxes(direction, 2, 3)[:, 0]
    r = jnp.swapaxes(residual, 2, 3)[:, 0]
    x = jnp.swapaxes(iterate, 2, 3)[:, 0]
    w = jnp.swapaxes(edge_weight, 1, 2).astype(f32)
    field = jnp.concatenate([d, w], axis=0)

    cos, sin = dft_tables(cols)
    by_slab = np.arange(cols).reshape(cols // rows, rows).T.reshape(-1)
    natural = jnp.asarray(np.concatenate([cos, sin], axis=0))
    forward = jnp.asarray(np.concatenate([cos[:, by_slab], sin[:, by_slab]], axis=0))
    inverse = jnp.asarray(np.concatenate([cos[by_slab], sin[by_slab]], axis=0))
    wide = jnp.asarray(np.concatenate([cos, sin], axis=1))

    place = jnp.stack([slab, jnp.int32(slabs), frame, jnp.int32(frames)]).astype(jnp.int32)
    fields = lax.all_gather(field, "coil", axis=0)
    up = [(i, i + 1) for i in range(slabs - 1)]
    before = lax.ppermute(field[:, rows - 1], slab_axes, up)
    after = lax.ppermute(field[:2, 0], slab_axes, [(j, i) for i, j in up])

    lines = slabs * first_rows
    (spectrum,) = call(images_kernel, (sens, fields, natural), [(lines, 128)], "images")
    spectrum = swap(spectrum, slab_axes)
    (mask,) = call(mask_kernel, (place, sampling), [(cols // 128, cols, 128)], "mask", 1)
    smooth, stats = call(
        smooth_kernel, (place, fields, before, after, r), [d.shape, (2, 128)], "smooth", 1
    )
    lines = slabs * second_rows
    (back,) = call(
        middle_kernel, (spectrum, mask, stats, forward, inverse), [(lines, 128)], "middle"
    )
    back = swap(back, slab_axes)
    (sums,) = call(
        combine_kernel, (back, sens, wide), [(frames, 2 * rows + 1, zdim, cols)], "combine"
    )
    sums = lax.all_to_all(sums, "coil", 0, 0, tiled=True)

    flat = (2 * rows, zdim, cols)
    near, far = ("y", "core"), ("z", "coil")
    new_x, new_r, norms, old = call(
        step_kernel,
        (sums, smooth.reshape(flat), x.reshape(flat), r.reshape(flat), d.reshape(flat)),
        [flat, flat, (lax.axis_size(near), 1, 128), (1, 128)],
        "step",
    )
    norms = lax.all_to_all(norms, near, 0, 0, tiled=True)
    norms = jnp.broadcast_to(
        jnp.sum(norms, axis=0, keepdims=True), (lax.axis_size(far), 1, 128)
    )
    norms = lax.all_to_all(norms, far, 0, 0, tiled=True)
    new_d, norm = call(
        finish_kernel, (norms, old, new_r, d.reshape(flat)), [flat, (1, 128)], "finish"
    )

    def restore(values):
        return jnp.swapaxes(values.reshape(2, 1, rows, zdim, cols), 2, 3)

    return restore(new_x), restore(new_r), restore(new_d), norm[0, 0]


def solution(mesh):
    fine = Mesh(mesh.devices.reshape(8, 8, 2, 4), ("z", "y", "core", "coil"))
    image = P(None, "coil", None, slab_axes, None)
    return jax.shard_map(
        body,
        mesh=fine,
        in_specs=(image, image, image, image, P(), P("coil", None, slab_axes, None)),
        out_specs=(image, image, image, P()),
        check_vma=False,
    )
```

profile of v0, /device:TPU:1, one launch (start us, length us, event | category | flops | bytes accessed | tf_op | source)
XLA Modules:
  0.0 153.3 jit_solution(7730176087173491816)
XLA Ops:
  0.6 0.0 copy-start.6
  0.6 0.8 fusion.2
  1.4 0.8 copy.25
  2.2 10.5 %all-gather = f32[12,3,4,384]{3,2,0,1:T(4,128)S(1)} all-gather(f32[3,3,4,384]{3,2,0,1:T(4,128)S(1)} %pad_maximum_fusion), channel_id=2, replica_groups=mesh['z'=8,'y'=8,'core'=2,'coil'=4] {'coil'}, dimensions={0}, use_global_device_ids=true | all-gather | bytes 276480 | tf_op jit(solution)/shard_map/all_gather | solution.py:289
  12.7 0.0 copy-done.6
  12.8 0.0 copy-start.3
  12.8 0.9 copy-done.3
  13.7 2.2 %images.1 = f32[2304,128]{1,0:T(8,128)} custom-call(bf16[2,8,3,4,384]{4,3,2,1,0:T(4,128)(2,1)S(1)} %bitcast.56, f32[4,3,3,4,384]{4,3,2,1,0:T(4,128)S(1)} %copy.16.field_ref, bf16[768,384]{1,0:T(8,128)(2,1)S(1)} %copy-done.6), custom_call_target="tpu_custom_call" | custom-call | tf_op jit(solution)/shard_map/images/pallas_call | solution.py:252
  15.8 20.5 %all-to-all-start = ((f32[1152,2,128]{2,1,0:T(2,128)}), f32[1152,2,128]{2,1,0:T(2,128)S(1)}, u32[]{:S(2)}, u32[]{:S(2)}) async-start(f32[1152,2,128]{2,1,0:T(2,128)} %bitcast.6), calls=%async_computation | async-start | bytes 2359296 | tf_op jit(solution)/shard_map/all_to_all | solution.py:264
  36.3 2.8 %collective-permute-start.1 = (f32[2,4,384]{2,1,0:T(4,128)S(1)}, f32[2,4,384]{2,1,0:T(4,128)S(1)}, u32[]{:S(2)}, u32[]{:S(2)}) collective-permute-start(f32[2,4,384]{2,1,0:T(4,128)S(1)} %slice_bitcast_fusion), channel_id=1, source_target_pairs={{4,0},{8,4},{12,8},{16,12},{20,16},{24,20},{28,24},{32,28},{36,32}... | collective-permute-start | bytes 36872 | tf_op jit(solution)/shard_map/ppermute | solution.py:292
  39.2 2.8 %collective-permute-start = (f32[3,4,384]{2,1,0:T(4,128)S(1)}, f32[3,4,384]{2,1,0:T(4,128)S(1)}, u32[]{:S(2)}, u32[]{:S(2)}) collective-permute-start(f32[3,4,384]{2,1,0:T(4,128)S(1)} %fusion.1), channel_id=1, source_target_pairs={{0,4},{4,8},{8,12},{12,16},{16,20},{20,24},{24,28},{28,32},{32,36}... | collective-permute-start | bytes 55304 | tf_op jit(solution)/shard_map/ppermute | solution.py:291
  41.9 0.1 pad_add_fusion.place_ref
  42.0 0.0 copy-start
  42.0 1.7 %copy-done = s32[4,384,384]{2,1,0:T(8,128)S(1)} copy-done((s32[4,384,384]{2,1,0:T(8,128)S(1)}, s32[4,384,384]{2,1,0:T(8,128)}, u32[]{:S(2)}) %copy-start) | copy-done | bytes 2359320
  43.7 0.0 copy-start.7
  43.7 0.0 copy-start.1
  43.7 0.0 copy-start.2
  43.7 1.4 mask.1.mask_ref
  45.1 18.6 %collective-permute-done.1.after_ref = f32[2,4,384]{2,1,0:T(4,128)S(1)} collective-permute-done((f32[2,4,384]{2,1,0:T(4,128)S(1)}, f32[2,4,384]{2,1,0:T(4,128)S(1)}, u32[]{:S(2)}, u32[]{:S(2)}) %collective-permute-start.1) | collective-permute-done | bytes 12320 | tf_op jit(solution)/shard_map/ppermute | solution.py:292
  63.7 0.0 collective-permute-done.before_ref
  63.7 0.0 copy-done.7
  63.7 0.8 smooth.1
  64.5 5.5 %all-to-all-done = f32[1152,2,128]{2,1,0:T(2,128)S(1)} async-done(((f32[1152,2,128]{2,1,0:T(2,128)}), f32[1152,2,128]{2,1,0:T(2,128)S(1)}, u32[]{:S(2)}, u32[]{:S(2)}) %all-to-all-start) | async-done | bytes 1179680 | tf_op jit(solution)/shard_map/all_to_all | solution.py:264
  70.0 0.0 copy-done.1
  70.0 0.0 copy-done.2
  70.0 2.7 %middle.1 = f32[2560,128]{1,0:T(8,128)S(1)} custom-call(f32[2304,128]{1,0:T(8,128)S(1)} %bitcast.55, f32[3,384,128]{2,1,0:T(8,128)S(1)} %mask.1.mask_ref, f32[2,128]{1,0:T(2,128)S(1)} %get-tuple-element.12.stats_ref, bf16[768,384]{1,0:T(8,128)(2,1)S(1)} %copy-done.2, bf16[768,384]{1,0:T(8,128)(2,1)S(1)} %copy-done.1), custom_call_target="tpu_custom_call" | custom-call | tf_op jit(solution)/shard_map/middle/pallas_call | solution.py:252
  72.8 0.0 copy-start.4
  72.8 0.0 copy-start.5
  72.8 43.0 %all_to_all.25 = f32[1280,2,128]{2,1,0:T(2,128)S(1)} all-to-all(f32[1280,2,128]{2,1,0:T(2,128)S(1)} %bitcast.53), channel_id=1, replica_groups=mesh['z'=8,'y'=8,'core'=2,'coil'=4] {'z','y','core'}, dimensions={0} | all-to-all | bytes 2621440 | tf_op jit(solution)/shard_map/all_to_all | solution.py:264
  115.8 0.0 copy-done.4
  115.8 0.0 copy-done.5
  115.8 0.0 copy-start.8
  115.8 1.9 %combine.1 = f32[4,7,4,384]{3,2,1,0:T(4,128)} custom-call(f32[2560,128]{1,0:T(8,128)S(1)} %bitcast.54, bf16[2,8,3,4,384]{4,3,2,1,0:T(4,128)(2,1)S(1)} %bitcast.57, bf16[384,768]{1,0:T(8,128)(2,1)S(1)} %copy-done.5), custom_call_target="tpu_custom_call" | custom-call | tf_op jit(solution)/shard_map/combine/pallas_call | solution.py:252
  117.7 3.4 %all-to-all-start.2 = ((f32[4,7,4,384]{3,2,1,0:T(4,128)}), f32[4,7,4,384]{3,2,1,0:T(4,128)S(1)}, u32[]{:S(2)}, u32[]{:S(2)}) async-start(f32[4,7,4,384]{3,2,1,0:T(4,128)} %combine.1), calls=%async_computation.2 | async-start | bytes 344064 | tf_op jit(solution)/shard_map/all_to_all | solution.py:309
  121.1 5.0 %all-to-all-done.2.sums_ref = f32[4,7,4,384]{3,2,1,0:T(4,128)S(1)} async-done(((f32[4,7,4,384]{3,2,1,0:T(4,128)}), f32[4,7,4,384]{3,2,1,0:T(4,128)S(1)}, u32[]{:S(2)}, u32[]{:S(2)}) %all-to-all-start.2) | async-done | bytes 172064 | tf_op jit(solution)/shard_map/all_to_all | solution.py:309
  126.1 0.0 copy-done.8
  126.1 0.7 step.1
  126.9 12.9 %all_to_all.26 = f32[16,1,128]{2,1,0:T(1,128)S(1)} all-to-all(f32[16,1,128]{2,1,0:T(1,128)S(1)} %get-tuple-element.16), channel_id=1, replica_groups=mesh['z'=8,'y'=8,'core'=2,'coil'=4] {'y','core'}, dimensions={0} | all-to-all | bytes 16384 | tf_op jit(solution)/shard_map/all_to_all | solution.py:319
  139.8 11.9 %all_to_all.27.norms_ref = f32[32,1,128]{2,1,0:T(1,128)S(1)} all-to-all(f32[32,1,128]{2,1,0:T(1,128)S(1)} %broadcast_in_dim.2), channel_id=1, replica_groups=mesh['z'=8,'y'=8,'core'=2,'coil'=4] {'z','coil'}, dimensions={0} | all-to-all | bytes 32768 | tf_op jit(solution)/shard_map/all_to_all | solution.py:323
  151.7 0.0 copy-start.9
  151.7 0.8 copy-done.9
  152.5 0.8 finish.1
  (7 shorter events, 0.1 us)
Async XLA Ops:
  0.6 12.1 %copy-start.6 = (bf16[768,384]{1,0:T(8,128)(2,1)S(1)}, bf16[768,384]{1,0:T(8,128)(2,1)}, u32[]{:S(2)}) copy-start(bf16[768,384]{1,0:T(8,128)(2,1)} %constant.35.clone.table_ref) | copy-start | bytes 1769476
  12.8 0.9 copy-start.3
  15.8 54.2 %all-to-all-start = ((f32[1152,2,128]{2,1,0:T(2,128)}), f32[1152,2,128]{2,1,0:T(2,128)S(1)}, u32[]{:S(2)}, u32[]{:S(2)}) async-start(f32[1152,2,128]{2,1,0:T(2,128)} %bitcast.6), calls=%async_computation | async-start | bytes 2359296 | tf_op jit(solution)/shard_map/all_to_all | solution.py:264
  36.3 27.4 %collective-permute-start.1 = (f32[2,4,384]{2,1,0:T(4,128)S(1)}, f32[2,4,384]{2,1,0:T(4,128)S(1)}, u32[]{:S(2)}, u32[]{:S(2)}) collective-permute-start(f32[2,4,384]{2,1,0:T(4,128)S(1)} %slice_bitcast_fusion), channel_id=1, source_target_pairs={{4,0},{8,4},{12,8},{16,12},{20,16},{24,20},{28,24},{32,28},{36,32}... | collective-permute-start | bytes 36872 | tf_op jit(solution)/shard_map/ppermute | solution.py:292
  39.2 24.5 %collective-permute-start = (f32[3,4,384]{2,1,0:T(4,128)S(1)}, f32[3,4,384]{2,1,0:T(4,128)S(1)}, u32[]{:S(2)}, u32[]{:S(2)}) collective-permute-start(f32[3,4,384]{2,1,0:T(4,128)S(1)} %fusion.1), channel_id=1, source_target_pairs={{0,4},{4,8},{8,12},{12,16},{16,20},{20,24},{24,28},{28,32},{32,36}... | collective-permute-start | bytes 55304 | tf_op jit(solution)/shard_map/ppermute | solution.py:291
  42.0 1.7 %copy-start = (s32[4,384,384]{2,1,0:T(8,128)S(1)}, s32[4,384,384]{2,1,0:T(8,128)}, u32[]{:S(2)}) copy-start(s32[4,384,384]{2,1,0:T(8,128)} %sampling_ref.1) | copy-start | bytes 7077892
  43.7 20.0 %copy-start.7 = (f32[2,1,4,3,384]{4,2,3,1,0:T(4,128)S(1)}, f32[2,1,4,3,384]{4,2,3,1,0:T(4,128)}, u32[]{:S(2)}) copy-start(f32[2,1,4,3,384]{4,2,3,1,0:T(4,128)} %param.11) | copy-start | bytes 110596
  43.7 26.3 %copy-start.1 = (bf16[768,384]{1,0:T(8,128)(2,1)S(1)}, bf16[768,384]{1,0:T(8,128)(2,1)}, u32[]{:S(2)}) copy-start(bf16[768,384]{1,0:T(8,128)(2,1)} %constant.37.clone.inverse_ref) | copy-start | bytes 1769476
  43.7 26.3 %copy-start.2 = (bf16[768,384]{1,0:T(8,128)(2,1)S(1)}, bf16[768,384]{1,0:T(8,128)(2,1)}, u32[]{:S(2)}) copy-start(bf16[768,384]{1,0:T(8,128)(2,1)} %constant.36.clone.forward_ref) | copy-start | bytes 1769476
  72.8 43.0 %copy-start.4 = (bf16[2,8,4,3,384]{4,2,3,1,0:T(4,128)(2,1)S(1)}, bf16[2,8,4,3,384]{4,2,3,1,0:T(4,128)(2,1)}, u32[]{:S(2)}) copy-start(bf16[2,8,4,3,384]{4,2,3,1,0:T(4,128)(2,1)} %param.13) | copy-start | bytes 442372
  72.8 43.0 %copy-start.5 = (bf16[384,768]{1,0:T(8,128)(2,1)S(1)}, bf16[384,768]{1,0:T(8,128)(2,1)}, u32[]{:S(2)}) copy-start(bf16[384,768]{1,0:T(8,128)(2,1)} %constant.38.clone.table_ref) | copy-start | bytes 1769476
  115.8 10.3 %copy-start.8 = (f32[2,1,4,3,384]{4,2,3,1,0:T(4,128)S(1)}, f32[2,1,4,3,384]{4,2,3,1,0:T(4,128)}, u32[]{:S(2)}) copy-start(f32[2,1,4,3,384]{4,2,3,1,0:T(4,128)} %param.10) | copy-start | bytes 110596
  117.7 8.4 %all-to-all-start.2 = ((f32[4,7,4,384]{3,2,1,0:T(4,128)}), f32[4,7,4,384]{3,2,1,0:T(4,128)S(1)}, u32[]{:S(2)}, u32[]{:S(2)}) async-start(f32[4,7,4,384]{3,2,1,0:T(4,128)} %combine.1), calls=%async_computation.2 | async-start | bytes 344064 | tf_op jit(solution)/shard_map/all_to_all | solution.py:309
  151.7 0.8 copy-start.9
where the time goes:
time: 154 us; the launch traced here: 153 us
  blocking collectives  78.3 us (51%)
  starting transfers between devices  29.4 us (19%)
  waiting for transfers between devices  29.1 us (19%)
  Pallas kernels  10.5 us (7%)
  local copies, waits for them, and re-layouts  4.19 us (3%)
    all_to_all x1, blocking collectives, swap(): return lax.all_to_all(pairs, axis, 0, 0, tiled=True).reshape(values.shape)  43 us
    all_to_all x1, starting transfers between devices, swap(): return lax.all_to_all(pairs, axis, 0, 0, tiled=True).reshape(values.shape)  20.5 us
    ppermute x1, waiting for transfers between devices, body(): after = lax.ppermute(field[:2, 0], slab_axes, [(j, i) for i, j in up])  18.6 us
    all_to_all x1, blocking collectives, body(): norms = lax.all_to_all(norms, near, 0, 0, tiled=True)  12.9 us
    all_to_all x1, blocking collectives, body(): norms = lax.all_to_all(norms, far, 0, 0, tiled=True)  11.9 us
    pallas_call x7, Pallas kernels, call(): pl.pallas_call(kernel, out_shape=shapes, in_specs=[smem] * scalars + [vme...  10.5 us
    all_gather x1, blocking collectives, body(): fields = lax.all_gather(field, 'coil', axis=0)  10.5 us
    all_to_all x1, waiting for transfers between devices, swap(): return lax.all_to_all(pairs, axis, 0, 0, tiled=True).reshape(values.shape)  5.52 us
  transfers between devices with their start and end apart: 4, of which 3 were waited for; matrix products, arithmetic and copies ran while one was open for 0% of the time, Pallas kernels for 1%

commit v1 on v0

v1 whole, which is shorter than its diff:
```python
import functools
import math

import jax
import jax.numpy as jnp
import ml_dtypes
import numpy as np
from jax import lax
from jax.experimental import pallas as pl
from jax.experimental.pallas import tpu as pltpu
from jax.sharding import Mesh
from jax.sharding import PartitionSpec as P

smooth_scale = 0.05
slab_axes = ("z", "y", "core")
f32 = jnp.float32
bf16 = jnp.bfloat16

extra = 18
message = 19


def dft_tables(length):
    counter = np.arange(length, dtype=np.int64)
    phases = (counter[:, None] * counter[None, :]) % length
    angles = phases.astype(np.float32) * np.float32(2.0 * math.pi / length)
    unit_norm = np.float32(1.0 / math.sqrt(length))
    wide = angles.astype(np.float64)
    cos = np.cos(wide).astype(np.float32) * unit_norm
    sin = np.sin(wide).astype(np.float32) * unit_norm
    return cos.astype(ml_dtypes.bfloat16), sin.astype(ml_dtypes.bfloat16)


def split(values):
    upper = values.astype(bf16)
    return upper, (values - upper.astype(f32)).astype(bf16)


def mm(a, b, contract):
    return lax.dot_general(a, b, (contract, ((), ())), preferred_element_type=f32)


def sens_rows(sens_ref, part, row, coils):
    pieces = [sens_ref[part, c, row].astype(f32) for c in range(coils)]
    return jnp.concatenate(pieces, axis=0)


def images_kernel(sens_ref, all_ref, own_ref, weight_ref, table_ref, out_ref):
    coils, rows, zdim = sens_ref.shape[1:4]
    frames = all_ref.shape[1]
    table = table_ref[...]
    table = jnp.concatenate([table, table], axis=1)
    half = table.shape[0] // 2
    groups = half // 128
    for r in range(rows):
        s_re = sens_rows(sens_ref, 0, r, coils)
        s_im = sens_rows(sens_ref, 1, r, coils)
        real, imag = [], []
        for f in range(frames):
            d_re = jnp.concatenate([all_ref[0, f, r]] * coils, axis=0)
            d_im = jnp.concatenate([all_ref[1, f, r]] * coils, axis=0)
            real.append(s_re * d_re - s_im * d_im)
            imag.append(s_re * d_im + s_im * d_re)
        upper, lower = split(jnp.concatenate(real + imag, axis=0))
        got = mm(table, jnp.concatenate([upper, lower], axis=1), ((1,), (1,)))
        re = got[:half, :128] + got[half:, 128:]
        im = got[:half, 128:] - got[half:, :128]
        for j in range(groups):
            at = (j * rows + r) * 2
            out_ref[pl.ds(at, 128, stride=message), :] = re[j * 128 : (j + 1) * 128]
            out_ref[pl.ds(at + 1, 128, stride=message), :] = im[j * 128 : (j + 1) * 128]
    pieces = []
    for r in range(rows):
        for values in (own_ref[0, r], own_ref[1, r], weight_ref[r].astype(f32)):
            pieces += [values[:, j * 128 : (j + 1) * 128] for j in range(groups)]
    pieces.append(jnp.zeros((128 - len(pieces) * zdim, 128), f32))
    out_ref[pl.ds(extra, 128, stride=message), :] = jnp.concatenate(pieces, axis=0).T


def mask_kernel(place_ref, sampling_ref, out_ref):
    frames, full, cols = sampling_ref.shape
    groups = cols // 128
    lane = lax.broadcasted_iota(jnp.int32, (cols, cols), 1)
    freq = lax.broadcasted_iota(jnp.int32, (cols, cols), 0)
    wanted = (lane // 128) * 128 + place_ref[0]
    total = jnp.zeros((full, cols), f32)
    for f in range(frames):
        mine = (freq == wanted) & ((lane % 128) // (128 // frames) == f)
        chosen = jnp.where(mine, 1.0, 0.0).astype(bf16)
        total += mm(sampling_ref[f].astype(f32).astype(bf16), chosen, ((1,), (0,)))
    for j in range(groups):
        out_ref[j] = total[:, j * 128 : (j + 1) * 128]


def lanes(values):
    row = jnp.sum(values, axis=0, keepdims=True)
    return row[:, :128] + row[:, 128:256] + row[:, 256:384]


def smooth_kernel(place_ref, all_ref, own_ref, weight_ref, residual_ref, out_ref, next_ref, stats_ref):
    frame, frames = place_ref[1], place_ref[2]
    rows, zdim, cols = own_ref.shape[1:]
    later = jnp.minimum(frame + 1, frames - 1)
    zero_col = jnp.zeros((zdim, 1), f32)
    zero_slice = jnp.zeros((1, cols), f32)
    dots = jnp.zeros((1, 128), f32)
    norm = jnp.zeros((1, 128), f32)
    for r in range(rows):
        weight = weight_ref[r].astype(f32)
        for p in range(2):
            v = own_ref[p, r]
            rise = all_ref[p, later, r] - v
            onward = smooth_scale * (weight * rise)
            flux = weight[:-1] * (v[1:] - v[:-1])
            term = jnp.concatenate([zero_slice, flux], axis=0)
            term -= jnp.concatenate([flux, zero_slice], axis=0)
            flux = weight[:, :-1] * (v[:, 1:] - v[:, :-1])
            term += jnp.concatenate([zero_col, flux], axis=1)
            term -= jnp.concatenate([flux, zero_col], axis=1)
            term = smooth_scale * term
            out_ref[p * rows + r] = term - onward
            next_ref[p * rows + r] = onward
            dots += lanes(v * term + onward * rise)
            norm += lanes(residual_ref[p, r] * residual_ref[p, r])
    stats_ref[0:1, :] = dots
    stats_ref[1:2, :] = norm


def row_smoothing(given, zdim, groups):
    span = groups * zdim
    v, weight = [], []
    for r in range(3):
        at = r * 3 * span
        w = given[:, at + 2 * span : at + 3 * span]
        v.append(given[:, at : at + 2 * span])
        weight.append(jnp.concatenate([w, w], axis=1))
    none = jnp.zeros((1, 2 * span), f32)
    first = weight[0] * (v[1] - v[0])
    second = weight[1] * (v[2] - v[1])
    third = weight[2][:-1] * (v[0][1:] - v[2][:-1])
    terms = [
        jnp.concatenate([none, third], axis=0) - first,
        first - second,
        second - jnp.concatenate([third, none], axis=0),
    ]
    terms = [smooth_scale * t for t in terms]
    dots = v[0] * terms[0] + v[1] * terms[1] + v[2] * terms[2]
    return terms, jnp.sum(jnp.sum(dots, axis=0, keepdims=True), axis=1, keepdims=True)


def middle_kernel(in_ref, mask_ref, stats_ref, forward_ref, inverse_ref, out_ref, *, zdim):
    groups = mask_ref.shape[0]
    rows = 3
    forward = forward_ref[...]
    forward = jnp.concatenate([forward, forward], axis=1)
    inverse = inverse_ref[...]
    inverse = jnp.concatenate([inverse, inverse], axis=1)
    half = forward.shape[0] // 2
    energy = stats_ref[0:1, :]
    for j in range(groups):
        parts = []
        for r in range(rows):
            at = (j * rows + r) * 2
            re = in_ref[pl.ds(at, 128, stride=message), :]
            im = in_ref[pl.ds(at + 1, 128, stride=message), :]
            parts.append(jnp.concatenate([re, im], axis=1))
        upper, lower = split(jnp.concatenate(parts, axis=0))
        got = mm(forward, jnp.concatenate([upper, lower], axis=0), ((1,), (0,)))
        mask = mask_ref[j]
        re = (got[:half, :128] + got[half:, 128:]) * mask
        im = (got[:half, 128:] - got[half:, :128]) * mask
        energy += jnp.sum(re * re + im * im, axis=0, keepdims=True)
        upper, lower = split(jnp.concatenate([re, im], axis=1))
        got = mm(inverse, jnp.concatenate([upper, lower], axis=0), ((1,), (0,)))
        re = got[:half, :128] - got[half:, 128:]
        im = got[:half, 128:] + got[half:, :128]
        for r in range(rows):
            at = (r * groups + j) * 2
            out_ref[pl.ds(at, 128, stride=message), :] = re[r * 128 : (r + 1) * 128]
            out_ref[pl.ds(at + 1, 128, stride=message), :] = im[r * 128 : (r + 1) * 128]
    terms, dots = row_smoothing(in_ref[pl.ds(extra, 128, stride=message), :], zdim, groups)
    energy = jnp.sum(energy, axis=1, keepdims=True) + dots
    norm = jnp.sum(stats_ref[1:2, :], axis=1, keepdims=True)
    used = 2 * rows * groups * zdim
    filler = jnp.zeros((128, 128 - used - 2), f32)
    sums = [jnp.broadcast_to(v, (128, 1)) for v in (energy, norm)]
    out_ref[pl.ds(extra, 128, stride=message), :] = jnp.concatenate(terms + sums + [filler], axis=1)


def combine_kernel(place_ref, in_ref, sens_ref, smooth_ref, next_ref, table_ref, out_ref):
    frame, frame_count = place_ref[1], place_ref[2]
    coils, rows, zdim, cols = sens_ref.shape[1:]
    frames = out_ref.shape[0]
    table = table_ref[...]
    table = jnp.concatenate([table, table], axis=0)
    groups = cols // 128
    span = coils * zdim
    for r in range(rows):
        real, imag = [], []
        for j in range(groups):
            at = (r * groups + j) * 2
            real.append(in_ref[pl.ds(at, 128, stride=message), :].T)
            imag.append(in_ref[pl.ds(at + 1, 128, stride=message), :].T)
        both = jnp.concatenate(
            [jnp.concatenate(real, axis=1), jnp.concatenate(imag, axis=1)], axis=0
        )
        upper, lower = split(both)
        got = mm(jnp.concatenate([upper, lower], axis=1), table, ((1,), (0,)))
        re = got[:128, :cols] - got[128:, cols:]
        im = got[128:, :cols] + got[:128, cols:]
        s_re = sens_rows(sens_ref, 0, r, coils)
        s_im = sens_rows(sens_ref, 1, r, coils)
        for f in range(frames):
            b_re = re[f * span : (f + 1) * span]
            b_im = im[f * span : (f + 1) * span]
            for p, t in enumerate((s_re * b_re + s_im * b_im, s_re * b_im - s_im * b_re)):
                eight = t[0:8]
                for g in range(1, span // 8):
                    eight = eight + t[g * 8 : (g + 1) * 8]
                out_ref[f, p * rows + r] = eight[0:zdim] + eight[zdim : 2 * zdim]
    given = in_ref[pl.ds(extra, 128, stride=message), :]
    used = 2 * rows * groups * zdim
    total = jnp.sum(given, axis=0, keepdims=True)
    energy = jnp.broadcast_to(total[:, used : used + 1], (1, cols))
    norm = jnp.broadcast_to(total[:, used + 1 : used + 2], (1, cols))
    plane = jnp.concatenate([energy, norm, jnp.zeros((zdim - 2, cols), f32)], axis=0)
    for f in range(frames):
        out_ref[f, 2 * rows] = plane
    turned = given.T
    for r in range(rows):
        for p in range(2):
            at = (r * 2 + p) * groups * zdim
            term = [turned[at + j * zdim : at + (j + 1) * zdim] for j in range(groups)]
            i = p * rows + r
            out_ref[frame, i] += smooth_ref[i] + jnp.concatenate(term, axis=1)

    @pl.when(frame < frame_count - 1)
    def _():
        for i in range(2 * rows):
            out_ref[frame + 1, i] += next_ref[i]


def step_kernel(
    sums_ref, iterate_ref, residual_ref, direction_ref, new_iterate_ref, new_residual_ref, norms_ref, old_ref
):
    planes = residual_ref.shape[0]
    sources = sums_ref.shape[0]

    def total(i):
        value = sums_ref[0, i]
        for k in range(1, sources):
            value = value + sums_ref[k, i]
        return value

    both = total(planes)
    old_norm = both[1:2, :1]
    step = old_norm / both[0:1, :1]
    norm = jnp.zeros((1, 128), f32)
    for i in range(planes):
        new_iterate_ref[i] = iterate_ref[i] + step * direction_ref[i]
        fresh = residual_ref[i] - step * total(i)
        new_residual_ref[i] = fresh
        norm = norm + lanes(fresh * fresh)
    norms_ref[...] = jnp.broadcast_to(norm[None], norms_ref.shape)
    old_ref[...] = jnp.broadcast_to(old_norm, old_ref.shape)


def finish_kernel(norms_ref, old_ref, new_residual_ref, direction_ref, new_direction_ref, norm_ref):
    row = jnp.sum(norms_ref[...], axis=0)
    new_norm = jnp.sum(row, axis=1, keepdims=True)
    ratio = new_norm / old_ref[0:1, 0:1]
    for i in range(direction_ref.shape[0]):
        new_direction_ref[i] = new_residual_ref[i] + ratio * direction_ref[i]
    norm_ref[...] = jnp.broadcast_to(new_norm, norm_ref.shape)


vmem = pl.BlockSpec(memory_space=pltpu.VMEM)
smem = pl.BlockSpec(memory_space=pltpu.SMEM)


def call(kernel, ins, outs, name, scalars=0):
    shapes = [jax.ShapeDtypeStruct(s, f32) for s in outs]
    return pl.pallas_call(
        kernel,
        out_shape=shapes,
        in_specs=[smem] * scalars + [vmem] * (len(ins) - scalars),
        out_specs=[vmem] * len(outs),
        compiler_params=pltpu.CompilerParams(vmem_limit_bytes=40 * 1024 * 1024),
        name=name,
    )(*ins)


def swap(values, axis):
    single = values.reshape(values.shape[0], 1, 128)
    return lax.all_to_all(single, axis, 0, 0, tiled=True).reshape(values.shape)


def body(iterate, residual, direction, sensitivity, sampling, edge_weight):
    slabs = lax.axis_size(slab_axes)
    frames = lax.axis_size("coil")
    rows, zdim, cols = direction.shape[3], direction.shape[2], direction.shape[4]

    sens = jnp.swapaxes(sensitivity, 2, 3)
    d = jnp.swapaxes(direction, 2, 3)[:, 0]
    r = jnp.swapaxes(residual, 2, 3)[:, 0]
    x = jnp.swapaxes(iterate, 2, 3)[:, 0]
    w = jnp.swapaxes(edge_weight, 1, 2)[0]

    cos, sin = dft_tables(cols)
    by_slab = np.arange(cols).reshape(cols // rows, rows).T.reshape(-1)
    natural = jnp.asarray(np.concatenate([cos, sin], axis=0))
    forward = jnp.asarray(np.concatenate([cos[:, by_slab], sin[:, by_slab]], axis=0))
    inverse = jnp.asarray(np.concatenate([cos[by_slab], sin[by_slab]], axis=0))
    wide = jnp.asarray(np.concatenate([cos, sin], axis=1))

    place = jnp.stack([lax.axis_index(slab_axes), lax.axis_index("coil"), jnp.int32(frames)])
    place = place.astype(jnp.int32)
    gathered = lax.all_gather(direction, "coil", axis=1, tiled=True)
    gathered = jnp.swapaxes(gathered, 2, 3)

    lines = slabs * message
    (spectrum,) = call(images_kernel, (sens, gathered, d, w, natural), [(lines, 128)], "images")
    spectrum = swap(spectrum, slab_axes)
    (mask,) = call(mask_kernel, (place, sampling), [(cols // 128, cols, 128)], "mask", 1)
    flat = (2 * rows, zdim, cols)
    smooth, onward, stats = call(
        smooth_kernel, (place, gathered, d, w, r), [flat, flat, (2, 128)], "smooth", 1
    )
    (back,) = call(
        functools.partial(middle_kernel, zdim=zdim),
        (spectrum, mask, stats, forward, inverse),
        [(lines, 128)],
        "middle",
    )
    back = swap(back, slab_axes)
    (sums,) = call(
        combine_kernel,
        (place, back, sens, smooth, onward, wide),
        [(frames, 2 * rows + 1, zdim, cols)],
        "combine",
        1,
    )
    sums = lax.all_to_all(sums, "coil", 0, 0, tiled=True)

    near, far = ("y", "core"), ("z", "coil")
    new_x, new_r, norms, old = call(
        step_kernel,
        (sums, x.reshape(flat), r.reshape(flat), d.reshape(flat)),
        [flat, flat, (lax.axis_size(near), 1, 128), (1, 128)],
        "step",
    )
    norms = lax.all_to_all(norms, near, 0, 0, tiled=True)
    norms = jnp.broadcast_to(
        jnp.sum(norms, axis=0, keepdims=True), (lax.axis_size(far), 1, 128)
    )
    norms = lax.all_to_all(norms, far, 0, 0, tiled=True)
    new_d, norm = call(
        finish_kernel, (norms, old, new_r, d.reshape(flat)), [flat, (1, 128)], "finish"
    )

    def restore(values):
        return jnp.swapaxes(values.reshape(2, 1, rows, zdim, cols), 2, 3)

    return restore(new_x), restore(new_r), restore(new_d), norm[0, 0]


def solution(mesh):
    fine = Mesh(mesh.devices.reshape(8, 8, 2, 4), ("z", "y", "core", "coil"))
    image = P(None, "coil", None, slab_axes, None)
    return jax.shard_map(
        body,
        mesh=fine,
        in_specs=(image, image, image, image, P(), P("coil", None, slab_axes, None)),
        out_specs=(image, image, image, P()),
        check_vma=False,
    )
```

time: 154 us -> 154 us (level)
  starting transfers between devices: 29.4 us -> 20.5 us
  blocking collectives: 78.3 us -> 85.4 us
  local copies, waits for them, and re-layouts: 4.19 us -> 5.95 us
  waiting for transfers between devices: 29.1 us -> 30.7 us
    all_to_all x2 -> x1, waiting for transfers between devices: 10.6 us -> 30.7 us  [swap(): return lax.all_to_all(single, axis, 0, 0, tiled=True).reshape(values.shape)]
    ppermute x2 -> x0, waiting for transfers between devices: 18.6 us -> none  [the longest x1 18.6 us: body(): after = lax.ppermute(field[:2, 0], slab_axes, [(j, i) for i, j in up])]
    all_to_all x1 -> x2, blocking collectives: 43 us -> 49.9 us  [the longest x1 41.7 us: swap(): return lax.all_to_all(single, axis, 0, 0, tiled=True).reshape(values.shape)]
    ppermute x2 -> x0, starting transfers between devices: 5.56 us -> none  [the longest x1 2.8 us: body(): after = lax.ppermute(field[:2, 0], slab_axes, [(j, i) for i, j in up])]
    all_to_all x2 -> x1, starting transfers between devices: 23.9 us -> 20.5 us  [swap(): return lax.all_to_all(single, axis, 0, 0, tiled=True).reshape(values.shape)]
    unnamed x21 -> x28, local copies, waits for them, and re-layouts: 4.15 us -> 5.94 us
  transfers between devices with their start and end apart: 4 -> 1, of which waited for: 3 -> 1; matrix products, arithmetic and copies ran while one was open for 0% -> 0% of each run, Pallas kernels for 1% -> 1%
where the time goes in v1:
time: 154 us
  blocking collectives  85.4 us (55%)
  waiting for transfers between devices  30.7 us (20%)
  starting transfers between devices  20.5 us (13%)
  Pallas kernels  10.5 us (7%)
  local copies, waits for them, and re-layouts  5.95 us (4%)
    all_to_all x1, blocking collectives, swap(): return lax.all_to_all(single, axis, 0, 0, tiled=True).reshape(values.shape)  41.7 us
    all_to_all x1, waiting for transfers between devices, swap(): return lax.all_to_all(single, axis, 0, 0, tiled=True).reshape(values.shape)  30.7 us
    all_to_all x1, starting transfers between devices, swap(): return lax.all_to_all(single, axis, 0, 0, tiled=True).reshape(values.shape)  20.5 us
    all_to_all x1, blocking collectives, body(): norms = lax.all_to_all(norms, near, 0, 0, tiled=True)  13 us
    all_to_all x1, blocking collectives, body(): norms = lax.all_to_all(norms, far, 0, 0, tiled=True)  11.9 us
    all_gather x1, blocking collectives, body(): gathered = lax.all_gather(direction, 'coil', axis=1, tiled=True)  10.6 us
    pallas_call x7, Pallas kernels, call(): pl.pallas_call(kernel, out_shape=shapes, in_specs=[smem] * scalars + [vme...  10.5 us
    all_to_all x1, blocking collectives, body(): sums = lax.all_to_all(sums, 'coil', 0, 0, tiled=True)  8.24 us
  transfers between devices with their start and end apart: 1, of which 1 were waited for; matrix products, arithmetic and copies ran while one was open for 0% of the time, Pallas kernels for 1%

profile of v1, /device:TPU:1, one launch (start us, length us, event | category | flops | bytes accessed | tf_op | source)
XLA Modules:
  0.0 153.8 jit_solution(11742536824594095300)
XLA Ops:
  0.6 10.6 %all_gather.3 = f32[2,4,4,3,384]{4,2,3,1,0:T(4,128)S(1)} all-gather(f32[2,1,4,3,384]{4,2,3,1,0:T(4,128)} %param.12), channel_id=1, replica_groups=mesh['z'=8,'y'=8,'core'=2,'coil'=4] {'coil'}, dimensions={1}, use_global_device_ids=true | all-gather | bytes 184320 | tf_op jit(solution)/shard_map/all_gather | solution.py:318
  11.2 0.0 copy-start.1
  11.2 0.8 copy-done.1
  12.0 0.0 copy-start.5
  12.0 0.9 copy-done.5
  12.9 0.0 copy-start.8
  12.9 1.1 copy-done.8
  13.9 0.0 copy-start.10
  13.9 0.7 copy-done.10
  14.6 2.2 %images.1 = f32[2432,128]{1,0:T(8,128)} custom-call(bf16[2,8,3,4,384]{4,3,2,1,0:T(4,128)(2,1)S(1)} %bitcast.58, f32[2,4,3,4,384]{4,3,2,1,0:T(4,128)S(1)} %bitcast.52, f32[2,3,4,384]{3,2,1,0:T(4,128)S(1)} %bitcast.54, s32[3,4,384]{2,1,0:T(4,128)S(1)} %bitcast.62, bf16[768,384]{1,0:T(8,128)(2,1)S(1)} %copy-done.8), custom_call_target="tpu_custom_call" | custom-call | tf_op jit(solution)/shard_map/images/pallas_call | solution.py:283
  16.9 20.5 %all-to-all-start = ((f32[2432,1,128]{2,1,0:T(1,128)}), f32[2432,1,128]{2,1,0:T(1,128)S(1)}, u32[]{:S(2)}, u32[]{:S(2)}) async-start(f32[2432,1,128]{2,1,0:T(1,128)} %bitcast.10), calls=%async_computation | async-start | bytes 2490368 | tf_op jit(solution)/shard_map/all_to_all | solution.py:295
  37.4 0.1 pad_add_fusion.place_ref
  37.5 0.0 copy-start
  37.5 1.7 %copy-done = s32[4,384,384]{2,1,0:T(8,128)S(1)} copy-done((s32[4,384,384]{2,1,0:T(8,128)S(1)}, s32[4,384,384]{2,1,0:T(8,128)}, u32[]{:S(2)}) %copy-start) | copy-done | bytes 2359320
  39.1 0.0 copy-start.2
  39.1 0.0 copy-start.9
  39.1 0.0 copy-start.11
  39.1 0.0 copy-start.3
  39.1 0.0 copy-start.4
  39.2 1.4 mask.1.mask_ref
  40.6 0.0 copy-done.2
  40.6 0.0 copy-done.9
  40.6 0.0 copy-done.11
  40.6 0.8 smooth.1
  41.4 30.7 %all-to-all-done = f32[2432,1,128]{2,1,0:T(1,128)S(1)} async-done(((f32[2432,1,128]{2,1,0:T(1,128)}), f32[2432,1,128]{2,1,0:T(1,128)S(1)}, u32[]{:S(2)}, u32[]{:S(2)}) %all-to-all-start) | async-done | bytes 1245216 | tf_op jit(solution)/shard_map/all_to_all | solution.py:295
  72.1 0.0 copy-done.3
  72.1 0.0 copy-done.4
  72.1 2.7 %middle.1 = f32[2432,128]{1,0:T(8,128)S(1)} custom-call(f32[2432,128]{1,0:T(8,128)S(1)} %bitcast.49, f32[3,384,128]{2,1,0:T(8,128)S(1)} %mask.1.mask_ref, f32[2,128]{1,0:T(2,128)S(1)} %get-tuple-element.13.stats_ref, bf16[768,384]{1,0:T(8,128)(2,1)S(1)} %copy-done.3, bf16[768,384]{1,0:T(8,128)(2,1)S(1)} %copy-done.4), custom_call_target="tpu_custom_call" | custom-call | tf_op jit(solution)/shard_map/middle/pallas_call | solution.py:283
  74.9 0.0 copy-start.6
  74.9 0.0 copy-start.7
  74.9 41.7 %all_to_all.25 = f32[2432,1,128]{2,1,0:T(1,128)S(1)} all-to-all(f32[2432,1,128]{2,1,0:T(1,128)S(1)} %bitcast.51), channel_id=1, replica_groups=mesh['z'=8,'y'=8,'core'=2,'coil'=4] {'z','y','core'}, dimensions={0} | all-to-all | bytes 2490368 | tf_op jit(solution)/shard_map/all_to_all | solution.py:295
  116.6 0.0 copy-done.6
  116.6 0.0 copy-done.7
  116.6 0.0 copy-start.12
  116.6 1.8 %combine.1 = f32[4,7,4,384]{3,2,1,0:T(4,128)S(1)} custom-call(s32[3]{0:T(128)S(1)} %pad_add_fusion.place_ref, f32[2432,128]{1,0:T(8,128)S(1)} %bitcast.50, bf16[2,8,3,4,384]{4,3,2,1,0:T(4,128)(2,1)S(1)} %bitcast.59, f32[6,4,384]{2,1,0:T(4,128)S(1)} %get-tuple-element.14.smooth_ref, f32[6,4,384]{2,1,0:T(4,128)S(1)} %get-tuple-element.15.next_ref, ...), custom_call_target="tpu_custom_call" | custom-call | tf_op jit(solution)/shard_map/combine/pallas_call | solution.py:283
  118.4 8.2 %all_to_all.26.sums_ref = f32[4,7,4,384]{3,2,1,0:T(4,128)S(1)} all-to-all(f32[4,7,4,384]{3,2,1,0:T(4,128)S(1)} %combine.1), channel_id=1, replica_groups=mesh['z'=8,'y'=8,'core'=2,'coil'=4] {'coil'}, dimensions={0} | all-to-all | bytes 344064 | tf_op jit(solution)/shard_map/all_to_all | solution.py:343
  126.6 0.0 copy-done.12
  126.6 0.7 step.1
  127.3 13.0 %all_to_all.27 = f32[16,1,128]{2,1,0:T(1,128)S(1)} all-to-all(f32[16,1,128]{2,1,0:T(1,128)S(1)} %get-tuple-element.18), channel_id=1, replica_groups=mesh['z'=8,'y'=8,'core'=2,'coil'=4] {'y','core'}, dimensions={0} | all-to-all | bytes 16384 | tf_op jit(solution)/shard_map/all_to_all | solution.py:352
  140.4 11.9 %all_to_all.28.norms_ref = f32[32,1,128]{2,1,0:T(1,128)S(1)} all-to-all(f32[32,1,128]{2,1,0:T(1,128)S(1)} %broadcast_in_dim.2), channel_id=1, replica_groups=mesh['z'=8,'y'=8,'core'=2,'coil'=4] {'z','coil'}, dimensions={0} | all-to-all | bytes 32768 | tf_op jit(solution)/shard_map/all_to_all | solution.py:356
  152.2 0.0 copy-start.13
  152.2 0.8 copy-done.13
  153.0 0.8 finish.1
  (2 shorter events, 0.0 us)
Async XLA Ops:
  11.2 0.8 copy-start.1
  12.0 0.9 copy-start.5
  12.9 1.1 copy-start.8
  13.9 0.7 copy-start.10
  16.9 55.2 %all-to-all-start = ((f32[2432,1,128]{2,1,0:T(1,128)}), f32[2432,1,128]{2,1,0:T(1,128)S(1)}, u32[]{:S(2)}, u32[]{:S(2)}) async-start(f32[2432,1,128]{2,1,0:T(1,128)} %bitcast.10), calls=%async_computation | async-start | bytes 2490368 | tf_op jit(solution)/shard_map/all_to_all | solution.py:295
  37.5 1.7 %copy-start = (s32[4,384,384]{2,1,0:T(8,128)S(1)}, s32[4,384,384]{2,1,0:T(8,128)}, u32[]{:S(2)}) copy-start(s32[4,384,384]{2,1,0:T(8,128)} %sampling_ref.1) | copy-start | bytes 7077892
  39.1 1.5 copy-start.2
  39.1 1.5 copy-start.9
  39.1 1.5 copy-start.11
  39.1 33.0 %copy-start.3 = (bf16[768,384]{1,0:T(8,128)(2,1)S(1)}, bf16[768,384]{1,0:T(8,128)(2,1)}, u32[]{:S(2)}) copy-start(bf16[768,384]{1,0:T(8,128)(2,1)} %constant.34.clone.forward_ref) | copy-start | bytes 1769476
  39.1 33.0 %copy-start.4 = (bf16[768,384]{1,0:T(8,128)(2,1)S(1)}, bf16[768,384]{1,0:T(8,128)(2,1)}, u32[]{:S(2)}) copy-start(bf16[768,384]{1,0:T(8,128)(2,1)} %constant.35.clone.inverse_ref) | copy-start | bytes 1769476
  74.9 41.7 %copy-start.6 = (bf16[2,8,4,3,384]{4,2,3,1,0:T(4,128)(2,1)S(1)}, bf16[2,8,4,3,384]{4,2,3,1,0:T(4,128)(2,1)}, u32[]{:S(2)}) copy-start(bf16[2,8,4,3,384]{4,2,3,1,0:T(4,128)(2,1)} %param.13) | copy-start | bytes 442372
  74.9 41.7 %copy-start.7 = (bf16[384,768]{1,0:T(8,128)(2,1)S(1)}, bf16[384,768]{1,0:T(8,128)(2,1)}, u32[]{:S(2)}) copy-start(bf16[384,768]{1,0:T(8,128)(2,1)} %constant.36.clone.table_ref) | copy-start | bytes 1769476
  116.6 10.0 %copy-start.12 = (f32[2,1,4,3,384]{4,2,3,1,0:T(4,128)S(1)}, f32[2,1,4,3,384]{4,2,3,1,0:T(4,128)}, u32[]{:S(2)}) copy-start(f32[2,1,4,3,384]{4,2,3,1,0:T(4,128)} %param.10) | copy-start | bytes 110596
  152.2 0.8 copy-start.13

commit v2 on v1

--- a/solution.py
+++ b/solution.py
@@ -45,9 +45,21 @@
     return jnp.concatenate(pieces, axis=0)
 
 
-def images_kernel(sens_ref, all_ref, own_ref, weight_ref, table_ref, out_ref):
+def fetch_kernel(field_ref, *refs):
+    count = (len(refs) - 2) // 2
+    sources, copies_ref, held, done = refs[:count], refs[count], refs[count + 1 : -1], refs[-1]
+    copies = [(sources[i], held[i]) for i in range(count)]
+    copies += [(field_ref, copies_ref.at[i]) for i in range(copies_ref.shape[0])]
+    copies = [pltpu.make_async_copy(a, b, done.at[i]) for i, (a, b) in enumerate(copies)]
+    for copy in copies:
+        copy.start()
+    for copy in copies:
+        copy.wait()
+
+
+def images_kernel(all_ref, sens_ref, table_ref, own_ref, weight_ref, out_ref):
     coils, rows, zdim = sens_ref.shape[1:4]
-    frames = all_ref.shape[1]
+    frames = all_ref.shape[0]
     table = table_ref[...]
     table = jnp.concatenate([table, table], axis=1)
     half = table.shape[0] // 2
@@ -57,8 +69,8 @@
         s_im = sens_rows(sens_ref, 1, r, coils)
         real, imag = [], []
         for f in range(frames):
-            d_re = jnp.concatenate([all_ref[0, f, r]] * coils, axis=0)
-            d_im = jnp.concatenate([all_ref[1, f, r]] * coils, axis=0)
+            d_re = jnp.concatenate([all_ref[f, 0, r]] * coils, axis=0)
+            d_im = jnp.concatenate([all_ref[f, 1, r]] * coils, axis=0)
             real.append(s_re * d_re - s_im * d_im)
             imag.append(s_re * d_im + s_im * d_re)
         upper, lower = split(jnp.concatenate(real + imag, axis=0))
@@ -109,7 +121,7 @@
         weight = weight_ref[r].astype(f32)
         for p in range(2):
             v = own_ref[p, r]
-            rise = all_ref[p, later, r] - v
+            rise = all_ref[later, p, r] - v
             onward = smooth_scale * (weight * rise)
             flux = weight[:-1] * (v[1:] - v[:-1])
             term = jnp.concatenate([zero_slice, flux], axis=0)
@@ -241,7 +253,7 @@
 
 
 def step_kernel(
-    sums_ref, iterate_ref, residual_ref, direction_ref, new_iterate_ref, new_residual_ref, norms_ref, old_ref
+    sums_ref, iterate_ref, residual_ref, direction_ref, new_iterate_ref, new_residual_ref, kept_ref, norms_ref, old_ref
 ):
     planes = residual_ref.shape[0]
     sources = sums_ref.shape[0]
@@ -260,6 +272,7 @@
         new_iterate_ref[i] = iterate_ref[i] + step * direction_ref[i]
         fresh = residual_ref[i] - step * total(i)
         new_residual_ref[i] = fresh
+        kept_ref[i] = fresh
         norm = norm + lanes(fresh * fresh)
     norms_ref[...] = jnp.broadcast_to(norm[None], norms_ref.shape)
     old_ref[...] = jnp.broadcast_to(old_norm, old_ref.shape)
@@ -276,18 +289,34 @@
 
 vmem = pl.BlockSpec(memory_space=pltpu.VMEM)
 smem = pl.BlockSpec(memory_space=pltpu.SMEM)
+hbm = pl.BlockSpec(memory_space=pltpu.HBM)
+
+
+params = pltpu.CompilerParams(vmem_limit_bytes=40 * 1024 * 1024)
 
 
 def call(kernel, ins, outs, name, scalars=0):
-    shapes = [jax.ShapeDtypeStruct(s, f32) for s in outs]
     return pl.pallas_call(
         kernel,
-        out_shape=shapes,
+        out_shape=[jax.ShapeDtypeStruct(s, f32) for s in outs],
         in_specs=[smem] * scalars + [vmem] * (len(ins) - scalars),
         out_specs=[vmem] * len(outs),
-        compiler_params=pltpu.CompilerParams(vmem_limit_bytes=40 * 1024 * 1024),
+        compiler_params=params,
         name=name,
     )(*ins)
+
+
+def fetch(field, copies, others):
+    shapes = [((copies,) + field.shape, field.dtype)] + [(a.shape, a.dtype) for a in others]
+    return pl.pallas_call(
+        fetch_kernel,
+        out_shape=[jax.ShapeDtypeStruct(*s) for s in shapes],
+        in_specs=[hbm] * (1 + len(others)),
+        out_specs=[vmem] * len(shapes),
+        scratch_shapes=[pltpu.SemaphoreType.DMA((copies + len(others),))],
+        compiler_params=params,
+        name="fetch",
+    )(field, *others)
 
 
 def swap(values, axis):
@@ -315,11 +344,11 @@
 
     place = jnp.stack([lax.axis_index(slab_axes), lax.axis_index("coil"), jnp.int32(frames)])
     place = place.astype(jnp.int32)
-    gathered = lax.all_gather(direction, "coil", axis=1, tiled=True)
-    gathered = jnp.swapaxes(gathered, 2, 3)
+    copies, *near_by = fetch(d, frames, (sens, natural, d, w))
+    gathered = lax.all_to_all(copies, "coil", 0, 0, tiled=True)
 
     lines = slabs * message
-    (spectrum,) = call(images_kernel, (sens, gathered, d, w, natural), [(lines, 128)], "images")
+    (spectrum,) = call(images_kernel, (gathered, *near_by), [(lines, 128)], "images")
     spectrum = swap(spectrum, slab_axes)
     (mask,) = call(mask_kernel, (place, sampling), [(cols // 128, cols, 128)], "mask", 1)
     flat = (2 * rows, zdim, cols)
@@ -343,10 +372,10 @@
     sums = lax.all_to_all(sums, "coil", 0, 0, tiled=True)
 
     near, far = ("y", "core"), ("z", "coil")
-    new_x, new_r, norms, old = call(
+    new_x, new_r, kept, norms, old = call(
         step_kernel,
         (sums, x.reshape(flat), r.reshape(flat), d.reshape(flat)),
-        [flat, flat, (lax.axis_size(near), 1, 128), (1, 128)],
+        [flat, flat, flat, (lax.axis_size(near), 1, 128), (1, 128)],
         "step",
     )
     norms = lax.all_to_all(norms, near, 0, 0, tiled=True)
@@ -355,7 +384,7 @@
     )
     norms = lax.all_to_all(norms, far, 0, 0, tiled=True)
     new_d, norm = call(
-        finish_kernel, (norms, old, new_r, d.reshape(flat)), [flat, (1, 128)], "finish"
+        finish_kernel, (norms, old, kept, d.reshape(flat)), [flat, (1, 128)], "finish"
     )
 
     def restore(values):

time: 154 us -> 151 us (0.981)
  blocking collectives: 85.4 us -> 83.3 us
    all_gather x1 -> x0, blocking collectives: 10.6 us -> none  [body(): gathered = lax.all_gather(direction, 'coil', axis=1, tiled=True)]
    all_to_all x0 -> x1, blocking collectives: none -> 9.56 us  [body(): gathered = lax.all_to_all(copies, 'coil', 0, 0, tiled=True)]
    unnamed x28 -> x26, local copies, waits for them, and re-layouts: 5.94 us -> 5.16 us
    pallas_call x7 -> x8, Pallas kernels: 10.5 us -> 11.1 us  [the longest x7 10.5 us: call(): pl.pallas_call(kernel, out_shape=[jax.ShapeDtypeStruct(s, f32) for s in o...]
where the time goes in v2:
time: 151 us; the launch traced here: 150 us
  blocking collectives  83.3 us (55%)
  waiting for transfers between devices  30.7 us (20%)
  starting transfers between devices  19 us (13%)
  Pallas kernels  11.1 us (7%)
  local copies, waits for them, and re-layouts  5.18 us (3%)
    all_to_all x1, blocking collectives, swap(): return lax.all_to_all(single, axis, 0, 0, tiled=True).reshape(values.shape)  41.7 us
    all_to_all x1, waiting for transfers between devices, swap(): return lax.all_to_all(single, axis, 0, 0, tiled=True).reshape(values.shape)  30.7 us
    all_to_all x1, starting transfers between devices, swap(): return lax.all_to_all(single, axis, 0, 0, tiled=True).reshape(values.shape)  19 us
    all_to_all x1, blocking collectives, body(): norms = lax.all_to_all(norms, near, 0, 0, tiled=True)  12.6 us
    all_to_all x1, blocking collectives, body(): norms = lax.all_to_all(norms, far, 0, 0, tiled=True)  11.9 us
    pallas_call x7, Pallas kernels, call(): pl.pallas_call(kernel, out_shape=[jax.ShapeDtypeStruct(s, f32) for s in o...  10.5 us
    all_to_all x1, blocking collectives, body(): gathered = lax.all_to_all(copies, 'coil', 0, 0, tiled=True)  9.56 us
    all_to_all x1, blocking collectives, body(): sums = lax.all_to_all(sums, 'coil', 0, 0, tiled=True)  7.48 us
  transfers between devices with their start and end apart: 1, of which 1 were waited for; matrix products, arithmetic and copies ran while one was open for 0% of the time, Pallas kernels for 1%

profile of v2, /device:TPU:1, one launch (start us, length us, event | category | flops | bytes accessed | tf_op | source)
XLA Modules:
  0.0 150.1 jit_solution(11218479525725946715)
XLA Ops:
  0.6 0.0 copy-start.1
  0.6 0.8 copy-done.1
  1.4 0.0 copy-start.5
  1.4 0.9 copy-done.5
  2.3 0.0 copy-start.8
  2.3 1.1 copy-done.8
  3.4 0.0 copy-start.10
  3.4 0.7 copy-done.10
  4.1 0.6 fetch.1
  4.7 9.6 %all_to_all.30.all_ref = f32[4,2,3,4,384]{4,3,2,1,0:T(4,128)S(1)} all-to-all(f32[4,2,3,4,384]{4,3,2,1,0:T(4,128)S(1)} %get-tuple-element.19), channel_id=1, replica_groups=mesh['z'=8,'y'=8,'core'=2,'coil'=4] {'coil'}, dimensions={0} | all-to-all | bytes 294912 | tf_op jit(solution)/shard_map/all_to_all | solution.py:348
  14.3 2.2 %images.1 = f32[2432,128]{1,0:T(8,128)} custom-call(f32[4,2,3,4,384]{4,3,2,1,0:T(4,128)S(1)} %all_to_all.30.all_ref, bf16[2,8,3,4,384]{4,3,2,1,0:T(4,128)(2,1)S(1)} %get-tuple-element.20.sens_ref, bf16[768,384]{1,0:T(8,128)(2,1)S(1)} %get-tuple-element.21.table_ref, f32[2,3,4,384]{3,2,1,0:T(4,128)S(1)} %get-tuple-element.22.own_ref, ...), custom_call_target="tpu_custom_call" | custom-call | tf_op jit(solution)/shard_map/images/pallas_call | solution.py:299
  16.5 19.0 %all-to-all-start.1 = ((f32[2432,1,128]{2,1,0:T(1,128)}), f32[2432,1,128]{2,1,0:T(1,128)S(1)}, u32[]{:S(2)}, u32[]{:S(2)}) async-start(f32[2432,1,128]{2,1,0:T(1,128)} %bitcast.9), calls=%async_computation.1 | async-start | bytes 2490368 | tf_op jit(solution)/shard_map/all_to_all | solution.py:324
  35.6 0.1 pad_add_fusion.place_ref
  35.6 0.0 copy-start
  35.6 1.7 %copy-done = s32[4,384,384]{2,1,0:T(8,128)S(1)} copy-done((s32[4,384,384]{2,1,0:T(8,128)S(1)}, s32[4,384,384]{2,1,0:T(8,128)}, u32[]{:S(2)}) %copy-start) | copy-done | bytes 2359320
  37.3 0.0 copy-start.2
  37.3 0.0 copy-start.9
  37.3 0.0 copy-start.11
  37.3 0.0 copy-start.3
  37.3 0.0 copy-start.4
  37.3 1.4 mask.1.mask_ref
  38.8 0.0 copy-done.2
  38.8 0.0 copy-done.9
  38.8 0.0 copy-done.11
  38.8 0.8 smooth.1
  39.6 30.7 %all-to-all-done.1 = f32[2432,1,128]{2,1,0:T(1,128)S(1)} async-done(((f32[2432,1,128]{2,1,0:T(1,128)}), f32[2432,1,128]{2,1,0:T(1,128)S(1)}, u32[]{:S(2)}, u32[]{:S(2)}) %all-to-all-start.1) | async-done | bytes 1245216 | tf_op jit(solution)/shard_map/all_to_all | solution.py:324
  70.3 0.0 copy-done.3
  70.3 0.0 copy-done.4
  70.3 2.7 %middle.1 = f32[2432,128]{1,0:T(8,128)S(1)} custom-call(f32[2432,128]{1,0:T(8,128)S(1)} %bitcast.48, f32[3,384,128]{2,1,0:T(8,128)S(1)} %mask.1.mask_ref, f32[2,128]{1,0:T(2,128)S(1)} %get-tuple-element.24.stats_ref, bf16[768,384]{1,0:T(8,128)(2,1)S(1)} %copy-done.3, bf16[768,384]{1,0:T(8,128)(2,1)S(1)} %copy-done.4), custom_call_target="tpu_custom_call" | custom-call | tf_op jit(solution)/shard_map/middle/pallas_call | solution.py:299
  73.1 0.0 copy-start.6
  73.1 0.0 copy-start.7
  73.1 41.7 %all_to_all.31 = f32[2432,1,128]{2,1,0:T(1,128)S(1)} all-to-all(f32[2432,1,128]{2,1,0:T(1,128)S(1)} %bitcast.50), channel_id=1, replica_groups=mesh['z'=8,'y'=8,'core'=2,'coil'=4] {'z','y','core'}, dimensions={0} | all-to-all | bytes 2490368 | tf_op jit(solution)/shard_map/all_to_all | solution.py:324
  114.8 0.0 copy-done.6
  114.8 0.0 copy-done.7
  114.8 0.0 copy-start.12
  114.8 1.8 %combine.1 = f32[4,7,4,384]{3,2,1,0:T(4,128)S(1)} custom-call(s32[3]{0:T(128)S(1)} %pad_add_fusion.place_ref, f32[2432,128]{1,0:T(8,128)S(1)} %bitcast.49, bf16[2,8,3,4,384]{4,3,2,1,0:T(4,128)(2,1)S(1)} %bitcast.57, f32[6,4,384]{2,1,0:T(4,128)S(1)} %get-tuple-element.25.smooth_ref, f32[6,4,384]{2,1,0:T(4,128)S(1)} %get-tuple-element.26.next_ref, ...), custom_call_target="tpu_custom_call" | custom-call | tf_op jit(solution)/shard_map/combine/pallas_call | solution.py:299
  116.6 7.5 %all_to_all.32.sums_ref = f32[4,7,4,384]{3,2,1,0:T(4,128)S(1)} all-to-all(f32[4,7,4,384]{3,2,1,0:T(4,128)S(1)} %combine.1), channel_id=1, replica_groups=mesh['z'=8,'y'=8,'core'=2,'coil'=4] {'coil'}, dimensions={0} | all-to-all | bytes 344064 | tf_op jit(solution)/shard_map/all_to_all | solution.py:372
  124.1 0.0 copy-done.12
  124.1 0.7 step.1
  124.7 12.6 %all_to_all.33 = f32[16,1,128]{2,1,0:T(1,128)S(1)} all-to-all(f32[16,1,128]{2,1,0:T(1,128)S(1)} %get-tuple-element.29), channel_id=1, replica_groups=mesh['z'=8,'y'=8,'core'=2,'coil'=4] {'y','core'}, dimensions={0} | all-to-all | bytes 16384 | tf_op jit(solution)/shard_map/all_to_all | solution.py:381
  137.4 11.9 %all_to_all.34.norms_ref = f32[32,1,128]{2,1,0:T(1,128)S(1)} all-to-all(f32[32,1,128]{2,1,0:T(1,128)S(1)} %broadcast_in_dim.2), channel_id=1, replica_groups=mesh['z'=8,'y'=8,'core'=2,'coil'=4] {'z','coil'}, dimensions={0} | all-to-all | bytes 32768 | tf_op jit(solution)/shard_map/all_to_all | solution.py:385
  149.3 0.8 finish.1
  (2 shorter events, 0.0 us)
Async XLA Ops:
  0.6 0.8 copy-start.1
  1.4 0.9 copy-start.5
  2.3 1.1 copy-start.8
  3.4 0.7 copy-start.10
  16.5 53.8 %all-to-all-start.1 = ((f32[2432,1,128]{2,1,0:T(1,128)}), f32[2432,1,128]{2,1,0:T(1,128)S(1)}, u32[]{:S(2)}, u32[]{:S(2)}) async-start(f32[2432,1,128]{2,1,0:T(1,128)} %bitcast.9), calls=%async_computation.1 | async-start | bytes 2490368 | tf_op jit(solution)/shard_map/all_to_all | solution.py:324
  35.6 1.7 %copy-start = (s32[4,384,384]{2,1,0:T(8,128)S(1)}, s32[4,384,384]{2,1,0:T(8,128)}, u32[]{:S(2)}) copy-start(s32[4,384,384]{2,1,0:T(8,128)} %sampling_ref.1) | copy-start | bytes 7077892
  37.3 1.5 copy-start.2
  37.3 1.5 copy-start.9
  37.3 1.5 copy-start.11
  37.3 33.0 %copy-start.3 = (bf16[768,384]{1,0:T(8,128)(2,1)S(1)}, bf16[768,384]{1,0:T(8,128)(2,1)}, u32[]{:S(2)}) copy-start(bf16[768,384]{1,0:T(8,128)(2,1)} %constant.34.clone.forward_ref) | copy-start | bytes 1769476
  37.3 33.0 %copy-start.4 = (bf16[768,384]{1,0:T(8,128)(2,1)S(1)}, bf16[768,384]{1,0:T(8,128)(2,1)}, u32[]{:S(2)}) copy-start(bf16[768,384]{1,0:T(8,128)(2,1)} %constant.35.clone.inverse_ref) | copy-start | bytes 1769476
  73.1 41.7 %copy-start.6 = (bf16[2,8,4,3,384]{4,2,3,1,0:T(4,128)(2,1)S(1)}, bf16[2,8,4,3,384]{4,2,3,1,0:T(4,128)(2,1)}, u32[]{:S(2)}) copy-start(bf16[2,8,4,3,384]{4,2,3,1,0:T(4,128)(2,1)} %param.13) | copy-start | bytes 442372
  73.1 41.7 %copy-start.7 = (bf16[384,768]{1,0:T(8,128)(2,1)S(1)}, bf16[384,768]{1,0:T(8,128)(2,1)}, u32[]{:S(2)}) copy-start(bf16[384,768]{1,0:T(8,128)(2,1)} %constant.36.clone.table_ref) | copy-start | bytes 1769476
  114.8 9.3 %copy-start.12 = (f32[2,1,4,3,384]{4,2,3,1,0:T(4,128)S(1)}, f32[2,1,4,3,384]{4,2,3,1,0:T(4,128)}, u32[]{:S(2)}) copy-start(f32[2,1,4,3,384]{4,2,3,1,0:T(4,128)} %param.10) | copy-start | bytes 110596

commit v3 on v1

--- a/solution.py
+++ b/solution.py
@@ -45,20 +45,34 @@
     return jnp.concatenate(pieces, axis=0)
 
 
-def images_kernel(sens_ref, all_ref, own_ref, weight_ref, table_ref, out_ref):
+def prepare_kernel(sens_ref, table_ref, own_ref, weight_ref, sens_out_ref, table_out_ref, extra_ref):
     coils, rows, zdim = sens_ref.shape[1:4]
-    frames = all_ref.shape[1]
+    for p in range(2):
+        for r in range(rows):
+            sens_out_ref[p, r] = sens_rows(sens_ref, p, r, coils)
+    table_out_ref[...] = table_ref[...]
+    groups = own_ref.shape[3] // 128
+    pieces = []
+    for r in range(rows):
+        for values in (own_ref[0, r], own_ref[1, r], weight_ref[r].astype(f32)):
+            pieces += [values[:, j * 128 : (j + 1) * 128] for j in range(groups)]
+    pieces.append(jnp.zeros((128 - len(pieces) * zdim, 128), f32))
+    extra_ref[...] = jnp.concatenate(pieces, axis=0).T
+
+
+def images_kernel(all_ref, sens_ref, table_ref, extra_ref, out_ref):
+    frames, _, rows, zdim, _ = all_ref.shape
+    coils = sens_ref.shape[2] // zdim
     table = table_ref[...]
     table = jnp.concatenate([table, table], axis=1)
     half = table.shape[0] // 2
     groups = half // 128
     for r in range(rows):
-        s_re = sens_rows(sens_ref, 0, r, coils)
-        s_im = sens_rows(sens_ref, 1, r, coils)
+        s_re, s_im = sens_ref[0, r], sens_ref[1, r]
         real, imag = [], []
         for f in range(frames):
-            d_re = jnp.concatenate([all_ref[0, f, r]] * coils, axis=0)
-            d_im = jnp.concatenate([all_ref[1, f, r]] * coils, axis=0)
+            d_re = jnp.concatenate([all_ref[f, 0, r]] * coils, axis=0)
+            d_im = jnp.concatenate([all_ref[f, 1, r]] * coils, axis=0)
             real.append(s_re * d_re - s_im * d_im)
             imag.append(s_re * d_im + s_im * d_re)
         upper, lower = split(jnp.concatenate(real + imag, axis=0))
@@ -69,12 +83,7 @@
             at = (j * rows + r) * 2
             out_ref[pl.ds(at, 128, stride=message), :] = re[j * 128 : (j + 1) * 128]
             out_ref[pl.ds(at + 1, 128, stride=message), :] = im[j * 128 : (j + 1) * 128]
-    pieces = []
-    for r in range(rows):
-        for values in (own_ref[0, r], own_ref[1, r], weight_ref[r].astype(f32)):
-            pieces += [values[:, j * 128 : (j + 1) * 128] for j in range(groups)]
-    pieces.append(jnp.zeros((128 - len(pieces) * zdim, 128), f32))
-    out_ref[pl.ds(extra, 128, stride=message), :] = jnp.concatenate(pieces, axis=0).T
+    out_ref[pl.ds(extra, 128, stride=message), :] = extra_ref[...]
 
 
 def mask_kernel(place_ref, sampling_ref, out_ref):
@@ -109,7 +118,7 @@
         weight = weight_ref[r].astype(f32)
         for p in range(2):
             v = own_ref[p, r]
-            rise = all_ref[p, later, r] - v
+            rise = all_ref[later, p, r] - v
             onward = smooth_scale * (weight * rise)
             flux = weight[:-1] * (v[1:] - v[:-1])
             term = jnp.concatenate([zero_slice, flux], axis=0)
@@ -189,12 +198,11 @@
 
 def combine_kernel(place_ref, in_ref, sens_ref, smooth_ref, next_ref, table_ref, out_ref):
     frame, frame_count = place_ref[1], place_ref[2]
-    coils, rows, zdim, cols = sens_ref.shape[1:]
-    frames = out_ref.shape[0]
+    frames, _, zdim, cols = out_ref.shape
+    rows, span = sens_ref.shape[1:3]
     table = table_ref[...]
     table = jnp.concatenate([table, table], axis=0)
     groups = cols // 128
-    span = coils * zdim
     for r in range(rows):
         real, imag = [], []
         for j in range(groups):
@@ -208,8 +216,7 @@
         got = mm(jnp.concatenate([upper, lower], axis=1), table, ((1,), (0,)))
         re = got[:128, :cols] - got[128:, cols:]
         im = got[128:, :cols] + got[:128, cols:]
-        s_re = sens_rows(sens_ref, 0, r, coils)
-        s_im = sens_rows(sens_ref, 1, r, coils)
+        s_re, s_im = sens_ref[0, r], sens_ref[1, r]
         for f in range(frames):
             b_re = re[f * span : (f + 1) * span]
             b_im = im[f * span : (f + 1) * span]
@@ -241,7 +248,7 @@
 
 
 def step_kernel(
-    sums_ref, iterate_ref, residual_ref, direction_ref, new_iterate_ref, new_residual_ref, norms_ref, old_ref
+    sums_ref, iterate_ref, residual_ref, direction_ref, new_iterate_ref, new_residual_ref, kept_ref, norms_ref, old_ref
 ):
     planes = residual_ref.shape[0]
     sources = sums_ref.shape[0]
@@ -260,6 +267,7 @@
         new_iterate_ref[i] = iterate_ref[i] + step * direction_ref[i]
         fresh = residual_ref[i] - step * total(i)
         new_residual_ref[i] = fresh
+        kept_ref[i] = fresh
         norm = norm + lanes(fresh * fresh)
     norms_ref[...] = jnp.broadcast_to(norm[None], norms_ref.shape)
     old_ref[...] = jnp.broadcast_to(old_norm, old_ref.shape)
@@ -278,14 +286,19 @@
 smem = pl.BlockSpec(memory_space=pltpu.SMEM)
 
 
+params = pltpu.CompilerParams(vmem_limit_bytes=40 * 1024 * 1024)
+
+
 def call(kernel, ins, outs, name, scalars=0):
-    shapes = [jax.ShapeDtypeStruct(s, f32) for s in outs]
     return pl.pallas_call(
         kernel,
-        out_shape=shapes,
+        out_shape=[
+            jax.ShapeDtypeStruct(s, f32) if isinstance(s, tuple) else jax.ShapeDtypeStruct(s.shape, s.dtype)
+            for s in outs
+        ],
         in_specs=[smem] * scalars + [vmem] * (len(ins) - scalars),
         out_specs=[vmem] * len(outs),
-        compiler_params=pltpu.CompilerParams(vmem_limit_bytes=40 * 1024 * 1024),
+        compiler_params=params,
         name=name,
     )(*ins)
 
@@ -315,11 +328,17 @@
 
     place = jnp.stack([lax.axis_index(slab_axes), lax.axis_index("coil"), jnp.int32(frames)])
     place = place.astype(jnp.int32)
-    gathered = lax.all_gather(direction, "coil", axis=1, tiled=True)
-    gathered = jnp.swapaxes(gathered, 2, 3)
+    copies = jnp.broadcast_to(d[None], (frames,) + d.shape)
+    gathered = lax.all_to_all(copies, "coil", 0, 0, tiled=True)
+    sens_shape = (2, rows, sens.shape[1] * zdim, cols)
+    sens, natural, extras = call(
+        prepare_kernel, (sens, natural, d, w), [sens_shape, natural, (128, 128)], "prepare"
+    )
 
     lines = slabs * message
-    (spectrum,) = call(images_kernel, (sens, gathered, d, w, natural), [(lines, 128)], "images")
+    (spectrum,) = call(
+        images_kernel, (gathered, sens, natural, extras), [(lines, 128)], "images"
+    )
     spectrum = swap(spectrum, slab_axes)
     (mask,) = call(mask_kernel, (place, sampling), [(cols // 128, cols, 128)], "mask", 1)
     flat = (2 * rows, zdim, cols)
@@ -343,10 +362,10 @@
     sums = lax.all_to_all(sums, "coil", 0, 0, tiled=True)
 
     near, far = ("y", "core"), ("z", "coil")
-    new_x, new_r, norms, old = call(
+    new_x, new_r, kept, norms, old = call(
         step_kernel,
         (sums, x.reshape(flat), r.reshape(flat), d.reshape(flat)),
-        [flat, flat, (lax.axis_size(near), 1, 128), (1, 128)],
+        [flat, flat, flat, (lax.axis_size(near), 1, 128), (1, 128)],
         "step",
     )
     norms = lax.all_to_all(norms, near, 0, 0, tiled=True)
@@ -355,7 +374,7 @@
     )
     norms = lax.all_to_all(norms, far, 0, 0, tiled=True)
     new_d, norm = call(
-        finish_kernel, (norms, old, new_r, d.reshape(flat)), [flat, (1, 128)], "finish"
+        finish_kernel, (norms, old, kept, d.reshape(flat)), [flat, (1, 128)], "finish"
     )
 
     def restore(values):

time: 154 us -> 148 us (0.961)
  blocking collectives: 85.4 us -> 73.7 us
  starting transfers between devices: 20.5 us -> 23.9 us
  local copies, waits for them, and re-layouts: 5.95 us -> 7.86 us
    all_gather x1 -> x0, blocking collectives: 10.6 us -> none  [body(): gathered = lax.all_gather(direction, 'coil', axis=1, tiled=True)]
    all_to_all x0 -> x1, starting transfers between devices: none -> 4.84 us  [body(): gathered = lax.all_to_all(copies, 'coil', 0, 0, tiled=True)]
    unnamed x28 -> x32, local copies, waits for them, and re-layouts: 5.94 us -> 6.4 us
    pallas_call x7 -> x8, Pallas kernels: 10.5 us -> 10.6 us  [call(): pl.pallas_call(kernel, out_shape=[jax.ShapeDtypeStruct(s, f32) if isinsta...]
  transfers between devices with their start and end apart: 1 -> 2, of which waited for: 1 -> 2; matrix products, arithmetic and copies ran while one was open for 0% -> 0% of each run, Pallas kernels for 1% -> 2%
where the time goes in v3:
time: 148 us
  blocking collectives  73.7 us (50%)
  waiting for transfers between devices  30.8 us (21%)
  starting transfers between devices  23.9 us (16%)
  Pallas kernels  10.6 us (7%)
  local copies, waits for them, and re-layouts  7.86 us (5%)
    all_to_all x1, blocking collectives, swap(): return lax.all_to_all(single, axis, 0, 0, tiled=True).reshape(values.shape)  41.7 us
    all_to_all x1, waiting for transfers between devices, swap(): return lax.all_to_all(single, axis, 0, 0, tiled=True).reshape(values.shape)  29.4 us
    all_to_all x1, starting transfers between devices, swap(): return lax.all_to_all(single, axis, 0, 0, tiled=True).reshape(values.shape)  19 us
    all_to_all x1, blocking collectives, body(): norms = lax.all_to_all(norms, near, 0, 0, tiled=True)  12.6 us
    all_to_all x1, blocking collectives, body(): norms = lax.all_to_all(norms, far, 0, 0, tiled=True)  11.9 us
    pallas_call x8, Pallas kernels, call(): pl.pallas_call(kernel, out_shape=[jax.ShapeDtypeStruct(s, f32) if isinsta...  10.6 us
    all_to_all x1, blocking collectives, body(): sums = lax.all_to_all(sums, 'coil', 0, 0, tiled=True)  7.49 us
    unnamed x32, local copies, waits for them, and re-layouts  6.4 us
  transfers between devices with their start and end apart: 2, of which 2 were waited for; matrix products, arithmetic and copies ran while one was open for 0% of the time, Pallas kernels for 2%

profile of v3, /device:TPU:1, one launch (start us, length us, event | category | flops | bytes accessed | tf_op | source)
XLA Modules:
  0.0 147.6 jit_solution(4900962738330781551)
XLA Ops:
  0.6 1.4 broadcast_in_dim.14
  2.1 4.8 %all-to-all-start = ((f32[4,2,3,4,384]{4,3,2,1,0:T(4,128)}), f32[4,2,3,4,384]{4,3,2,1,0:T(4,128)S(1)}, u32[]{:S(2)}, u32[]{:S(2)}) async-start(f32[4,2,3,4,384]{4,3,2,1,0:T(4,128)} %broadcast_in_dim.14), calls=%async_computation | async-start | bytes 294912 | tf_op jit(solution)/shard_map/all_to_all | solution.py:332
  6.9 0.0 copy-start.1
  6.9 0.8 copy-done.1
  7.7 0.0 copy-start.5
  7.7 1.1 copy-done.5
  8.8 0.0 copy-start.8
  8.8 0.9 copy-done.8
  9.7 0.0 copy-start.9
  9.7 0.7 copy-done.9
  10.4 0.1 prepare.1
  10.5 1.3 all-to-all-done.all_ref
  11.8 2.2 %images.1 = f32[2432,128]{1,0:T(8,128)} custom-call(f32[4,2,3,4,384]{4,3,2,1,0:T(4,128)S(1)} %all-to-all-done.all_ref, f32[2,3,32,384]{3,2,1,0:T(8,128)S(1)} %get-tuple-element.17.sens_ref, bf16[768,384]{1,0:T(8,128)(2,1)S(1)} %get-tuple-element.18.table_ref, f32[128,128]{1,0:T(8,128)S(1)} %get-tuple-element.19.extra_ref), custom_call_target="tpu_custom_call" | custom-call | tf_op jit(solution)/shard_map/images/pallas_call | solution.py:293
  14.0 19.0 %all-to-all-start.1 = ((f32[2432,1,128]{2,1,0:T(1,128)}), f32[2432,1,128]{2,1,0:T(1,128)S(1)}, u32[]{:S(2)}, u32[]{:S(2)}) async-start(f32[2432,1,128]{2,1,0:T(1,128)} %bitcast.11), calls=%async_computation.1 | async-start | bytes 2490368 | tf_op jit(solution)/shard_map/all_to_all | solution.py:308
  33.1 0.1 pad_add_fusion.place_ref
  33.1 0.0 copy-start
  33.1 1.7 %copy-done = s32[4,384,384]{2,1,0:T(8,128)S(1)} copy-done((s32[4,384,384]{2,1,0:T(8,128)S(1)}, s32[4,384,384]{2,1,0:T(8,128)}, u32[]{:S(2)}) %copy-start) | copy-done | bytes 2359320
  34.8 0.0 copy-start.2
  34.8 0.0 copy-start.7
  34.8 0.0 copy-start.10
  34.8 0.0 copy-start.3
  34.8 0.0 copy-start.4
  34.8 1.4 mask.1.mask_ref
  36.3 0.0 copy-done.2
  36.3 0.0 copy-done.7
  36.3 0.0 copy-done.10
  36.3 0.8 smooth.1
  37.1 0.0 copy-start.12
  37.1 0.6 copy-done.12
  37.7 0.0 copy-start.14
  37.7 0.6 copy-done.14
  38.4 29.4 %all-to-all-done.1 = f32[2432,1,128]{2,1,0:T(1,128)S(1)} async-done(((f32[2432,1,128]{2,1,0:T(1,128)}), f32[2432,1,128]{2,1,0:T(1,128)S(1)}, u32[]{:S(2)}, u32[]{:S(2)}) %all-to-all-start.1) | async-done | bytes 1245216 | tf_op jit(solution)/shard_map/all_to_all | solution.py:308
  67.8 0.0 copy-done.3
  67.8 0.0 copy-done.4
  67.8 2.8 %middle.1 = f32[2432,128]{1,0:T(8,128)S(1)} custom-call(f32[2432,128]{1,0:T(8,128)S(1)} %bitcast.48, f32[3,384,128]{2,1,0:T(8,128)S(1)} %mask.1.mask_ref, f32[2,128]{1,0:T(2,128)S(1)} %get-tuple-element.20.stats_ref, bf16[768,384]{1,0:T(8,128)(2,1)S(1)} %copy-done.3, bf16[768,384]{1,0:T(8,128)(2,1)S(1)} %copy-done.4), custom_call_target="tpu_custom_call" | custom-call | tf_op jit(solution)/shard_map/middle/pallas_call | solution.py:293
  70.6 0.0 copy-start.6
  70.6 0.0 copy-start.13
  70.6 0.0 copy-start.15
  70.6 41.7 %all_to_all.30 = f32[2432,1,128]{2,1,0:T(1,128)S(1)} all-to-all(f32[2432,1,128]{2,1,0:T(1,128)S(1)} %bitcast.49), channel_id=1, replica_groups=mesh['z'=8,'y'=8,'core'=2,'coil'=4] {'z','y','core'}, dimensions={0} | all-to-all | bytes 2490368 | tf_op jit(solution)/shard_map/all_to_all | solution.py:308
  112.3 0.0 copy-done.6
  112.3 0.0 copy-done.13
  112.3 0.0 copy-done.15
  112.3 0.0 copy-start.11
  112.3 1.8 %combine.1 = f32[4,7,4,384]{3,2,1,0:T(4,128)S(1)} custom-call(s32[3]{0:T(128)S(1)} %pad_add_fusion.place_ref, f32[2432,128]{1,0:T(8,128)S(1)} %bitcast.50, f32[2,3,32,384]{3,2,1,0:T(8,128)S(1)} %get-tuple-element.17.sens_ref, f32[6,4,384]{2,1,0:T(4,128)S(1)} %copy-done.13, f32[6,4,384]{2,1,0:T(4,128)S(1)} %copy-done.15, bf16[384,768]{1,0:T(8,128)(2,1)S(1)} %copy-done.6), custom_call_target="tpu_custom_call" | custom-call | tf_op jit(solution)/shard_map/combine/pallas_call | solution.py:293
  114.1 7.5 %all_to_all.31.sums_ref = f32[4,7,4,384]{3,2,1,0:T(4,128)S(1)} all-to-all(f32[4,7,4,384]{3,2,1,0:T(4,128)S(1)} %combine.1), channel_id=1, replica_groups=mesh['z'=8,'y'=8,'core'=2,'coil'=4] {'coil'}, dimensions={0} | all-to-all | bytes 344064 | tf_op jit(solution)/shard_map/all_to_all | solution.py:362
  121.6 0.0 copy-done.11
  121.6 0.7 step.1
  122.3 12.6 %all_to_all.32 = f32[16,1,128]{2,1,0:T(1,128)S(1)} all-to-all(f32[16,1,128]{2,1,0:T(1,128)S(1)} %get-tuple-element.25), channel_id=1, replica_groups=mesh['z'=8,'y'=8,'core'=2,'coil'=4] {'y','core'}, dimensions={0} | all-to-all | bytes 16384 | tf_op jit(solution)/shard_map/all_to_all | solution.py:371
  135.0 11.9 %all_to_all.33.norms_ref = f32[32,1,128]{2,1,0:T(1,128)S(1)} all-to-all(f32[32,1,128]{2,1,0:T(1,128)S(1)} %broadcast_in_dim.15), channel_id=1, replica_groups=mesh['z'=8,'y'=8,'core'=2,'coil'=4] {'z','coil'}, dimensions={0} | all-to-all | bytes 32768 | tf_op jit(solution)/shard_map/all_to_all | solution.py:375
  146.8 0.8 finish.1
  (2 shorter events, 0.0 us)
Async XLA Ops:
  2.1 9.8 %all-to-all-start = ((f32[4,2,3,4,384]{4,3,2,1,0:T(4,128)}), f32[4,2,3,4,384]{4,3,2,1,0:T(4,128)S(1)}, u32[]{:S(2)}, u32[]{:S(2)}) async-start(f32[4,2,3,4,384]{4,3,2,1,0:T(4,128)} %broadcast_in_dim.14), calls=%async_computation | async-start | bytes 294912 | tf_op jit(solution)/shard_map/all_to_all | solution.py:332
  6.9 0.8 copy-start.1
  7.7 1.1 copy-start.5
  8.8 0.9 copy-start.8
  9.7 0.7 copy-start.9
  14.0 53.8 %all-to-all-start.1 = ((f32[2432,1,128]{2,1,0:T(1,128)}), f32[2432,1,128]{2,1,0:T(1,128)S(1)}, u32[]{:S(2)}, u32[]{:S(2)}) async-start(f32[2432,1,128]{2,1,0:T(1,128)} %bitcast.11), calls=%async_computation.1 | async-start | bytes 2490368 | tf_op jit(solution)/shard_map/all_to_all | solution.py:308
  33.1 1.7 %copy-start = (s32[4,384,384]{2,1,0:T(8,128)S(1)}, s32[4,384,384]{2,1,0:T(8,128)}, u32[]{:S(2)}) copy-start(s32[4,384,384]{2,1,0:T(8,128)} %sampling_ref.1) | copy-start | bytes 7077892
  34.8 1.5 copy-start.2
  34.8 1.5 copy-start.7
  34.8 1.5 %copy-start.10 = (s32[1,4,3,384]{3,1,2,0:T(4,128)S(1)}, s32[1,4,3,384]{3,1,2,0:T(4,128)}, u32[]{:S(2)}) copy-start(s32[1,4,3,384]{3,1,2,0:T(4,128)} %param.15) | copy-start | bytes 55300
  34.8 33.0 %copy-start.3 = (bf16[768,384]{1,0:T(8,128)(2,1)S(1)}, bf16[768,384]{1,0:T(8,128)(2,1)}, u32[]{:S(2)}) copy-start(bf16[768,384]{1,0:T(8,128)(2,1)} %constant.34.clone.forward_ref) | copy-start | bytes 1769476
  34.8 33.0 %copy-start.4 = (bf16[768,384]{1,0:T(8,128)(2,1)S(1)}, bf16[768,384]{1,0:T(8,128)(2,1)}, u32[]{:S(2)}) copy-start(bf16[768,384]{1,0:T(8,128)(2,1)} %constant.35.clone.inverse_ref) | copy-start | bytes 1769476
  37.1 0.6 copy-start.12
  37.7 0.6 copy-start.14
  70.6 41.7 %copy-start.6 = (bf16[384,768]{1,0:T(8,128)(2,1)S(1)}, bf16[384,768]{1,0:T(8,128)(2,1)}, u32[]{:S(2)}) copy-start(bf16[384,768]{1,0:T(8,128)(2,1)} %constant.36.clone.table_ref) | copy-start | bytes 1769476
  70.6 41.7 %copy-start.13 = (f32[6,4,384]{2,1,0:T(4,128)S(1)}, f32[6,4,384]{2,1,0:T(4,128)}, u32[]{:S(2)}) copy-start(f32[6,4,384]{2,1,0:T(4,128)} %copy-done.12) | copy-start | bytes 110596
  70.6 41.7 %copy-start.15 = (f32[6,4,384]{2,1,0:T(4,128)S(1)}, f32[6,4,384]{2,1,0:T(4,128)}, u32[]{:S(2)}) copy-start(f32[6,4,384]{2,1,0:T(4,128)} %copy-done.14) | copy-start | bytes 110596
  112.3 9.3 %copy-start.11 = (f32[2,1,4,3,384]{4,2,3,1,0:T(4,128)S(1)}, f32[2,1,4,3,384]{4,2,3,1,0:T(4,128)}, u32[]{:S(2)}) copy-start(f32[2,1,4,3,384]{4,2,3,1,0:T(4,128)} %param.10) | copy-start | bytes 110596

commit v4 on v3

v4 whole, which is shorter than its diff:
```python
import math

import jax
import jax.numpy as jnp
import ml_dtypes
import numpy as np
from jax import lax
from jax.experimental import pallas as pl
from jax.experimental.pallas import tpu as pltpu
from jax.sharding import Mesh
from jax.sharding import PartitionSpec as P

smooth_scale = 0.05
slab_axes = ("z", "y", "core")
f32 = jnp.float32
bf16 = jnp.bfloat16

message = 18


def dft_tables(length):
    counter = np.arange(length, dtype=np.int64)
    phases = (counter[:, None] * counter[None, :]) % length
    angles = phases.astype(np.float32) * np.float32(2.0 * math.pi / length)
    unit_norm = np.float32(1.0 / math.sqrt(length))
    wide = angles.astype(np.float64)
    cos = np.cos(wide).astype(np.float32) * unit_norm
    sin = np.sin(wide).astype(np.float32) * unit_norm
    return cos.astype(ml_dtypes.bfloat16), sin.astype(ml_dtypes.bfloat16)


def split(values):
    upper = values.astype(bf16)
    return upper, (values - upper.astype(f32)).astype(bf16)


def mm(a, b, contract):
    return lax.dot_general(a, b, (contract, ((), ())), preferred_element_type=f32)


def staggered(count, first, second):
    held, results = first(0), []
    for i in range(count):
        ahead = first(i + 1) if i + 1 < count else None
        results.append(second(i, held))
        held = ahead
    return results


def sens_rows(sens_ref, part, row, coils):
    pieces = [sens_ref[part, c, row].astype(f32) for c in range(coils)]
    return jnp.concatenate(pieces, axis=0)


def relay_kernel(sens_ref, sens_out_ref):
    coils, rows = sens_ref.shape[1:3]
    for p in range(2):
        for r in range(rows):
            sens_out_ref[p, r] = sens_rows(sens_ref, p, r, coils)


def table_kernel(table_ref, out_ref):
    out_ref[...] = table_ref[...]


def images_kernel(all_ref, sens_ref, table_ref, out_ref):
    frames, _, rows, zdim, _ = all_ref.shape
    coils = sens_ref.shape[2] // zdim
    table = table_ref[...]
    table = jnp.concatenate([table, table], axis=1)
    half = table.shape[0] // 2
    groups = half // 128

    def forward(r):
        s_re, s_im = sens_ref[0, r], sens_ref[1, r]
        real, imag = [], []
        for f in range(frames):
            d_re = jnp.concatenate([all_ref[f, 0, r]] * coils, axis=0)
            d_im = jnp.concatenate([all_ref[f, 1, r]] * coils, axis=0)
            real.append(s_re * d_re - s_im * d_im)
            imag.append(s_re * d_im + s_im * d_re)
        upper, lower = split(jnp.concatenate(real + imag, axis=0))
        return mm(table, jnp.concatenate([upper, lower], axis=1), ((1,), (1,)))

    def store(r, got):
        re = got[:half, :128] + got[half:, 128:]
        im = got[:half, 128:] - got[half:, :128]
        for j in range(groups):
            at = (j * rows + r) * 2
            out_ref[pl.ds(at, 128, stride=message), :] = re[j * 128 : (j + 1) * 128]
            out_ref[pl.ds(at + 1, 128, stride=message), :] = im[j * 128 : (j + 1) * 128]

    staggered(rows, forward, store)


def mask_kernel(place_ref, sampling_ref, out_ref):
    frames, full, cols = sampling_ref.shape
    groups = cols // 128
    lane = lax.broadcasted_iota(jnp.int32, (cols, cols), 1)
    freq = lax.broadcasted_iota(jnp.int32, (cols, cols), 0)
    wanted = (lane // 128) * 128 + place_ref[0]
    total = jnp.zeros((full, cols), f32)
    for f in range(frames):
        mine = (freq == wanted) & ((lane % 128) // (128 // frames) == f)
        chosen = jnp.where(mine, 1.0, 0.0).astype(bf16)
        total += mm(sampling_ref[f].astype(f32).astype(bf16), chosen, ((1,), (0,)))
    for j in range(groups):
        out_ref[j] = total[:, j * 128 : (j + 1) * 128]


def edges_kernel(own_ref, weight_ref, last_ref, first_ref):
    rows = weight_ref.shape[0]
    for p in range(2):
        last_ref[p] = own_ref[p, rows - 1]
        first_ref[p] = own_ref[p, 0]
    last_ref[2] = weight_ref[rows - 1].astype(f32)


def smooth_kernel(
    place_ref, all_ref, own_ref, weight_ref, before_ref, after_ref, out_ref, next_ref
):
    slab, frame, slabs, frames = (place_ref[i] for i in range(4))
    rows, zdim, cols = own_ref.shape[1:]
    later = jnp.minimum(frame + 1, frames - 1)
    has_next_row = jnp.where(slab < slabs - 1, 1.0, 0.0)
    has_previous_row = jnp.where(slab > 0, 1.0, 0.0)
    zero_col = jnp.zeros((zdim, 1), f32)
    zero_slice = jnp.zeros((1, cols), f32)
    weights = [weight_ref[r].astype(f32) for r in range(rows)]
    for p in range(2):
        values = [own_ref[p, r] for r in range(rows)]
        flux = (before_ref[2] * has_previous_row) * (values[0] - before_ref[p])
        for r in range(rows):
            v, weight = values[r], weights[r]
            term = flux
            if r < rows - 1:
                flux = weight * (values[r + 1] - v)
            else:
                flux = (weight * has_next_row) * (after_ref[p] - v)
            term -= flux
            onward = smooth_scale * (weight * (all_ref[later, p, r] - v))
            across = weight[:-1] * (v[1:] - v[:-1])
            term += jnp.concatenate([zero_slice, across], axis=0)
            term -= jnp.concatenate([across, zero_slice], axis=0)
            across = weight[:, :-1] * (v[:, 1:] - v[:, :-1])
            term += jnp.concatenate([zero_col, across], axis=1)
            term -= jnp.concatenate([across, zero_col], axis=1)
            out_ref[p * rows + r] = smooth_scale * term - onward
            next_ref[p * rows + r] = onward


def middle_kernel(in_ref, mask_ref, forward_ref, inverse_ref, out_ref):
    groups = mask_ref.shape[0]
    rows = 3
    forward = forward_ref[...]
    forward = jnp.concatenate([forward, forward], axis=1)
    inverse = inverse_ref[...]
    inverse = jnp.concatenate([inverse, inverse], axis=1)
    half = forward.shape[0] // 2

    def gather(j):
        parts = []
        for r in range(rows):
            at = (j * rows + r) * 2
            re = in_ref[pl.ds(at, 128, stride=message), :]
            im = in_ref[pl.ds(at + 1, 128, stride=message), :]
            parts.append(jnp.concatenate([re, im], axis=1))
        upper, lower = split(jnp.concatenate(parts, axis=0))
        return mm(forward, jnp.concatenate([upper, lower], axis=0), ((1,), (0,)))

    def sample(j, got):
        mask = mask_ref[j]
        re = (got[:half, :128] + got[half:, 128:]) * mask
        im = (got[:half, 128:] - got[half:, :128]) * mask
        upper, lower = split(jnp.concatenate([re, im], axis=1))
        back = mm(inverse, jnp.concatenate([upper, lower], axis=0), ((1,), (0,)))
        store(j, back)

    def store(j, got):
        re = got[:half, :128] - got[half:, 128:]
        im = got[:half, 128:] + got[half:, :128]
        for r in range(rows):
            at = (r * groups + j) * 2
            out_ref[pl.ds(at, 128, stride=message), :] = re[r * 128 : (r + 1) * 128]
            out_ref[pl.ds(at + 1, 128, stride=message), :] = im[r * 128 : (r + 1) * 128]

    staggered(groups, gather, sample)


def combine_kernel(place_ref, in_ref, sens_ref, smooth_ref, next_ref, table_ref, out_ref):
    frame, frame_count = place_ref[1], place_ref[3]
    frames, _, zdim, cols = out_ref.shape
    rows, span = sens_ref.shape[1:3]
    table = table_ref[...]
    table = jnp.concatenate([table, table], axis=0)
    groups = cols // 128

    def backward(r):
        real, imag = [], []
        for j in range(groups):
            at = (r * groups + j) * 2
            real.append(in_ref[pl.ds(at, 128, stride=message), :].T)
            imag.append(in_ref[pl.ds(at + 1, 128, stride=message), :].T)
        both = jnp.concatenate(
            [jnp.concatenate(real, axis=1), jnp.concatenate(imag, axis=1)], axis=0
        )
        upper, lower = split(both)
        return mm(jnp.concatenate([upper, lower], axis=1), table, ((1,), (0,)))

    def add_coils(r, got):
        re = got[:128, :cols] - got[128:, cols:]
        im = got[128:, :cols] + got[:128, cols:]
        s_re, s_im = sens_ref[0, r], sens_ref[1, r]
        for f in range(frames):
            b_re = re[f * span : (f + 1) * span]
            b_im = im[f * span : (f + 1) * span]
            for p, t in enumerate((s_re * b_re + s_im * b_im, s_re * b_im - s_im * b_re)):
                eight = t[0:8]
                for g in range(1, span // 8):
                    eight = eight + t[g * 8 : (g + 1) * 8]
                out_ref[f, p * rows + r] = eight[0:zdim] + eight[zdim : 2 * zdim]

    staggered(rows, backward, add_coils)
    for i in range(2 * rows):
        out_ref[frame, i] += smooth_ref[i]

    @pl.when(frame < frame_count - 1)
    def _():
        for i in range(2 * rows):
            out_ref[frame + 1, i] += next_ref[i]


def whole(values):
    return jnp.sum(jnp.sum(values, axis=0, keepdims=True), axis=1, keepdims=True)


def in_lanes(values):
    lane = lax.broadcasted_iota(jnp.int32, (1, 128), 1)
    row = jnp.zeros((1, 128), f32)
    for i, value in enumerate(values):
        row = jnp.where(lane == i, value, row)
    return row


def share(value, weight):
    return jnp.where(weight > 0, value / jnp.where(weight > 0, weight, 1.0), 0.0)


def sums_kernel(sums_ref, residual_ref, direction_ref, applied_ref, out_ref):
    planes = residual_ref.shape[0]
    sources = sums_ref.shape[0]
    zero = jnp.zeros(residual_ref.shape[1:], f32)
    norm, curvature, size, cross, rest = zero, zero, zero, zero, zero
    for i in range(planes):
        value = sums_ref[0, i]
        for k in range(1, sources):
            value = value + sums_ref[k, i]
        applied_ref[i] = value
        r = residual_ref[i]
        norm += r * r
        curvature += direction_ref[i] * value
        size += value * value
        cross += r * value
    size = whole(size)
    ratio = share(whole(cross), size)
    for i in range(planes):
        left = residual_ref[i] - ratio * applied_ref[i]
        rest += left * left
    row = in_lanes([whole(norm), whole(curvature), size, ratio, whole(rest)])
    out_ref[...] = jnp.broadcast_to(row[None], out_ref.shape)


def joined(parts):
    size, ratio = parts[:, 2:3], parts[:, 3:4]
    norm, curvature = whole(parts[:, 0:1]), whole(parts[:, 1:2])
    all_size = whole(size)
    all_ratio = share(whole(size * ratio), all_size)
    away = ratio - all_ratio
    rest = whole(parts[:, 4:5] + (size * away) * away)
    return norm, curvature, all_size, all_ratio, rest


def join_kernel(parts_ref, out_ref):
    row = in_lanes(joined(parts_ref[:, 0, :]))
    out_ref[...] = jnp.broadcast_to(row[None], out_ref.shape)


def finish_kernel(
    parts_ref, applied_ref, iterate_ref, residual_ref, direction_ref, new_iterate_ref, new_residual_ref, new_direction_ref, norm_ref
):
    old_norm, curvature, size, ratio, rest = joined(parts_ref[:, 0, :])
    step = old_norm / curvature
    away = ratio - step
    new_norm = rest + (size * away) * away
    turn = new_norm / old_norm
    for i in range(direction_ref.shape[0]):
        d = direction_ref[i]
        fresh = residual_ref[i] - step * applied_ref[i]
        new_iterate_ref[i] = iterate_ref[i] + step * d
        new_residual_ref[i] = fresh
        new_direction_ref[i] = fresh + turn * d
    norm_ref[...] = jnp.broadcast_to(new_norm, norm_ref.shape)


vmem = pl.BlockSpec(memory_space=pltpu.VMEM)
smem = pl.BlockSpec(memory_space=pltpu.SMEM)


params = pltpu.CompilerParams(vmem_limit_bytes=40 * 1024 * 1024)


def call(kernel, ins, outs, name, scalars=0):
    return pl.pallas_call(
        kernel,
        out_shape=[
            jax.ShapeDtypeStruct(s, f32) if isinstance(s, tuple) else jax.ShapeDtypeStruct(s.shape, s.dtype)
            for s in outs
        ],
        in_specs=[smem] * scalars + [vmem] * (len(ins) - scalars),
        out_specs=[vmem] * len(outs),
        compiler_params=params,
        name=name,
    )(*ins)


def swap(values, axis):
    pairs = values.reshape(values.shape[0] // 2, 2, 128)
    return lax.all_to_all(pairs, axis, 0, 0, tiled=True).reshape(values.shape)


def body(iterate, residual, direction, sensitivity, sampling, edge_weight):
    slabs = lax.axis_size(slab_axes)
    frames = lax.axis_size("coil")
    rows, zdim, cols = direction.shape[3], direction.shape[2], direction.shape[4]

    sens = jnp.swapaxes(sensitivity, 2, 3)
    d = jnp.swapaxes(direction, 2, 3)[:, 0]
    r = jnp.swapaxes(residual, 2, 3)[:, 0]
    x = jnp.swapaxes(iterate, 2, 3)[:, 0]
    w = jnp.swapaxes(edge_weight, 1, 2)[0]

    cos, sin = dft_tables(cols)
    by_slab = np.arange(cols).reshape(cols // rows, rows).T.reshape(-1)
    natural = jnp.asarray(np.concatenate([cos, sin], axis=0))
    forward = jnp.asarray(np.concatenate([cos[:, by_slab], sin[:, by_slab]], axis=0))
    inverse = jnp.asarray(np.concatenate([cos[by_slab], sin[by_slab]], axis=0))
    wide = jnp.asarray(np.concatenate([cos, sin], axis=1))

    place = jnp.stack(
        [lax.axis_index(slab_axes), lax.axis_index("coil"), jnp.int32(slabs), jnp.int32(frames)]
    ).astype(jnp.int32)
    copies = jnp.broadcast_to(d[None], (frames,) + d.shape)
    gathered = lax.all_to_all(copies, "coil", 0, 0, tiled=True)
    sens_shape = (2, rows, sens.shape[1] * zdim, cols)
    (sens,) = call(relay_kernel, (sens,), [sens_shape], "relay")
    (natural,) = call(table_kernel, (natural,), [natural], "table")

    lines = slabs * message
    (spectrum,) = call(images_kernel, (gathered, sens, natural), [(lines, 128)], "images")
    spectrum = swap(spectrum, slab_axes)
    last, first = call(edges_kernel, (d, w), [(3, zdim, cols), (2, zdim, cols)], "edges")
    up = [(i, i + 1) for i in range(slabs - 1)]
    before = lax.ppermute(last, slab_axes, up)
    after = lax.ppermute(first, slab_axes, [(j, i) for i, j in up])
    (mask,) = call(mask_kernel, (place, sampling), [(cols // 128, cols, 128)], "mask", 1)
    flat = (2 * rows, zdim, cols)
    smooth, onward = call(
        smooth_kernel, (place, gathered, d, w, before, after), [flat, flat], "smooth", 1
    )
    spectrum, smooth, onward = lax.optimization_barrier((spectrum, smooth, onward))
    (back,) = call(
        middle_kernel, (spectrum, mask, forward, inverse), [(lines, 128)], "middle"
    )
    back = swap(back, slab_axes)
    (sums,) = call(
        combine_kernel,
        (place, back, sens, smooth, onward, wide),
        [(frames,) + flat],
        "combine",
        1,
    )
    sums = lax.all_to_all(sums, "coil", 0, 0, tiled=True)

    near, far = ("y", "core"), ("z", "coil")
    x, r, d = (v.reshape(flat) for v in (x, r, d))
    applied, parts = call(
        sums_kernel, (sums, r, d), [flat, (lax.axis_size(near), 1, 128)], "sums"
    )
    parts = lax.all_to_all(parts, near, 0, 0, tiled=True)
    (parts,) = call(join_kernel, (parts,), [(lax.axis_size(far), 1, 128)], "join")
    parts = lax.all_to_all(parts, far, 0, 0, tiled=True)
    new_x, new_r, new_d, norm = call(
        finish_kernel, (parts, applied, x, r, d), [flat, flat, flat, (1, 128)], "finish"
    )

    def restore(values):
        return jnp.swapaxes(values.reshape(2, 1, rows, zdim, cols), 2, 3)

    return restore(new_x), restore(new_r), restore(new_d), norm[0, 0]


def solution(mesh):
    fine = Mesh(mesh.devices.reshape(8, 8, 2, 4), ("z", "y", "core", "coil"))
    image = P(None, "coil", None, slab_axes, None)
    return jax.shard_map(
        body,
        mesh=fine,
        in_specs=(image, image, image, image, P(), P("coil", None, slab_axes, None)),
        out_specs=(image, image, image, P()),
        check_vma=False,
    )
```

time: 148 us -> 145 us (0.980)
  starting transfers between devices: 23.9 us -> 29.6 us
  local copies, waits for them, and re-layouts: 7.86 us -> 4.13 us
  waiting for transfers between devices: 30.8 us -> 28 us
  blocking collectives: 73.7 us -> 72.1 us
    all_to_all x1, waiting for transfers between devices: 29.4 us -> 5.54 us  [swap(): return lax.all_to_all(pairs, axis, 0, 0, tiled=True).reshape(values.shape)]
    ppermute x0 -> x2, waiting for transfers between devices: none -> 18.6 us  [the longest x1 18.6 us: body(): after = lax.ppermute(first, slab_axes, [(j, i) for i, j in up])]
    ppermute x0 -> x2, starting transfers between devices: none -> 5.56 us  [the longest x1 2.8 us: body(): after = lax.ppermute(first, slab_axes, [(j, i) for i, j in up])]
    unnamed x32 -> x24, local copies, waits for them, and re-layouts: 6.4 us -> 2.62 us
    all_to_all x1, waiting for transfers between devices: 1.32 us -> 3.9 us  [body(): gathered = lax.all_to_all(copies, 'coil', 0, 0, tiled=True)]
    pallas_call x8 -> x11, Pallas kernels: 10.6 us -> 9.65 us  [call(): pl.pallas_call(kernel, out_shape=[jax.ShapeDtypeStruct(s, f32) if isinsta...]
  transfers between devices with their start and end apart: 2 -> 4, of which waited for: 2 -> 3; matrix products, arithmetic and copies ran while one was open for 0% -> 0% of each run, Pallas kernels for 2% -> 2%
where the time goes in v4:
time: 145 us; the launch traced here: 144 us
  blocking collectives  72.1 us (50%)
  starting transfers between devices  29.6 us (20%)
  waiting for transfers between devices  28 us (19%)
  Pallas kernels  9.65 us (7%)
  local copies, waits for them, and re-layouts  4.13 us (3%)
    all_to_all x1, blocking collectives, swap(): return lax.all_to_all(pairs, axis, 0, 0, tiled=True).reshape(values.shape)  40.4 us
    all_to_all x1, starting transfers between devices, swap(): return lax.all_to_all(pairs, axis, 0, 0, tiled=True).reshape(values.shape)  19.2 us
    ppermute x1, waiting for transfers between devices, body(): after = lax.ppermute(first, slab_axes, [(j, i) for i, j in up])  18.6 us
    all_to_all x1, blocking collectives, body(): parts = lax.all_to_all(parts, near, 0, 0, tiled=True)  12.5 us
    all_to_all x1, blocking collectives, body(): parts = lax.all_to_all(parts, far, 0, 0, tiled=True)  11.9 us
    pallas_call x11, Pallas kernels, call(): pl.pallas_call(kernel, out_shape=[jax.ShapeDtypeStruct(s, f32) if isinsta...  9.65 us
    all_to_all x1, blocking collectives, body(): sums = lax.all_to_all(sums, 'coil', 0, 0, tiled=True)  7.26 us
    all_to_all x1, waiting for transfers between devices, swap(): return lax.all_to_all(pairs, axis, 0, 0, tiled=True).reshape(values.shape)  5.54 us
  transfers between devices with their start and end apart: 4, of which 3 were waited for; matrix products, arithmetic and copies ran while one was open for 0% of the time, Pallas kernels for 2%

profile of v4, /device:TPU:1, one launch (start us, length us, event | category | flops | bytes accessed | tf_op | source)
XLA Modules:
  0.0 144.3 jit_solution(14214803308624823937)
XLA Ops:
  0.6 0.0 copy-start.3
  0.6 1.5 %broadcast_in_dim.8 = f32[4,2,3,4,384]{4,3,2,1,0:T(4,128)} broadcast(f32[2,3,4,384]{3,2,1,0:T(4,128)} %bitcast.43), dimensions={1,2,3,4} | broadcast | bytes 184320 | tf_op jit(solution)/shard_map/broadcast_in_dim | solution.py:352
  2.2 4.8 %all-to-all-start = ((f32[4,2,3,4,384]{4,3,2,1,0:T(4,128)}), f32[4,2,3,4,384]{4,3,2,1,0:T(4,128)S(1)}, u32[]{:S(2)}, u32[]{:S(2)}) async-start(f32[4,2,3,4,384]{4,3,2,1,0:T(4,128)} %broadcast_in_dim.8), calls=%async_computation | async-start | bytes 294912 | tf_op jit(solution)/shard_map/all_to_all | solution.py:353
  7.0 0.0 copy-start.6
  7.0 0.9 copy-done.6
  7.9 0.0 copy-done.3
  8.0 0.1 table.1.table_ref
  8.0 3.9 %all-to-all-done.all_ref = f32[4,2,3,4,384]{4,3,2,1,0:T(4,128)S(1)} async-done(((f32[4,2,3,4,384]{4,3,2,1,0:T(4,128)}), f32[4,2,3,4,384]{4,3,2,1,0:T(4,128)S(1)}, u32[]{:S(2)}, u32[]{:S(2)}) %all-to-all-start) | async-done | bytes 147488 | tf_op jit(solution)/shard_map/all_to_all | solution.py:353
  11.9 2.2 %images.1 = f32[2304,128]{1,0:T(8,128)} custom-call(f32[4,2,3,4,384]{4,3,2,1,0:T(4,128)S(1)} %all-to-all-done.all_ref, f32[2,3,32,384]{3,2,1,0:T(8,128)S(1)} %relay.1.sens_ref, bf16[768,384]{1,0:T(8,128)(2,1)S(1)} %table.1.table_ref), custom_call_target="tpu_custom_call" | custom-call | tf_op jit(solution)/shard_map/images/pallas_call | solution.py:313
  14.1 0.0 copy-start.1
  14.1 0.0 copy-start.8
  14.1 19.2 %all-to-all-start.1 = ((f32[1152,2,128]{2,1,0:T(2,128)}), f32[1152,2,128]{2,1,0:T(2,128)S(1)}, u32[]{:S(2)}, u32[]{:S(2)}) async-start(f32[1152,2,128]{2,1,0:T(2,128)} %bitcast.6), calls=%async_computation.1 | async-start | bytes 2359296 | tf_op jit(solution)/shard_map/all_to_all | solution.py:328
  33.3 0.0 copy-done.1
  33.3 0.0 copy-done.8
  33.3 2.8 %collective-permute-start.1 = (f32[2,4,384]{2,1,0:T(4,128)S(1)}, f32[2,4,384]{2,1,0:T(4,128)S(1)}, u32[]{:S(2)}, u32[]{:S(2)}) collective-permute-start(f32[2,4,384]{2,1,0:T(4,128)S(1)} %get-tuple-element.18), channel_id=1, source_target_pairs={{4,0},{8,4},{12,8},{16,12},{20,16},{24,20},{28,24},{32,28},{36,32}... | collective-permute-start | bytes 36872 | tf_op jit(solution)/shard_map/ppermute | solution.py:364
  36.1 2.8 %collective-permute-start = (f32[3,4,384]{2,1,0:T(4,128)S(1)}, f32[3,4,384]{2,1,0:T(4,128)S(1)}, u32[]{:S(2)}, u32[]{:S(2)}) collective-permute-start(f32[3,4,384]{2,1,0:T(4,128)S(1)} %get-tuple-element.17), channel_id=1, source_target_pairs={{0,4},{4,8},{8,12},{12,16},{16,20},{20,24},{24,28},{28,32},{32,36}... | collective-permute-start | bytes 55304 | tf_op jit(solution)/shard_map/ppermute | solution.py:363
  38.9 0.1 pad_add_fusion.place_ref
  39.0 0.0 copy-start
  39.0 1.7 %copy-done = s32[4,384,384]{2,1,0:T(8,128)S(1)} copy-done((s32[4,384,384]{2,1,0:T(8,128)S(1)}, s32[4,384,384]{2,1,0:T(8,128)}, u32[]{:S(2)}) %copy-start) | copy-done | bytes 2359320
  40.6 0.0 copy-start.10
  40.6 0.0 copy-start.4
  40.6 0.0 copy-start.5
  40.6 1.4 mask.1.mask_ref
  42.1 18.6 %collective-permute-done.1.after_ref = f32[2,4,384]{2,1,0:T(4,128)S(1)} collective-permute-done((f32[2,4,384]{2,1,0:T(4,128)S(1)}, f32[2,4,384]{2,1,0:T(4,128)S(1)}, u32[]{:S(2)}, u32[]{:S(2)}) %collective-permute-start.1) | collective-permute-done | bytes 12320 | tf_op jit(solution)/shard_map/ppermute | solution.py:364
  60.6 0.0 collective-permute-done.before_ref
  60.6 0.0 copy-done.10
  60.6 0.8 smooth.1
  61.4 5.5 %all-to-all-done.1 = f32[1152,2,128]{2,1,0:T(2,128)S(1)} async-done(((f32[1152,2,128]{2,1,0:T(2,128)}), f32[1152,2,128]{2,1,0:T(2,128)S(1)}, u32[]{:S(2)}, u32[]{:S(2)}) %all-to-all-start.1) | async-done | bytes 1179680 | tf_op jit(solution)/shard_map/all_to_all | solution.py:328
  67.0 0.0 copy-done.4
  67.0 0.0 copy-done.5
  67.0 2.1 %middle.1 = f32[2304,128]{1,0:T(8,128)S(1)} custom-call(f32[2304,128]{1,0:T(8,128)S(1)} %bitcast.41, f32[3,384,128]{2,1,0:T(8,128)S(1)} %mask.1.mask_ref, bf16[768,384]{1,0:T(8,128)(2,1)S(1)} %copy-done.5, bf16[768,384]{1,0:T(8,128)(2,1)S(1)} %copy-done.4), custom_call_target="tpu_custom_call" | custom-call | tf_op jit(solution)/shard_map/middle/pallas_call | solution.py:313
  69.1 0.0 copy-start.2
  69.1 0.0 copy-start.11
  69.1 40.4 %all_to_all.30 = f32[1152,2,128]{2,1,0:T(2,128)S(1)} all-to-all(f32[1152,2,128]{2,1,0:T(2,128)S(1)} %bitcast.42), channel_id=1, replica_groups=mesh['z'=8,'y'=8,'core'=2,'coil'=4] {'z','y','core'}, dimensions={0} | all-to-all | bytes 2359296 | tf_op jit(solution)/shard_map/all_to_all | solution.py:328
  109.5 0.0 copy-done.2
  109.5 0.0 copy-done.11
  109.5 0.0 copy-start.7
  109.5 0.0 copy-start.9
  109.5 1.7 %combine.1 = f32[4,6,4,384]{3,2,1,0:T(4,128)S(1)} custom-call(s32[4]{0:T(128)S(1)} %copy-done.11, f32[2304,128]{1,0:T(8,128)S(1)} %bitcast.40, f32[2,3,32,384]{3,2,1,0:T(8,128)S(1)} %relay.1.sens_ref, f32[6,4,384]{2,1,0:T(4,128)S(1)} %get-tuple-element.22.smooth_ref, f32[6,4,384]{2,1,0:T(4,128)S(1)} %get-tuple-element.23.next_ref, bf16[384,768]{1,0:T(8,128)(2,1)S(1)} %copy-done.2), custom_call_target="tpu_custom_call" | custom-call | tf_op jit(solution)/shard_map/combine/pallas_call | solution.py:313
  111.3 7.3 %all_to_all.31.sums_ref = f32[4,6,4,384]{3,2,1,0:T(4,128)S(1)} all-to-all(f32[4,6,4,384]{3,2,1,0:T(4,128)S(1)} %combine.1), channel_id=1, replica_groups=mesh['z'=8,'y'=8,'core'=2,'coil'=4] {'coil'}, dimensions={0} | all-to-all | bytes 294912 | tf_op jit(solution)/shard_map/all_to_all | solution.py:382
  118.5 0.0 copy-done.7
  118.5 0.2 sums.1
  118.7 12.5 %all_to_all.32.parts_ref = f32[16,1,128]{2,1,0:T(1,128)S(1)} all-to-all(f32[16,1,128]{2,1,0:T(1,128)S(1)} %get-tuple-element.24), channel_id=1, replica_groups=mesh['z'=8,'y'=8,'core'=2,'coil'=4] {'y','core'}, dimensions={0} | all-to-all | bytes 16384 | tf_op jit(solution)/shard_map/all_to_all | solution.py:389
  131.3 0.2 join.1
  131.5 11.9 %all_to_all.33.parts_ref = f32[32,1,128]{2,1,0:T(1,128)S(1)} all-to-all(f32[32,1,128]{2,1,0:T(1,128)S(1)} %join.1), channel_id=1, replica_groups=mesh['z'=8,'y'=8,'core'=2,'coil'=4] {'z','coil'}, dimensions={0} | all-to-all | bytes 32768 | tf_op jit(solution)/shard_map/all_to_all | solution.py:391
  143.4 0.0 copy-done.9
  143.4 0.9 finish.1
  (2 shorter events, 0.0 us)
Async XLA Ops:
  0.6 7.3 %copy-start.3 = (bf16[768,384]{1,0:T(8,128)(2,1)S(1)}, bf16[768,384]{1,0:T(8,128)(2,1)}, u32[]{:S(2)}) copy-start(bf16[768,384]{1,0:T(8,128)(2,1)} %constant.33.clone.table_ref) | copy-start | bytes 1769476
  2.2 9.8 %all-to-all-start = ((f32[4,2,3,4,384]{4,3,2,1,0:T(4,128)}), f32[4,2,3,4,384]{4,3,2,1,0:T(4,128)S(1)}, u32[]{:S(2)}, u32[]{:S(2)}) async-start(f32[4,2,3,4,384]{4,3,2,1,0:T(4,128)} %broadcast_in_dim.8), calls=%async_computation | async-start | bytes 294912 | tf_op jit(solution)/shard_map/all_to_all | solution.py:353
  7.0 0.9 copy-start.6
  14.1 19.2 %copy-start.1 = (f32[2,1,4,3,384]{4,2,3,1,0:T(4,128)S(1)}, f32[2,1,4,3,384]{4,2,3,1,0:T(4,128)}, u32[]{:S(2)}) copy-start(f32[2,1,4,3,384]{4,2,3,1,0:T(4,128)} %param.12) | copy-start | bytes 110596
  14.1 19.2 %copy-start.8 = (s32[1,4,3,384]{3,1,2,0:T(4,128)S(1)}, s32[1,4,3,384]{3,1,2,0:T(4,128)}, u32[]{:S(2)}) copy-start(s32[1,4,3,384]{3,1,2,0:T(4,128)} %param.15) | copy-start | bytes 55300
  14.1 52.9 %all-to-all-start.1 = ((f32[1152,2,128]{2,1,0:T(2,128)}), f32[1152,2,128]{2,1,0:T(2,128)S(1)}, u32[]{:S(2)}, u32[]{:S(2)}) async-start(f32[1152,2,128]{2,1,0:T(2,128)} %bitcast.6), calls=%async_computation.1 | async-start | bytes 2359296 | tf_op jit(solution)/shard_map/all_to_all | solution.py:328
  33.3 27.3 %collective-permute-start.1 = (f32[2,4,384]{2,1,0:T(4,128)S(1)}, f32[2,4,384]{2,1,0:T(4,128)S(1)}, u32[]{:S(2)}, u32[]{:S(2)}) collective-permute-start(f32[2,4,384]{2,1,0:T(4,128)S(1)} %get-tuple-element.18), channel_id=1, source_target_pairs={{4,0},{8,4},{12,8},{16,12},{20,16},{24,20},{28,24},{32,28},{36,32}... | collective-permute-start | bytes 36872 | tf_op jit(solution)/shard_map/ppermute | solution.py:364
  36.1 24.5 %collective-permute-start = (f32[3,4,384]{2,1,0:T(4,128)S(1)}, f32[3,4,384]{2,1,0:T(4,128)S(1)}, u32[]{:S(2)}, u32[]{:S(2)}) collective-permute-start(f32[3,4,384]{2,1,0:T(4,128)S(1)} %get-tuple-element.17), channel_id=1, source_target_pairs={{0,4},{4,8},{8,12},{12,16},{16,20},{20,24},{24,28},{28,32},{32,36}... | collective-permute-start | bytes 55304 | tf_op jit(solution)/shard_map/ppermute | solution.py:363
  39.0 1.7 %copy-start = (s32[4,384,384]{2,1,0:T(8,128)S(1)}, s32[4,384,384]{2,1,0:T(8,128)}, u32[]{:S(2)}) copy-start(s32[4,384,384]{2,1,0:T(8,128)} %sampling_ref.1) | copy-start | bytes 7077892
  40.6 20.0 %copy-start.10 = (s32[4]{0:T(128)}, s32[4]{0:T(128)S(1)}, u32[]{:S(2)}) copy-start(s32[4]{0:T(128)S(1)} %pad_add_fusion.place_ref) | copy-start | bytes 52
  40.6 26.3 %copy-start.4 = (bf16[768,384]{1,0:T(8,128)(2,1)S(1)}, bf16[768,384]{1,0:T(8,128)(2,1)}, u32[]{:S(2)}) copy-start(bf16[768,384]{1,0:T(8,128)(2,1)} %constant.35.clone.inverse_ref) | copy-start | bytes 1769476
  40.6 26.3 %copy-start.5 = (bf16[768,384]{1,0:T(8,128)(2,1)S(1)}, bf16[768,384]{1,0:T(8,128)(2,1)}, u32[]{:S(2)}) copy-start(bf16[768,384]{1,0:T(8,128)(2,1)} %constant.34.clone.forward_ref) | copy-start | bytes 1769476
  69.1 40.4 %copy-start.2 = (bf16[384,768]{1,0:T(8,128)(2,1)S(1)}, bf16[384,768]{1,0:T(8,128)(2,1)}, u32[]{:S(2)}) copy-start(bf16[384,768]{1,0:T(8,128)(2,1)} %constant.36.clone.table_ref) | copy-start | bytes 1769476
  69.1 40.4 %copy-start.11 = (s32[4]{0:T(128)S(1)}, s32[4]{0:T(128)}, u32[]{:S(2)}) copy-start(s32[4]{0:T(128)} %copy-done.10) | copy-start | bytes 52
  109.5 9.0 %copy-start.7 = (f32[2,1,4,3,384]{4,2,3,1,0:T(4,128)S(1)}, f32[2,1,4,3,384]{4,2,3,1,0:T(4,128)}, u32[]{:S(2)}) copy-start(f32[2,1,4,3,384]{4,2,3,1,0:T(4,128)} %param.11) | copy-start | bytes 110596
  109.5 33.9 %copy-start.9 = (f32[2,1,4,3,384]{4,2,3,1,0:T(4,128)S(1)}, f32[2,1,4,3,384]{4,2,3,1,0:T(4,128)}, u32[]{:S(2)}) copy-start(f32[2,1,4,3,384]{4,2,3,1,0:T(4,128)} %param.10) | copy-start | bytes 110596

commit v5 on v4

v5 whole, which is shorter than its diff:
```python
import math

import jax
import jax.numpy as jnp
import ml_dtypes
import numpy as np
from jax import lax
from jax.experimental import pallas as pl
from jax.experimental.pallas import tpu as pltpu
from jax.sharding import Mesh
from jax.sharding import PartitionSpec as P

smooth_scale = 0.05
slab_axes = ("z", "y", "core")
f32 = jnp.float32
bf16 = jnp.bfloat16

message = 18

rows, coils = 3, 8
at_direction = 2 * rows * coils
at_residual = at_direction + 2 * rows
at_smooth = at_residual + 2 * rows
at_weight = at_smooth + 2 * rows
told = 72


def dft_tables(length):
    counter = np.arange(length, dtype=np.int64)
    phases = (counter[:, None] * counter[None, :]) % length
    angles = phases.astype(np.float32) * np.float32(2.0 * math.pi / length)
    unit_norm = np.float32(1.0 / math.sqrt(length))
    wide = angles.astype(np.float64)
    cos = np.cos(wide).astype(np.float32) * unit_norm
    sin = np.sin(wide).astype(np.float32) * unit_norm
    return cos.astype(ml_dtypes.bfloat16), sin.astype(ml_dtypes.bfloat16)


def split(values):
    upper = values.astype(bf16)
    return upper, (values - upper.astype(f32)).astype(bf16)


def mm(a, b, contract):
    return lax.dot_general(a, b, (contract, ((), ())), preferred_element_type=f32)


def staggered(count, first, second):
    held, results = first(0), []
    for i in range(count):
        ahead = first(i + 1) if i + 1 < count else None
        results.append(second(i, held))
        held = ahead
    return results


def sens_rows(all_ref, part, row):
    at = (part * rows + row) * coils
    return jnp.concatenate([all_ref[k, at : at + coils] for k in range(all_ref.shape[0])], axis=0)


def tell_kernel(*refs):
    sources, out_ref, held, done = refs[:4], refs[4], refs[5:9], refs[9]
    copies = [pltpu.make_async_copy(sources[i], held[i], done.at[i]) for i in range(4)]
    for copy in copies:
        copy.start()
    for copy in copies:
        copy.wait()
    sens_ref, direction_ref, residual_ref, weight_ref = held
    slices, _, cols = out_ref.shape
    zero_slice = jnp.zeros((1, cols), f32)

    def put(row, values):
        for z in range(slices):
            out_ref[z, row : row + 1] = values[z : z + 1]

    for r in range(rows):
        weight = weight_ref[r].astype(f32)
        put(at_weight + r, weight)
        for p in range(2):
            i = p * rows + r
            tiles = [sens_ref[p, c, r].astype(f32) for c in range(coils)]
            for z in range(slices):
                out_ref[z, i * coils : (i + 1) * coils] = jnp.concatenate(
                    [t[z : z + 1] for t in tiles], axis=0
                )
            v = direction_ref[p, r]
            put(at_direction + i, v)
            put(at_residual + i, residual_ref[p, r])
            flux = weight[:-1] * (v[1:] - v[:-1])
            put(
                at_smooth + i,
                jnp.concatenate([zero_slice, flux], axis=0)
                - jnp.concatenate([flux, zero_slice], axis=0),
            )
    for z in range(slices):
        out_ref[z, at_weight + rows :] = jnp.zeros((told - at_weight - rows, cols), f32)


def table_kernel(table_ref, out_ref):
    out_ref[...] = table_ref[...]


def images_kernel(all_ref, table_ref, out_ref):
    frames, _, cols = all_ref.shape
    table = table_ref[...]
    table = jnp.concatenate([table, table], axis=1)
    half = table.shape[0] // 2
    groups = half // 128

    def forward(r):
        s_re, s_im = sens_rows(all_ref, 0, r), sens_rows(all_ref, 1, r)
        real, imag = [], []
        for f in range(frames):
            at = at_direction + r
            d_re = jnp.broadcast_to(all_ref[f, at : at + 1], s_re.shape)
            d_im = jnp.broadcast_to(all_ref[f, at + rows : at + rows + 1], s_re.shape)
            real.append(s_re * d_re - s_im * d_im)
            imag.append(s_re * d_im + s_im * d_re)
        upper, lower = split(jnp.concatenate(real + imag, axis=0))
        return mm(table, jnp.concatenate([upper, lower], axis=1), ((1,), (1,)))

    def store(r, got):
        re = got[:half, :128] + got[half:, 128:]
        im = got[:half, 128:] - got[half:, :128]
        for j in range(groups):
            at = (j * rows + r) * 2
            out_ref[pl.ds(at, 128, stride=message), :] = re[j * 128 : (j + 1) * 128]
            out_ref[pl.ds(at + 1, 128, stride=message), :] = im[j * 128 : (j + 1) * 128]

    staggered(rows, forward, store)


def mask_kernel(place_ref, sampling_ref, out_ref):
    frames, full, cols = sampling_ref.shape
    groups = cols // 128
    lane = lax.broadcasted_iota(jnp.int32, (cols, cols), 1)
    freq = lax.broadcasted_iota(jnp.int32, (cols, cols), 0)
    wanted = (lane // 128) * 128 + place_ref[0]
    total = jnp.zeros((full, cols), f32)
    for f in range(frames):
        mine = (freq == wanted) & ((lane % 128) // (128 // frames) == f)
        chosen = jnp.where(mine, 1.0, 0.0).astype(bf16)
        total += mm(sampling_ref[f].astype(f32).astype(bf16), chosen, ((1,), (0,)))
    for j in range(groups):
        out_ref[j] = total[:, j * 128 : (j + 1) * 128]


def edges_kernel(all_ref, last_ref, first_ref):
    for f in range(all_ref.shape[0]):
        for p in range(2):
            at = at_direction + p * rows
            last_ref[f, p : p + 1] = all_ref[f, at + rows - 1 : at + rows]
            first_ref[f, p : p + 1] = all_ref[f, at : at + 1]
        last_ref[f, 2:3] = all_ref[f, at_weight + rows - 1 : at_weight + rows]


def smooth_kernel(place_ref, all_ref, before_ref, after_ref, out_ref):
    slab, slabs = place_ref[0], place_ref[1]
    frames, _, cols = all_ref.shape
    has_next_row = jnp.where(slab < slabs - 1, 1.0, 0.0)
    has_previous_row = jnp.where(slab > 0, 1.0, 0.0)
    zero_col = jnp.zeros((rows, 1), f32)
    for p in range(2):
        at = at_direction + p * rows
        from_frame = None
        for f in range(frames):
            v = all_ref[f, at : at + rows]
            weight = all_ref[f, at_weight : at_weight + rows]
            term = all_ref[f, at_smooth + p * rows : at_smooth + (p + 1) * rows]
            if from_frame is not None:
                term = term + from_frame
            if f < frames - 1:
                from_frame = weight * (all_ref[f + 1, at : at + rows] - v)
                term = term - from_frame
            flux = weight[:, :-1] * (v[:, 1:] - v[:, :-1])
            term += jnp.concatenate([zero_col, flux], axis=1)
            term -= jnp.concatenate([flux, zero_col], axis=1)
            previous = before_ref[f, p : p + 1]
            following = after_ref[f, p : p + 1]
            first = (before_ref[f, 2:3] * has_previous_row) * (v[0:1] - previous)
            inner = weight[:-1] * (v[1:] - v[:-1])
            final = (weight[-1:] * has_next_row) * (following - v[-1:])
            term += jnp.concatenate([first, inner], axis=0)
            term -= jnp.concatenate([inner, final], axis=0)
            out_ref[f, p * rows : (p + 1) * rows] = smooth_scale * term


def middle_kernel(in_ref, mask_ref, forward_ref, inverse_ref, out_ref):
    groups = mask_ref.shape[0]
    forward = forward_ref[...]
    forward = jnp.concatenate([forward, forward], axis=1)
    inverse = inverse_ref[...]
    inverse = jnp.concatenate([inverse, inverse], axis=1)
    half = forward.shape[0] // 2

    def gather(j):
        parts = []
        for r in range(rows):
            at = (j * rows + r) * 2
            re = in_ref[pl.ds(at, 128, stride=message), :]
            im = in_ref[pl.ds(at + 1, 128, stride=message), :]
            parts.append(jnp.concatenate([re, im], axis=1))
        upper, lower = split(jnp.concatenate(parts, axis=0))
        return mm(forward, jnp.concatenate([upper, lower], axis=0), ((1,), (0,)))

    def sample(j, got):
        mask = mask_ref[j]
        re = (got[:half, :128] + got[half:, 128:]) * mask
        im = (got[:half, 128:] - got[half:, :128]) * mask
        upper, lower = split(jnp.concatenate([re, im], axis=1))
        back = mm(inverse, jnp.concatenate([upper, lower], axis=0), ((1,), (0,)))
        store(j, back)

    def store(j, got):
        re = got[:half, :128] - got[half:, 128:]
        im = got[:half, 128:] + got[half:, :128]
        for r in range(rows):
            at = (r * groups + j) * 2
            out_ref[pl.ds(at, 128, stride=message), :] = re[r * 128 : (r + 1) * 128]
            out_ref[pl.ds(at + 1, 128, stride=message), :] = im[r * 128 : (r + 1) * 128]

    staggered(groups, gather, sample)


def whole(values):
    return jnp.sum(jnp.sum(values, axis=0, keepdims=True), axis=1, keepdims=True)


def in_lanes(values):
    lane = lax.broadcasted_iota(jnp.int32, (1, 128), 1)
    row = jnp.zeros((1, 128), f32)
    for i, value in enumerate(values):
        row = jnp.where(lane == i, value, row)
    return row


def share(value, weight):
    return jnp.where(weight > 0, value / jnp.where(weight > 0, weight, 1.0), 0.0)


def combine_kernel(in_ref, all_ref, smooth_ref, table_ref, applied_ref, out_ref):
    frames, _, cols = all_ref.shape
    table = table_ref[...]
    table = jnp.concatenate([table, table], axis=0)
    groups = cols // 128
    span = 128 // frames
    zero = jnp.zeros((1, cols), f32)

    def backward(r):
        real, imag = [], []
        for j in range(groups):
            at = (r * groups + j) * 2
            real.append(in_ref[pl.ds(at, 128, stride=message), :].T)
            imag.append(in_ref[pl.ds(at + 1, 128, stride=message), :].T)
        both = jnp.concatenate(
            [jnp.concatenate(real, axis=1), jnp.concatenate(imag, axis=1)], axis=0
        )
        upper, lower = split(both)
        return mm(jnp.concatenate([upper, lower], axis=1), table, ((1,), (0,)))

    def add_coils(r, got):
        re = got[:128, :cols] - got[128:, cols:]
        im = got[128:, :cols] + got[:128, cols:]
        s_re, s_im = sens_rows(all_ref, 0, r), sens_rows(all_ref, 1, r)
        for f in range(frames):
            b_re = re[f * span : (f + 1) * span]
            b_im = im[f * span : (f + 1) * span]
            for p, t in enumerate((s_re * b_re + s_im * b_im, s_re * b_im - s_im * b_re)):
                i = p * rows + r
                total = jnp.sum(t, axis=0, keepdims=True)
                applied_ref[f, i : i + 1] = total + smooth_ref[f, i : i + 1]

    staggered(rows, backward, add_coils)
    six = 2 * rows
    zero = jnp.zeros((six, cols), f32)
    norm, curvature, size, cross, rest = zero, zero, zero, zero, zero
    for f in range(frames):
        value = applied_ref[f, 0:six]
        r = all_ref[f, at_residual : at_residual + six]
        norm += r * r
        curvature += all_ref[f, at_direction : at_direction + six] * value
        size += value * value
        cross += r * value
    size = whole(size)
    ratio = share(whole(cross), size)
    for f in range(frames):
        left = all_ref[f, at_residual : at_residual + six] - ratio * applied_ref[f, 0:six]
        rest += left * left
        applied_ref[f, six:] = jnp.zeros((applied_ref.shape[1] - six, cols), f32)
    row = in_lanes([whole(norm), whole(curvature), size, ratio, whole(rest)])
    out_ref[...] = jnp.broadcast_to(row[None], out_ref.shape)


def joined(parts):
    size, ratio = parts[:, 2:3], parts[:, 3:4]
    norm, curvature = whole(parts[:, 0:1]), whole(parts[:, 1:2])
    all_size = whole(size)
    all_ratio = share(whole(size * ratio), all_size)
    away = ratio - all_ratio
    rest = whole(parts[:, 4:5] + (size * away) * away)
    return norm, curvature, all_size, all_ratio, rest


def join_kernel(parts_ref, applied_ref, out_ref):
    row = in_lanes(joined(parts_ref[:, 0, :]))
    out_ref[...] = applied_ref[...]
    for f in range(out_ref.shape[0]):
        out_ref[f, 2 * rows : 2 * rows + 1, 0:128] = row


def finish_kernel(
    all_ref, iterate_ref, residual_ref, direction_ref, new_iterate_ref, new_residual_ref, new_direction_ref, norm_ref
):
    slices = all_ref.shape[0]
    parts = [all_ref[z, 2 * rows : 2 * rows + 1, 0:128] for z in range(slices)]
    old_norm, curvature, size, ratio, rest = joined(jnp.concatenate(parts, axis=0))
    step = old_norm / curvature
    away = ratio - step
    new_norm = rest + (size * away) * away
    turn = new_norm / old_norm
    for i in range(direction_ref.shape[0]):
        d = direction_ref[i]
        applied = jnp.concatenate([all_ref[z, i : i + 1] for z in range(slices)], axis=0)
        fresh = residual_ref[i] - step * applied
        new_iterate_ref[i] = iterate_ref[i] + step * d
        new_residual_ref[i] = fresh
        new_direction_ref[i] = fresh + turn * d
    norm_ref[...] = jnp.broadcast_to(new_norm, norm_ref.shape)


vmem = pl.BlockSpec(memory_space=pltpu.VMEM)
smem = pl.BlockSpec(memory_space=pltpu.SMEM)
hbm = pl.BlockSpec(memory_space=pltpu.HBM)


params = pltpu.CompilerParams(vmem_limit_bytes=40 * 1024 * 1024)


def call(kernel, ins, outs, name, scalars=0):
    return pl.pallas_call(
        kernel,
        out_shape=[
            jax.ShapeDtypeStruct(s, f32) if isinstance(s, tuple) else jax.ShapeDtypeStruct(s.shape, s.dtype)
            for s in outs
        ],
        in_specs=[smem] * scalars + [vmem] * (len(ins) - scalars),
        out_specs=[vmem] * len(outs),
        compiler_params=params,
        name=name,
    )(*ins)


def tell(arrays, slices, cols):
    return pl.pallas_call(
        tell_kernel,
        out_shape=jax.ShapeDtypeStruct((slices, told, cols), f32),
        in_specs=[hbm] * len(arrays),
        out_specs=vmem,
        scratch_shapes=[pltpu.VMEM(a.shape, a.dtype) for a in arrays]
        + [pltpu.SemaphoreType.DMA((len(arrays),))],
        compiler_params=pltpu.CompilerParams(vmem_limit_bytes=65_000_000),
        name="tell",
    )(*arrays)


def swap(values, axis):
    pairs = values.reshape(values.shape[0] // 2, 2, 128)
    return lax.all_to_all(pairs, axis, 0, 0, tiled=True).reshape(values.shape)


def body(iterate, residual, direction, sensitivity, sampling, edge_weight):
    slabs = lax.axis_size(slab_axes)
    frames = lax.axis_size("coil")
    zdim, cols = direction.shape[2], direction.shape[4]

    sens = jnp.swapaxes(sensitivity, 2, 3)
    d = jnp.swapaxes(direction, 2, 3)[:, 0]
    r = jnp.swapaxes(residual, 2, 3)[:, 0]
    x = jnp.swapaxes(iterate, 2, 3)[:, 0]
    w = jnp.swapaxes(edge_weight, 1, 2)[0]

    cos, sin = dft_tables(cols)
    by_slab = np.arange(cols).reshape(cols // rows, rows).T.reshape(-1)
    natural = jnp.asarray(np.concatenate([cos, sin], axis=0))
    forward = jnp.asarray(np.concatenate([cos[:, by_slab], sin[:, by_slab]], axis=0))
    inverse = jnp.asarray(np.concatenate([cos[by_slab], sin[by_slab]], axis=0))
    wide = jnp.asarray(np.concatenate([cos, sin], axis=1))

    place = jnp.stack([lax.axis_index(slab_axes), jnp.int32(slabs)]).astype(jnp.int32)
    mine = lax.all_to_all(tell((sens, d, r, w), zdim, cols), "coil", 0, 0, tiled=True)
    (natural,) = call(table_kernel, (natural,), [natural], "table")

    lines = slabs * message
    (spectrum,) = call(images_kernel, (mine, natural), [(lines, 128)], "images")
    spectrum = swap(spectrum, slab_axes)
    last, first = call(edges_kernel, (mine,), [(frames, 3, cols), (frames, 2, cols)], "edges")
    up = [(i, i + 1) for i in range(slabs - 1)]
    before = lax.ppermute(last, slab_axes, up)
    after = lax.ppermute(first, slab_axes, [(j, i) for i, j in up])
    (mask,) = call(mask_kernel, (place, sampling), [(cols // 128, cols, 128)], "mask", 1)
    (smooth,) = call(
        smooth_kernel, (place, mine, before, after), [(frames, 2 * rows, cols)], "smooth", 1
    )
    spectrum, smooth = lax.optimization_barrier((spectrum, smooth))
    (back,) = call(
        middle_kernel, (spectrum, mask, forward, inverse), [(lines, 128)], "middle"
    )
    back = swap(back, slab_axes)
    applied, parts = call(
        combine_kernel,
        (back, mine, smooth, wide),
        [(frames, 8, cols), (slabs, 1, 128)],
        "combine",
    )
    parts = lax.all_to_all(parts, slab_axes, 0, 0, tiled=True)
    (applied,) = call(join_kernel, (parts, applied), [applied], "join")
    applied = lax.all_to_all(applied, "coil", 0, 0, tiled=True)

    flat = (2 * rows, zdim, cols)
    x, r, d = (v.reshape(flat) for v in (x, r, d))
    new_x, new_r, new_d, norm = call(
        finish_kernel, (applied, x, r, d), [flat, flat, flat, (1, 128)], "finish"
    )

    def restore(values):
        return jnp.swapaxes(values.reshape(2, 1, rows, zdim, cols), 2, 3)

    return restore(new_x), restore(new_r), restore(new_d), norm[0, 0]


def solution(mesh):
    fine = Mesh(mesh.devices.reshape(8, 8, 2, 4), ("z", "y", "core", "coil"))
    image = P(None, "coil", None, slab_axes, None)
    return jax.shard_map(
        body,
        mesh=fine,
        in_specs=(image, image, image, image, P(), P("coil", None, slab_axes, None)),
        out_specs=(image, image, image, P()),
        check_vma=False,
    )
```

time: 145 us -> 141 us (0.972)
  blocking collectives: 72.1 us -> 65.6 us
  waiting for transfers between devices: 28 us -> 30.6 us
  local copies, waits for them, and re-layouts: 4.13 us -> 1.7 us
  Pallas kernels: 9.65 us -> 11.4 us
    all_to_all x3 -> x2, blocking collectives: 31.7 us -> 24.9 us  [the longest x1 18.2 us: body(): parts = lax.all_to_all(parts, slab_axes, 0, 0, tiled=True)]
    all_to_all x1, waiting for transfers between devices: 3.9 us -> 6.44 us  [body(): lax.all_to_all(tell((sens, d, r, w), zdim, cols), 'coil', 0, 0, tiled=True)]
    pallas_call x0 -> x1, Pallas kernels: none -> 1.98 us  [tell(): pl.pallas_call(tell_kernel, out_shape=jax.ShapeDtypeStruct((slices, told,...]
    broadcast_in_dim x1 -> x0, local copies, waits for them, and re-layouts: 1.51 us -> none  [body(): copies = jnp.broadcast_to(d[None], (frames,) + d.shape)]
    pallas_call x11 -> x9, Pallas kernels: 9.65 us -> 9.45 us  [call(): pl.pallas_call(kernel, out_shape=[jax.ShapeDtypeStruct(s, f32) if isinsta...]
where the time goes in v5:
time: 141 us; the launch traced here: 140 us
  blocking collectives  65.6 us (47%)
  waiting for transfers between devices  30.6 us (22%)
  starting transfers between devices  30.3 us (21%)
  Pallas kernels  11.4 us (8%)
  local copies, waits for them, and re-layouts  1.7 us (1%)
    all_to_all x1, blocking collectives, swap(): return lax.all_to_all(pairs, axis, 0, 0, tiled=True).reshape(values.shape)  40.7 us
    all_to_all x1, starting transfers between devices, swap(): return lax.all_to_all(pairs, axis, 0, 0, tiled=True).reshape(values.shape)  20 us
    ppermute x1, waiting for transfers between devices, body(): after = lax.ppermute(first, slab_axes, [(j, i) for i, j in up])  18.7 us
    all_to_all x1, blocking collectives, body(): parts = lax.all_to_all(parts, slab_axes, 0, 0, tiled=True)  18.2 us
    pallas_call x9, Pallas kernels, call(): pl.pallas_call(kernel, out_shape=[jax.ShapeDtypeStruct(s, f32) if isinsta...  9.45 us
    all_to_all x1, blocking collectives, body(): applied = lax.all_to_all(applied, 'coil', 0, 0, tiled=True)  6.74 us
    all_to_all x1, waiting for transfers between devices, body(): lax.all_to_all(tell((sens, d, r, w), zdim, cols), 'coil', 0, 0, tiled=True)  6.44 us
    all_to_all x1, waiting for transfers between devices, swap(): return lax.all_to_all(pairs, axis, 0, 0, tiled=True).reshape(values.shape)  5.46 us
  transfers between devices with their start and end apart: 4, of which 3 were waited for; matrix products, arithmetic and copies ran while one was open for 0% of the time, Pallas kernels for 2%

profile of v5, /device:TPU:1, one launch (start us, length us, event | category | flops | bytes accessed | tf_op | source)
XLA Modules:
  0.0 140.4 jit_solution(637452023745325818)
XLA Ops:
  0.6 0.0 copy-start.1
  0.6 2.0 %tell.1 = f32[4,72,384]{2,1,0:T(8,128)} custom-call(bf16[2,8,3,4,384]{4,3,2,1,0:T(4,128)(2,1)} %bitcast.51, f32[2,3,4,384]{3,2,1,0:T(4,128)} %bitcast.46, f32[2,3,4,384]{3,2,1,0:T(4,128)} %bitcast.48, s32[3,4,384]{2,1,0:T(4,128)} %bitcast.52), custom_call_target="tpu_custom_call" | custom-call | tf_op jit(solution)/shard_map/tell/pallas_call | solution.py:355
  2.6 4.9 %all-to-all-start = ((f32[4,72,384]{2,1,0:T(8,128)}), f32[4,72,384]{2,1,0:T(8,128)S(1)}, u32[]{:S(2)}, u32[]{:S(2)}) async-start(f32[4,72,384]{2,1,0:T(8,128)} %tell.1), calls=%async_computation | async-start | bytes 884736 | tf_op jit(solution)/shard_map/all_to_all | solution.py:391
  7.5 0.0 copy-done.1
  7.5 0.1 table.1.table_ref
  7.5 6.4 %all-to-all-done.all_ref = f32[4,72,384]{2,1,0:T(8,128)S(1)} async-done(((f32[4,72,384]{2,1,0:T(8,128)}), f32[4,72,384]{2,1,0:T(8,128)S(1)}, u32[]{:S(2)}, u32[]{:S(2)}) %all-to-all-start) | async-done | bytes 442400 | tf_op jit(solution)/shard_map/all_to_all | solution.py:391
  14.0 2.2 %images.1 = f32[2304,128]{1,0:T(8,128)} custom-call(f32[4,72,384]{2,1,0:T(8,128)S(1)} %all-to-all-done.all_ref, bf16[768,384]{1,0:T(8,128)(2,1)S(1)} %table.1.table_ref), custom_call_target="tpu_custom_call" | custom-call | tf_op jit(solution)/shard_map/images/pallas_call | solution.py:341
  16.1 20.0 %all-to-all-start.1 = ((f32[1152,2,128]{2,1,0:T(2,128)}), f32[1152,2,128]{2,1,0:T(2,128)S(1)}, u32[]{:S(2)}, u32[]{:S(2)}) async-start(f32[1152,2,128]{2,1,0:T(2,128)} %bitcast.9), calls=%async_computation.1 | async-start | bytes 2359296 | tf_op jit(solution)/shard_map/all_to_all | solution.py:369
  36.2 3.5 %collective-permute-start = (f32[4,3,384]{2,1,0:T(4,128)S(1)}, f32[4,3,384]{2,1,0:T(4,128)S(1)}, u32[]{:S(2)}, u32[]{:S(2)}) collective-permute-start(f32[4,3,384]{2,1,0:T(4,128)S(1)} %get-tuple-element.14), channel_id=1, source_target_pairs={{0,4},{4,8},{8,12},{12,16},{16,20},{20,24},{24,28},{28,32},{32,36}... | collective-permute-start | bytes 55304 | tf_op jit(solution)/shard_map/ppermute | solution.py:399
  39.7 1.9 %collective-permute-start.1 = (f32[4,2,384]{2,1,0:T(2,128)S(1)}, f32[4,2,384]{2,1,0:T(2,128)S(1)}, u32[]{:S(2)}, u32[]{:S(2)}) collective-permute-start(f32[4,2,384]{2,1,0:T(2,128)S(1)} %get-tuple-element.15), channel_id=1, source_target_pairs={{4,0},{8,4},{12,8},{16,12},{20,16},{24,20},{28,24},{32,28},{36,32}... | collective-permute-start | bytes 36872 | tf_op jit(solution)/shard_map/ppermute | solution.py:400
  41.6 0.1 pad_add_fusion.place_ref
  41.7 0.0 copy-start
  41.7 1.7 %copy-done = s32[4,384,384]{2,1,0:T(8,128)S(1)} copy-done((s32[4,384,384]{2,1,0:T(8,128)S(1)}, s32[4,384,384]{2,1,0:T(8,128)}, u32[]{:S(2)}) %copy-start) | copy-done | bytes 2359320
  43.4 0.0 copy-start.3
  43.4 0.0 copy-start.4
  43.4 1.4 %mask.1.mask_ref = f32[3,384,128]{2,1,0:T(8,128)S(1)} custom-call(s32[2]{0:T(128)S(1)} %pad_add_fusion.place_ref, s32[4,384,384]{2,1,0:T(8,128)S(1)} %copy-done), custom_call_target="tpu_custom_call" | custom-call | tf_op jit(solution)/shard_map/mask/pallas_call | solution.py:341
  44.8 18.7 %collective-permute-done.1.after_ref = f32[4,2,384]{2,1,0:T(2,128)S(1)} collective-permute-done((f32[4,2,384]{2,1,0:T(2,128)S(1)}, f32[4,2,384]{2,1,0:T(2,128)S(1)}, u32[]{:S(2)}, u32[]{:S(2)}) %collective-permute-start.1) | collective-permute-done | bytes 12320 | tf_op jit(solution)/shard_map/ppermute | solution.py:400
  63.5 0.0 collective-permute-done.before_ref
  63.5 0.8 smooth.1.smooth_ref
  64.3 5.5 %all-to-all-done.1 = f32[1152,2,128]{2,1,0:T(2,128)S(1)} async-done(((f32[1152,2,128]{2,1,0:T(2,128)}), f32[1152,2,128]{2,1,0:T(2,128)S(1)}, u32[]{:S(2)}, u32[]{:S(2)}) %all-to-all-start.1) | async-done | bytes 1179680 | tf_op jit(solution)/shard_map/all_to_all | solution.py:369
  69.8 0.0 copy-done.3
  69.8 0.0 copy-done.4
  69.8 2.1 %middle.1 = f32[2304,128]{1,0:T(8,128)S(1)} custom-call(f32[2304,128]{1,0:T(8,128)S(1)} %bitcast.44, f32[3,384,128]{2,1,0:T(8,128)S(1)} %mask.1.mask_ref, bf16[768,384]{1,0:T(8,128)(2,1)S(1)} %copy-done.3, bf16[768,384]{1,0:T(8,128)(2,1)S(1)} %copy-done.4), custom_call_target="tpu_custom_call" | custom-call | tf_op jit(solution)/shard_map/middle/pallas_call | solution.py:341
  71.9 0.0 copy-start.2
  71.9 40.7 %all_to_all.25 = f32[1152,2,128]{2,1,0:T(2,128)S(1)} all-to-all(f32[1152,2,128]{2,1,0:T(2,128)S(1)} %bitcast.45), channel_id=1, replica_groups=mesh['z'=8,'y'=8,'core'=2,'coil'=4] {'z','y','core'}, dimensions={0} | all-to-all | bytes 2359296 | tf_op jit(solution)/shard_map/all_to_all | solution.py:369
  112.6 0.0 copy-done.2
  112.6 0.0 copy-start.5
  112.6 0.0 copy-start.6
  112.6 0.0 copy-start.7
  112.6 1.5 %combine.1 = (f32[4,8,384]{2,1,0:T(8,128)S(1)}, f32[128,1,128]{2,1,0:T(1,128)S(1)}) custom-call(f32[2304,128]{1,0:T(8,128)S(1)} %bitcast.43, f32[4,72,384]{2,1,0:T(8,128)S(1)} %all-to-all-done.all_ref, f32[4,6,384]{2,1,0:T(8,128)S(1)} %smooth.1.smooth_ref, bf16[384,768]{1,0:T(8,128)(2,1)S(1)} %copy-done.2), custom_call_target="tpu_custom_call" | custom-call | tf_op jit(solution)/shard_map/combine/pallas_call | solution.py:341
  114.1 18.2 %all_to_all.26.parts_ref = f32[128,1,128]{2,1,0:T(1,128)S(1)} all-to-all(f32[128,1,128]{2,1,0:T(1,128)S(1)} %get-tuple-element.18), channel_id=1, replica_groups=mesh['z'=8,'y'=8,'core'=2,'coil'=4] {'z','y','core'}, dimensions={0} | all-to-all | bytes 131072 | tf_op jit(solution)/shard_map/all_to_all | solution.py:416
  132.3 0.3 join.1
  132.6 6.7 %all_to_all.27.all_ref = f32[4,8,384]{2,1,0:T(8,128)S(1)} all-to-all(f32[4,8,384]{2,1,0:T(8,128)S(1)} %join.1), channel_id=1, replica_groups=mesh['z'=8,'y'=8,'core'=2,'coil'=4] {'coil'}, dimensions={0} | all-to-all | bytes 98304 | tf_op jit(solution)/shard_map/all_to_all | solution.py:418
  139.4 0.0 copy-done.5
  139.4 0.0 copy-done.6
  139.4 0.0 copy-done.7
  139.4 1.0 finish.1
  (1 shorter events, 0.0 us)
Async XLA Ops:
  0.6 6.9 %copy-start.1 = (bf16[768,384]{1,0:T(8,128)(2,1)S(1)}, bf16[768,384]{1,0:T(8,128)(2,1)}, u32[]{:S(2)}) copy-start(bf16[768,384]{1,0:T(8,128)(2,1)} %constant.29.clone.table_ref) | copy-start | bytes 1769476
  2.6 11.3 %all-to-all-start = ((f32[4,72,384]{2,1,0:T(8,128)}), f32[4,72,384]{2,1,0:T(8,128)S(1)}, u32[]{:S(2)}, u32[]{:S(2)}) async-start(f32[4,72,384]{2,1,0:T(8,128)} %tell.1), calls=%async_computation | async-start | bytes 884736 | tf_op jit(solution)/shard_map/all_to_all | solution.py:391
  16.1 53.7 %all-to-all-start.1 = ((f32[1152,2,128]{2,1,0:T(2,128)}), f32[1152,2,128]{2,1,0:T(2,128)S(1)}, u32[]{:S(2)}, u32[]{:S(2)}) async-start(f32[1152,2,128]{2,1,0:T(2,128)} %bitcast.9), calls=%async_computation.1 | async-start | bytes 2359296 | tf_op jit(solution)/shard_map/all_to_all | solution.py:369
  36.2 27.4 %collective-permute-start = (f32[4,3,384]{2,1,0:T(4,128)S(1)}, f32[4,3,384]{2,1,0:T(4,128)S(1)}, u32[]{:S(2)}, u32[]{:S(2)}) collective-permute-start(f32[4,3,384]{2,1,0:T(4,128)S(1)} %get-tuple-element.14), channel_id=1, source_target_pairs={{0,4},{4,8},{8,12},{12,16},{16,20},{20,24},{24,28},{28,32},{32,36}... | collective-permute-start | bytes 55304 | tf_op jit(solution)/shard_map/ppermute | solution.py:399
  39.7 23.8 %collective-permute-start.1 = (f32[4,2,384]{2,1,0:T(2,128)S(1)}, f32[4,2,384]{2,1,0:T(2,128)S(1)}, u32[]{:S(2)}, u32[]{:S(2)}) collective-permute-start(f32[4,2,384]{2,1,0:T(2,128)S(1)} %get-tuple-element.15), channel_id=1, source_target_pairs={{4,0},{8,4},{12,8},{16,12},{20,16},{24,20},{28,24},{32,28},{36,32}... | collective-permute-start | bytes 36872 | tf_op jit(solution)/shard_map/ppermute | solution.py:400
  41.7 1.7 %copy-start = (s32[4,384,384]{2,1,0:T(8,128)S(1)}, s32[4,384,384]{2,1,0:T(8,128)}, u32[]{:S(2)}) copy-start(s32[4,384,384]{2,1,0:T(8,128)} %sampling_ref.1) | copy-start | bytes 7077892
  43.4 26.4 %copy-start.3 = (bf16[768,384]{1,0:T(8,128)(2,1)S(1)}, bf16[768,384]{1,0:T(8,128)(2,1)}, u32[]{:S(2)}) copy-start(bf16[768,384]{1,0:T(8,128)(2,1)} %constant.30.clone.forward_ref) | copy-start | bytes 1769476
  43.4 26.4 %copy-start.4 = (bf16[768,384]{1,0:T(8,128)(2,1)S(1)}, bf16[768,384]{1,0:T(8,128)(2,1)}, u32[]{:S(2)}) copy-start(bf16[768,384]{1,0:T(8,128)(2,1)} %constant.31.clone.inverse_ref) | copy-start | bytes 1769476
  71.9 40.7 %copy-start.2 = (bf16[384,768]{1,0:T(8,128)(2,1)S(1)}, bf16[384,768]{1,0:T(8,128)(2,1)}, u32[]{:S(2)}) copy-start(bf16[384,768]{1,0:T(8,128)(2,1)} %constant.32.clone.table_ref) | copy-start | bytes 1769476
  112.6 26.8 %copy-start.5 = (f32[2,1,4,3,384]{4,2,3,1,0:T(4,128)S(1)}, f32[2,1,4,3,384]{4,2,3,1,0:T(4,128)}, u32[]{:S(2)}) copy-start(f32[2,1,4,3,384]{4,2,3,1,0:T(4,128)} %param.12) | copy-start | bytes 110596
  112.6 26.8 %copy-start.6 = (f32[2,1,4,3,384]{4,2,3,1,0:T(4,128)S(1)}, f32[2,1,4,3,384]{4,2,3,1,0:T(4,128)}, u32[]{:S(2)}) copy-start(f32[2,1,4,3,384]{4,2,3,1,0:T(4,128)} %param.11) | copy-start | bytes 110596
  112.6 26.8 %copy-start.7 = (f32[2,1,4,3,384]{4,2,3,1,0:T(4,128)S(1)}, f32[2,1,4,3,384]{4,2,3,1,0:T(4,128)}, u32[]{:S(2)}) copy-start(f32[2,1,4,3,384]{4,2,3,1,0:T(4,128)} %param.10) | copy-start | bytes 110596

commit v6 on v5

--- a/solution.py
+++ b/solution.py
@@ -12,6 +12,7 @@
 
 smooth_scale = 0.05
 slab_axes = ("z", "y", "core")
+swap_axes = ("z", "core", "y")
 f32 = jnp.float32
 bf16 = jnp.bfloat16
 
@@ -19,10 +20,11 @@
 
 rows, coils = 3, 8
 at_direction = 2 * rows * coils
-at_residual = at_direction + 2 * rows
-at_smooth = at_residual + 2 * rows
-at_weight = at_smooth + 2 * rows
-told = 72
+at_edge = at_direction + 2 * rows
+told = at_edge + 2
+at_smooth = 2 * rows
+at_weight = 4 * rows
+told_later = 16
 
 
 def dft_tables(length):
@@ -60,41 +62,53 @@
 
 
 def tell_kernel(*refs):
-    sources, out_ref, held, done = refs[:4], refs[4], refs[5:9], refs[9]
-    copies = [pltpu.make_async_copy(sources[i], held[i], done.at[i]) for i in range(4)]
+    sources, out_ref, held, done = refs[:3], refs[3], refs[4:7], refs[7]
+    copies = [pltpu.make_async_copy(sources[i], held[i], done.at[i]) for i in range(3)]
     for copy in copies:
         copy.start()
     for copy in copies:
         copy.wait()
-    sens_ref, direction_ref, residual_ref, weight_ref = held
+    sens_ref, direction_ref, weight_ref = held
     slices, _, cols = out_ref.shape
-    zero_slice = jnp.zeros((1, cols), f32)
 
     def put(row, values):
         for z in range(slices):
             out_ref[z, row : row + 1] = values[z : z + 1]
 
-    for r in range(rows):
-        weight = weight_ref[r].astype(f32)
-        put(at_weight + r, weight)
-        for p in range(2):
+    for p in range(2):
+        for r in range(rows):
             i = p * rows + r
             tiles = [sens_ref[p, c, r].astype(f32) for c in range(coils)]
             for z in range(slices):
                 out_ref[z, i * coils : (i + 1) * coils] = jnp.concatenate(
                     [t[z : z + 1] for t in tiles], axis=0
                 )
+            put(at_direction + i, direction_ref[p, r])
+    put(at_edge, weight_ref[rows - 1].astype(f32))
+    put(at_edge + 1, jnp.zeros((slices, cols), f32))
+
+
+def later_kernel(place_ref, direction_ref, residual_ref, weight_ref, *refs):
+    out_refs, held_ref = refs[:-1], refs[-1]
+    plane, planes = place_ref[3], len(out_refs)
+    cols = direction_ref.shape[3]
+    zero_slice = jnp.zeros((1, cols), f32)
+    for r in range(rows):
+        weight = weight_ref[r].astype(f32)
+        held_ref[at_weight + r] = weight
+        for p in range(2):
+            i = p * rows + r
             v = direction_ref[p, r]
-            put(at_direction + i, v)
-            put(at_residual + i, residual_ref[p, r])
+            held_ref[i] = residual_ref[p, r]
             flux = weight[:-1] * (v[1:] - v[:-1])
-            put(
-                at_smooth + i,
-                jnp.concatenate([zero_slice, flux], axis=0)
-                - jnp.concatenate([flux, zero_slice], axis=0),
+            held_ref[at_smooth + i] = jnp.concatenate([zero_slice, flux], axis=0) - jnp.concatenate(
+                [flux, zero_slice], axis=0
             )
-    for z in range(slices):
-        out_ref[z, at_weight + rows :] = jnp.zeros((told - at_weight - rows, cols), f32)
+    for k in range(planes):
+        z = lax.rem(plane + k, planes)
+        for i in range(at_weight + rows):
+            out_refs[k][i : i + 1] = held_ref[i, pl.ds(z, 1), :]
+        out_refs[k][at_weight + rows :] = jnp.zeros((told_later - at_weight - rows, cols), f32)
 
 
 def table_kernel(table_ref, out_ref):
@@ -152,12 +166,16 @@
             at = at_direction + p * rows
             last_ref[f, p : p + 1] = all_ref[f, at + rows - 1 : at + rows]
             first_ref[f, p : p + 1] = all_ref[f, at : at + 1]
-        last_ref[f, 2:3] = all_ref[f, at_weight + rows - 1 : at_weight + rows]
-
-
-def smooth_kernel(place_ref, all_ref, before_ref, after_ref, out_ref):
-    slab, slabs = place_ref[0], place_ref[1]
+        last_ref[f, 2:3] = all_ref[f, at_edge : at_edge + 1]
+
+
+def smooth_kernel(place_ref, all_ref, before_ref, after_ref, *refs):
+    later_refs, out_ref, residual_ref, later_ref = refs[:-3], *refs[-3:]
+    slab, slabs, plane = place_ref[1], place_ref[2], place_ref[3]
     frames, _, cols = all_ref.shape
+    for k in range(frames):
+        later_ref[lax.rem(plane + frames - k, frames)] = later_refs[k][...]
+    residual_ref[...] = later_ref[:, : 2 * rows]
     has_next_row = jnp.where(slab < slabs - 1, 1.0, 0.0)
     has_previous_row = jnp.where(slab > 0, 1.0, 0.0)
     zero_col = jnp.zeros((rows, 1), f32)
@@ -166,8 +184,8 @@
         from_frame = None
         for f in range(frames):
             v = all_ref[f, at : at + rows]
-            weight = all_ref[f, at_weight : at_weight + rows]
-            term = all_ref[f, at_smooth + p * rows : at_smooth + (p + 1) * rows]
+            weight = later_ref[f, at_weight : at_weight + rows]
+            term = later_ref[f, at_smooth + p * rows : at_smooth + (p + 1) * rows]
             if from_frame is not None:
                 term = term + from_frame
             if f < frames - 1:
@@ -239,7 +257,7 @@
     return jnp.where(weight > 0, value / jnp.where(weight > 0, weight, 1.0), 0.0)
 
 
-def combine_kernel(in_ref, all_ref, smooth_ref, table_ref, applied_ref, out_ref):
+def combine_kernel(in_ref, all_ref, smooth_ref, residual_ref, table_ref, applied_ref, out_ref):
     frames, _, cols = all_ref.shape
     table = table_ref[...]
     table = jnp.concatenate([table, table], axis=0)
@@ -277,7 +295,7 @@
     norm, curvature, size, cross, rest = zero, zero, zero, zero, zero
     for f in range(frames):
         value = applied_ref[f, 0:six]
-        r = all_ref[f, at_residual : at_residual + six]
+        r = residual_ref[f]
         norm += r * r
         curvature += all_ref[f, at_direction : at_direction + six] * value
         size += value * value
@@ -285,7 +303,7 @@
     size = whole(size)
     ratio = share(whole(cross), size)
     for f in range(frames):
-        left = all_ref[f, at_residual : at_residual + six] - ratio * applied_ref[f, 0:six]
+        left = residual_ref[f] - ratio * applied_ref[f, 0:six]
         rest += left * left
         applied_ref[f, six:] = jnp.zeros((applied_ref.shape[1] - six, cols), f32)
     row = in_lanes([whole(norm), whole(curvature), size, ratio, whole(rest)])
@@ -337,7 +355,7 @@
 params = pltpu.CompilerParams(vmem_limit_bytes=40 * 1024 * 1024)
 
 
-def call(kernel, ins, outs, name, scalars=0):
+def call(kernel, ins, outs, name, scalars=0, scratch=()):
     return pl.pallas_call(
         kernel,
         out_shape=[
@@ -346,6 +364,7 @@
         ],
         in_specs=[smem] * scalars + [vmem] * (len(ins) - scalars),
         out_specs=[vmem] * len(outs),
+        scratch_shapes=list(scratch),
         compiler_params=params,
         name=name,
     )(*ins)
@@ -381,35 +400,56 @@
     w = jnp.swapaxes(edge_weight, 1, 2)[0]
 
     cos, sin = dft_tables(cols)
-    by_slab = np.arange(cols).reshape(cols // rows, rows).T.reshape(-1)
+    sizes = [lax.axis_size(a) for a in slab_axes]
+    order = [slab_axes.index(a) for a in swap_axes]
+    by_slab = np.arange(cols).reshape(*sizes, rows).transpose(3, *order).reshape(-1)
     natural = jnp.asarray(np.concatenate([cos, sin], axis=0))
     forward = jnp.asarray(np.concatenate([cos[:, by_slab], sin[:, by_slab]], axis=0))
     inverse = jnp.asarray(np.concatenate([cos[by_slab], sin[by_slab]], axis=0))
     wide = jnp.asarray(np.concatenate([cos, sin], axis=1))
 
-    place = jnp.stack([lax.axis_index(slab_axes), jnp.int32(slabs)]).astype(jnp.int32)
-    mine = lax.all_to_all(tell((sens, d, r, w), zdim, cols), "coil", 0, 0, tiled=True)
+    place = jnp.stack(
+        [lax.axis_index(swap_axes), lax.axis_index(slab_axes), jnp.int32(slabs), lax.axis_index("coil")]
+    ).astype(jnp.int32)
+    mine = lax.all_to_all(tell((sens, d, w), zdim, cols), "coil", 0, 0, tiled=True)
     (natural,) = call(table_kernel, (natural,), [natural], "table")
 
     lines = slabs * message
     (spectrum,) = call(images_kernel, (mine, natural), [(lines, 128)], "images")
-    spectrum = swap(spectrum, slab_axes)
+    spectrum = swap(spectrum, swap_axes)
     last, first = call(edges_kernel, (mine,), [(frames, 3, cols), (frames, 2, cols)], "edges")
     up = [(i, i + 1) for i in range(slabs - 1)]
     before = lax.ppermute(last, slab_axes, up)
     after = lax.ppermute(first, slab_axes, [(j, i) for i, j in up])
     (mask,) = call(mask_kernel, (place, sampling), [(cols // 128, cols, 128)], "mask", 1)
-    (smooth,) = call(
-        smooth_kernel, (place, mine, before, after), [(frames, 2 * rows, cols)], "smooth", 1
-    )
-    spectrum, smooth = lax.optimization_barrier((spectrum, smooth))
+    own, *others = call(
+        later_kernel,
+        (place, d, r, w),
+        [(told_later, cols)] * frames,
+        "later",
+        1,
+        [pltpu.VMEM((told_later, zdim, cols), f32)],
+    )
+    later = [own]
+    for k, other in enumerate(others, 1):
+        later.append(lax.ppermute(other, "coil", [(i, (i + k) % frames) for i in range(frames)]))
+    six = (frames, 2 * rows, cols)
+    smooth, rest = call(
+        smooth_kernel,
+        (place, mine, before, after, *later),
+        [six, six],
+        "smooth",
+        1,
+        [pltpu.VMEM((frames, told_later, cols), f32)],
+    )
+    spectrum, smooth, rest = lax.optimization_barrier((spectrum, smooth, rest))
     (back,) = call(
         middle_kernel, (spectrum, mask, forward, inverse), [(lines, 128)], "middle"
     )
-    back = swap(back, slab_axes)
+    back = swap(back, swap_axes)
     applied, parts = call(
         combine_kernel,
-        (back, mine, smooth, wide),
+        (back, mine, smooth, rest, wide),
         [(frames, 8, cols), (slabs, 1, 128)],
         "combine",
     )

time: 141 us -> 140 us (level)
  waiting for transfers between devices: 30.6 us -> 20.7 us
  starting transfers between devices: 30.3 us -> 38.9 us
    ppermute x1, waiting for transfers between devices: 18.7 us -> 9.03 us  [body(): after = lax.ppermute(first, slab_axes, [(j, i) for i, j in up])]
    ppermute x0 -> x3, starting transfers between devices: none -> 8.42 us  [body(): lax.ppermute(other, 'coil', [(i, (i + k) % frames) for i in range(frames)])]
    pallas_call x9 -> x10, Pallas kernels: 9.45 us -> 10.2 us  [call(): pl.pallas_call(kernel, out_shape=[jax.ShapeDtypeStruct(s, f32) if isinsta...]
  transfers between devices with their start and end apart: 4 -> 7, of which waited for: 3 -> 3; matrix products, arithmetic and copies ran while one was open for 0% -> 0% of each run, Pallas kernels for 2% -> 2%
where the time goes in v6:
time: 140 us; the launch traced here: 139 us
  blocking collectives  65 us (46%)
  starting transfers between devices  38.9 us (28%)
  waiting for transfers between devices  20.7 us (15%)
  Pallas kernels  12 us (9%)
  local copies, waits for them, and re-layouts  1.7 us (1%)
    all_to_all x1, blocking collectives, swap(): return lax.all_to_all(pairs, axis, 0, 0, tiled=True).reshape(values.shape)  40.6 us
    all_to_all x1, starting transfers between devices, swap(): return lax.all_to_all(pairs, axis, 0, 0, tiled=True).reshape(values.shape)  19.6 us
    all_to_all x1, blocking collectives, body(): parts = lax.all_to_all(parts, slab_axes, 0, 0, tiled=True)  17.7 us
    pallas_call x10, Pallas kernels, call(): pl.pallas_call(kernel, out_shape=[jax.ShapeDtypeStruct(s, f32) if isinsta...  10.2 us
    ppermute x1, waiting for transfers between devices, body(): after = lax.ppermute(first, slab_axes, [(j, i) for i, j in up])  9.03 us
    ppermute x3, starting transfers between devices, body(): lax.ppermute(other, 'coil', [(i, (i + k) % frames) for i in range(frames)])  8.42 us
    all_to_all x1, blocking collectives, body(): applied = lax.all_to_all(applied, 'coil', 0, 0, tiled=True)  6.74 us
    all_to_all x1, waiting for transfers between devices, body(): lax.all_to_all(tell((sens, d, w), zdim, cols), 'coil', 0, 0, tiled=True)  5.91 us
  transfers between devices with their start and end apart: 7, of which 3 were waited for; matrix products, arithmetic and copies ran while one was open for 0% of the time, Pallas kernels for 2%

profile of v6, /device:TPU:1, one launch (start us, length us, event | category | flops | bytes accessed | tf_op | source)
XLA Modules:
  0.0 139.2 jit_solution(3029705126860828930)
XLA Ops:
  0.6 0.0 copy-start.1
  0.6 1.9 %tell.1 = f32[4,56,384]{2,1,0:T(8,128)} custom-call(bf16[2,8,3,4,384]{4,3,2,1,0:T(4,128)(2,1)} %bitcast.56, f32[2,3,4,384]{3,2,1,0:T(4,128)} %bitcast.48, s32[3,4,384]{2,1,0:T(4,128)} %bitcast.53), custom_call_target="tpu_custom_call" | custom-call | tf_op jit(solution)/shard_map/tell/pallas_call | solution.py:374
  2.5 4.9 %all-to-all-start = ((f32[4,56,384]{2,1,0:T(8,128)}), f32[4,56,384]{2,1,0:T(8,128)S(1)}, u32[]{:S(2)}, u32[]{:S(2)}) async-start(f32[4,56,384]{2,1,0:T(8,128)} %tell.1), calls=%async_computation | async-start | bytes 688128 | tf_op jit(solution)/shard_map/all_to_all | solution.py:414
  7.4 0.0 copy-done.1
  7.4 0.1 table.1.table_ref
  7.5 5.9 %all-to-all-done.all_ref = f32[4,56,384]{2,1,0:T(8,128)S(1)} async-done(((f32[4,56,384]{2,1,0:T(8,128)}), f32[4,56,384]{2,1,0:T(8,128)S(1)}, u32[]{:S(2)}, u32[]{:S(2)}) %all-to-all-start) | async-done | bytes 344096 | tf_op jit(solution)/shard_map/all_to_all | solution.py:414
  13.4 2.2 %images.1 = f32[2304,128]{1,0:T(8,128)} custom-call(f32[4,56,384]{2,1,0:T(8,128)S(1)} %all-to-all-done.all_ref, bf16[768,384]{1,0:T(8,128)(2,1)S(1)} %table.1.table_ref), custom_call_target="tpu_custom_call" | custom-call | tf_op jit(solution)/shard_map/images/pallas_call | solution.py:359
  15.6 0.0 copy-start.5
  15.6 0.0 copy-start.6
  15.6 0.0 copy-start.7
  15.6 19.6 %all-to-all-start.1 = ((f32[1152,2,128]{2,1,0:T(2,128)}), f32[1152,2,128]{2,1,0:T(2,128)S(1)}, u32[]{:S(2)}, u32[]{:S(2)}) async-start(f32[1152,2,128]{2,1,0:T(2,128)} %bitcast.6), calls=%async_computation.1 | async-start | bytes 2359296 | tf_op jit(solution)/shard_map/all_to_all | solution.py:388
  35.2 0.1 pad_add_fusion.place_ref
  35.2 0.0 copy-done.5
  35.2 0.0 copy-done.6
  35.2 0.0 copy-done.7
  35.3 0.6 later.1
  35.9 2.2 %collective-permute-start.2 = (f32[16,384]{1,0:T(8,128)S(1)}, f32[16,384]{1,0:T(8,128)S(1)}, u32[]{:S(2)}, u32[]{:S(2)}) collective-permute-start(f32[16,384]{1,0:T(8,128)S(1)} %get-tuple-element.24), channel_id=1, source_target_pairs={{0,1},{1,2},{2,3},{3,0},{4,5},{5,6},{6,7},{7,4},{8,9},{9,10},{10,1... | collective-permute-start | bytes 73736 | tf_op jit(solution)/shard_map/ppermute | solution.py:435
  38.1 3.7 %collective-permute-start.3 = (f32[16,384]{1,0:T(8,128)S(1)}, f32[16,384]{1,0:T(8,128)S(1)}, u32[]{:S(2)}, u32[]{:S(2)}) collective-permute-start(f32[16,384]{1,0:T(8,128)S(1)} %get-tuple-element.25), channel_id=1, source_target_pairs={{0,2},{1,3},{2,0},{3,1},{4,6},{5,7},{6,4},{7,5},{8,10},{9,11},{10,... | collective-permute-start | bytes 73736 | tf_op jit(solution)/shard_map/ppermute | solution.py:435
  41.8 2.5 %collective-permute-start.4 = (f32[16,384]{1,0:T(8,128)S(1)}, f32[16,384]{1,0:T(8,128)S(1)}, u32[]{:S(2)}, u32[]{:S(2)}) collective-permute-start(f32[16,384]{1,0:T(8,128)S(1)} %get-tuple-element.26), channel_id=1, source_target_pairs={{0,3},{1,0},{2,1},{3,2},{4,7},{5,4},{6,5},{7,6},{8,11},{9,8},{10,9... | collective-permute-start | bytes 73736 | tf_op jit(solution)/shard_map/ppermute | solution.py:435
  44.3 4.1 %collective-permute-start = (f32[4,3,384]{2,1,0:T(4,128)S(1)}, f32[4,3,384]{2,1,0:T(4,128)S(1)}, u32[]{:S(2)}, u32[]{:S(2)}) collective-permute-start(f32[4,3,384]{2,1,0:T(4,128)S(1)} %get-tuple-element.21), channel_id=1, source_target_pairs={{0,4},{4,8},{8,12},{12,16},{16,20},{20,24},{24,28},{28,32},{32,36}... | collective-permute-start | bytes 55304 | tf_op jit(solution)/shard_map/ppermute | solution.py:422
  48.4 1.9 %collective-permute-start.1 = (f32[4,2,384]{2,1,0:T(2,128)S(1)}, f32[4,2,384]{2,1,0:T(2,128)S(1)}, u32[]{:S(2)}, u32[]{:S(2)}) collective-permute-start(f32[4,2,384]{2,1,0:T(2,128)S(1)} %get-tuple-element.22), channel_id=1, source_target_pairs={{4,0},{8,4},{12,8},{16,12},{20,16},{24,20},{28,24},{32,28},{36,32}... | collective-permute-start | bytes 36872 | tf_op jit(solution)/shard_map/ppermute | solution.py:423
  50.4 0.0 copy-start
  50.4 1.7 %copy-done = s32[4,384,384]{2,1,0:T(8,128)S(1)} copy-done((s32[4,384,384]{2,1,0:T(8,128)S(1)}, s32[4,384,384]{2,1,0:T(8,128)}, u32[]{:S(2)}) %copy-start) | copy-done | bytes 2359320
  52.0 0.0 copy-start.3
  52.0 0.0 copy-start.4
  52.0 1.4 %mask.1.mask_ref = f32[3,384,128]{2,1,0:T(8,128)S(1)} custom-call(s32[4]{0:T(128)S(1)} %pad_add_fusion.place_ref, s32[4,384,384]{2,1,0:T(8,128)S(1)} %copy-done), custom_call_target="tpu_custom_call" | custom-call | tf_op jit(solution)/shard_map/mask/pallas_call | solution.py:359
  53.5 0.0 collective-permute-done.2.refs_1_
  53.5 0.0 collective-permute-done.3.refs_2_
  53.5 0.0 collective-permute-done.4.refs_3_
  53.5 9.0 %collective-permute-done.1.after_ref = f32[4,2,384]{2,1,0:T(2,128)S(1)} collective-permute-done((f32[4,2,384]{2,1,0:T(2,128)S(1)}, f32[4,2,384]{2,1,0:T(2,128)S(1)}, u32[]{:S(2)}, u32[]{:S(2)}) %collective-permute-start.1) | collective-permute-done | bytes 12320 | tf_op jit(solution)/shard_map/ppermute | solution.py:423
  62.5 0.0 collective-permute-done.before_ref
  62.5 0.8 smooth.1
  63.4 5.7 %all-to-all-done.1 = f32[1152,2,128]{2,1,0:T(2,128)S(1)} async-done(((f32[1152,2,128]{2,1,0:T(2,128)}), f32[1152,2,128]{2,1,0:T(2,128)S(1)}, u32[]{:S(2)}, u32[]{:S(2)}) %all-to-all-start.1) | async-done | bytes 1179680 | tf_op jit(solution)/shard_map/all_to_all | solution.py:388
  69.1 0.0 copy-done.3
  69.1 0.0 copy-done.4
  69.1 2.1 %middle.1 = f32[2304,128]{1,0:T(8,128)S(1)} custom-call(f32[2304,128]{1,0:T(8,128)S(1)} %bitcast.46, f32[3,384,128]{2,1,0:T(8,128)S(1)} %mask.1.mask_ref, bf16[768,384]{1,0:T(8,128)(2,1)S(1)} %copy-done.3, bf16[768,384]{1,0:T(8,128)(2,1)S(1)} %copy-done.4), custom_call_target="tpu_custom_call" | custom-call | tf_op jit(solution)/shard_map/middle/pallas_call | solution.py:359
  71.2 0.0 copy-start.2
  71.2 40.6 %all_to_all.25 = f32[1152,2,128]{2,1,0:T(2,128)S(1)} all-to-all(f32[1152,2,128]{2,1,0:T(2,128)S(1)} %bitcast.47), channel_id=1, replica_groups=mesh['z'=8,'y'=8,'core'=2,'coil'=4] {'z','core','y'}, dimensions={0} | all-to-all | bytes 2359296 | tf_op jit(solution)/shard_map/all_to_all | solution.py:388
  111.8 0.0 copy-done.2
  111.8 0.0 copy-start.8
  111.8 1.6 %combine.1 = (f32[4,8,384]{2,1,0:T(8,128)S(1)}, f32[128,1,128]{2,1,0:T(1,128)S(1)}) custom-call(f32[2304,128]{1,0:T(8,128)S(1)} %bitcast.45, f32[4,56,384]{2,1,0:T(8,128)S(1)} %all-to-all-done.all_ref, f32[4,6,384]{2,1,0:T(8,128)S(1)} %get-tuple-element.30.smooth_ref, f32[4,6,384]{2,1,0:T(8,128)S(1)} %get-tuple-element.31.residual_ref, ...), custom_call_target="tpu_custom_call" | custom-call | tf_op jit(solution)/shard_map/combine/pallas_call | solution.py:359
  113.4 17.7 %all_to_all.26.parts_ref = f32[128,1,128]{2,1,0:T(1,128)S(1)} all-to-all(f32[128,1,128]{2,1,0:T(1,128)S(1)} %get-tuple-element.32), channel_id=1, replica_groups=mesh['z'=8,'y'=8,'core'=2,'coil'=4] {'z','y','core'}, dimensions={0} | all-to-all | bytes 131072 | tf_op jit(solution)/shard_map/all_to_all | solution.py:456
  131.1 0.3 join.1
  131.4 6.7 %all_to_all.27.all_ref = f32[4,8,384]{2,1,0:T(8,128)S(1)} all-to-all(f32[4,8,384]{2,1,0:T(8,128)S(1)} %join.1), channel_id=1, replica_groups=mesh['z'=8,'y'=8,'core'=2,'coil'=4] {'coil'}, dimensions={0} | all-to-all | bytes 98304 | tf_op jit(solution)/shard_map/all_to_all | solution.py:458
  138.2 0.0 copy-done.8
  138.2 1.0 finish.1
  (1 shorter events, 0.0 us)
Async XLA Ops:
  0.6 6.8 %copy-start.1 = (bf16[768,384]{1,0:T(8,128)(2,1)S(1)}, bf16[768,384]{1,0:T(8,128)(2,1)}, u32[]{:S(2)}) copy-start(bf16[768,384]{1,0:T(8,128)(2,1)} %constant.33.clone.table_ref) | copy-start | bytes 1769476
  2.5 10.8 %all-to-all-start = ((f32[4,56,384]{2,1,0:T(8,128)}), f32[4,56,384]{2,1,0:T(8,128)S(1)}, u32[]{:S(2)}, u32[]{:S(2)}) async-start(f32[4,56,384]{2,1,0:T(8,128)} %tell.1), calls=%async_computation | async-start | bytes 688128 | tf_op jit(solution)/shard_map/all_to_all | solution.py:414
  15.6 19.7 %copy-start.5 = (f32[2,1,4,3,384]{4,2,3,1,0:T(4,128)S(1)}, f32[2,1,4,3,384]{4,2,3,1,0:T(4,128)}, u32[]{:S(2)}) copy-start(f32[2,1,4,3,384]{4,2,3,1,0:T(4,128)} %param.12) | copy-start | bytes 110596
  15.6 19.7 %copy-start.6 = (f32[2,1,4,3,384]{4,2,3,1,0:T(4,128)S(1)}, f32[2,1,4,3,384]{4,2,3,1,0:T(4,128)}, u32[]{:S(2)}) copy-start(f32[2,1,4,3,384]{4,2,3,1,0:T(4,128)} %param.11) | copy-start | bytes 110596
  15.6 19.7 %copy-start.7 = (s32[1,4,3,384]{3,1,2,0:T(4,128)S(1)}, s32[1,4,3,384]{3,1,2,0:T(4,128)}, u32[]{:S(2)}) copy-start(s32[1,4,3,384]{3,1,2,0:T(4,128)} %param.15) | copy-start | bytes 55300
  15.6 53.5 %all-to-all-start.1 = ((f32[1152,2,128]{2,1,0:T(2,128)}), f32[1152,2,128]{2,1,0:T(2,128)S(1)}, u32[]{:S(2)}, u32[]{:S(2)}) async-start(f32[1152,2,128]{2,1,0:T(2,128)} %bitcast.6), calls=%async_computation.1 | async-start | bytes 2359296 | tf_op jit(solution)/shard_map/all_to_all | solution.py:388
  35.9 17.6 %collective-permute-start.2 = (f32[16,384]{1,0:T(8,128)S(1)}, f32[16,384]{1,0:T(8,128)S(1)}, u32[]{:S(2)}, u32[]{:S(2)}) collective-permute-start(f32[16,384]{1,0:T(8,128)S(1)} %get-tuple-element.24), channel_id=1, source_target_pairs={{0,1},{1,2},{2,3},{3,0},{4,5},{5,6},{6,7},{7,4},{8,9},{9,10},{10,1... | collective-permute-start | bytes 73736 | tf_op jit(solution)/shard_map/ppermute | solution.py:435
  38.1 15.4 %collective-permute-start.3 = (f32[16,384]{1,0:T(8,128)S(1)}, f32[16,384]{1,0:T(8,128)S(1)}, u32[]{:S(2)}, u32[]{:S(2)}) collective-permute-start(f32[16,384]{1,0:T(8,128)S(1)} %get-tuple-element.25), channel_id=1, source_target_pairs={{0,2},{1,3},{2,0},{3,1},{4,6},{5,7},{6,4},{7,5},{8,10},{9,11},{10,... | collective-permute-start | bytes 73736 | tf_op jit(solution)/shard_map/ppermute | solution.py:435
  41.8 11.7 %collective-permute-start.4 = (f32[16,384]{1,0:T(8,128)S(1)}, f32[16,384]{1,0:T(8,128)S(1)}, u32[]{:S(2)}, u32[]{:S(2)}) collective-permute-start(f32[16,384]{1,0:T(8,128)S(1)} %get-tuple-element.26), channel_id=1, source_target_pairs={{0,3},{1,0},{2,1},{3,2},{4,7},{5,4},{6,5},{7,6},{8,11},{9,8},{10,9... | collective-permute-start | bytes 73736 | tf_op jit(solution)/shard_map/ppermute | solution.py:435
  44.3 18.2 %collective-permute-start = (f32[4,3,384]{2,1,0:T(4,128)S(1)}, f32[4,3,384]{2,1,0:T(4,128)S(1)}, u32[]{:S(2)}, u32[]{:S(2)}) collective-permute-start(f32[4,3,384]{2,1,0:T(4,128)S(1)} %get-tuple-element.21), channel_id=1, source_target_pairs={{0,4},{4,8},{8,12},{12,16},{16,20},{20,24},{24,28},{28,32},{32,36}... | collective-permute-start | bytes 55304 | tf_op jit(solution)/shard_map/ppermute | solution.py:422
  48.4 14.1 %collective-permute-start.1 = (f32[4,2,384]{2,1,0:T(2,128)S(1)}, f32[4,2,384]{2,1,0:T(2,128)S(1)}, u32[]{:S(2)}, u32[]{:S(2)}) collective-permute-start(f32[4,2,384]{2,1,0:T(2,128)S(1)} %get-tuple-element.22), channel_id=1, source_target_pairs={{4,0},{8,4},{12,8},{16,12},{20,16},{24,20},{28,24},{32,28},{36,32}... | collective-permute-start | bytes 36872 | tf_op jit(solution)/shard_map/ppermute | solution.py:423
  50.4 1.7 %copy-start = (s32[4,384,384]{2,1,0:T(8,128)S(1)}, s32[4,384,384]{2,1,0:T(8,128)}, u32[]{:S(2)}) copy-start(s32[4,384,384]{2,1,0:T(8,128)} %sampling_ref.1) | copy-start | bytes 7077892
  52.0 17.1 %copy-start.3 = (bf16[768,384]{1,0:T(8,128)(2,1)S(1)}, bf16[768,384]{1,0:T(8,128)(2,1)}, u32[]{:S(2)}) copy-start(bf16[768,384]{1,0:T(8,128)(2,1)} %constant.34.clone.forward_ref) | copy-start | bytes 1769476
  52.0 17.1 %copy-start.4 = (bf16[768,384]{1,0:T(8,128)(2,1)S(1)}, bf16[768,384]{1,0:T(8,128)(2,1)}, u32[]{:S(2)}) copy-start(bf16[768,384]{1,0:T(8,128)(2,1)} %constant.35.clone.inverse_ref) | copy-start | bytes 1769476
  71.2 40.6 %copy-start.2 = (bf16[384,768]{1,0:T(8,128)(2,1)S(1)}, bf16[384,768]{1,0:T(8,128)(2,1)}, u32[]{:S(2)}) copy-start(bf16[384,768]{1,0:T(8,128)(2,1)} %constant.36.clone.table_ref) | copy-start | bytes 1769476
  111.8 26.3 %copy-start.8 = (f32[2,1,4,3,384]{4,2,3,1,0:T(4,128)S(1)}, f32[2,1,4,3,384]{4,2,3,1,0:T(4,128)}, u32[]{:S(2)}) copy-start(f32[2,1,4,3,384]{4,2,3,1,0:T(4,128)} %param.10) | copy-start | bytes 110596

commit v7 on v6

--- a/solution.py
+++ b/solution.py
@@ -453,7 +453,9 @@
         [(frames, 8, cols), (slabs, 1, 128)],
         "combine",
     )
-    parts = lax.all_to_all(parts, slab_axes, 0, 0, tiled=True)
+    turned = np.roll(np.arange(slabs).reshape(sizes), [n // 2 for n in sizes[:2]], (0, 1))
+    turned = [int(v) for v in turned.reshape(-1)]
+    parts = lax.all_to_all(parts, slab_axes, 0, 0, axis_index_groups=[turned], tiled=True)
     (applied,) = call(join_kernel, (parts, applied), [applied], "join")
     applied = lax.all_to_all(applied, "coil", 0, 0, tiled=True)
 

time: 140 us -> 138 us (0.986)
  blocking collectives: 65 us -> 63.2 us
    all_to_all x1, blocking collectives: 17.7 us -> 15.9 us  [body(): lax.all_to_all(parts, slab_axes, 0, 0, axis_index_groups=[turned], tiled=...]
where the time goes in v7:
time: 138 us; the launch traced here: 137 us
  blocking collectives  63.2 us (46%)
  starting transfers between devices  38.9 us (28%)
  waiting for transfers between devices  20.7 us (15%)
  Pallas kernels  12 us (9%)
  local copies, waits for them, and re-layouts  1.7 us (1%)
    all_to_all x1, blocking collectives, swap(): return lax.all_to_all(pairs, axis, 0, 0, tiled=True).reshape(values.shape)  40.6 us
    all_to_all x1, starting transfers between devices, swap(): return lax.all_to_all(pairs, axis, 0, 0, tiled=True).reshape(values.shape)  19.6 us
    all_to_all x1, blocking collectives, body(): lax.all_to_all(parts, slab_axes, 0, 0, axis_index_groups=[turned], tiled=...  15.9 us
    pallas_call x10, Pallas kernels, call(): pl.pallas_call(kernel, out_shape=[jax.ShapeDtypeStruct(s, f32) if isinsta...  10.2 us
    ppermute x1, waiting for transfers between devices, body(): after = lax.ppermute(first, slab_axes, [(j, i) for i, j in up])  9.03 us
    ppermute x3, starting transfers between devices, body(): lax.ppermute(other, 'coil', [(i, (i + k) % frames) for i in range(frames)])  8.42 us
    all_to_all x1, blocking collectives, body(): applied = lax.all_to_all(applied, 'coil', 0, 0, tiled=True)  6.74 us
    all_to_all x1, waiting for transfers between devices, body(): lax.all_to_all(tell((sens, d, w), zdim, cols), 'coil', 0, 0, tiled=True)  5.91 us
  transfers between devices with their start and end apart: 7, of which 3 were waited for; matrix products, arithmetic and copies ran while one was open for 0% of the time, Pallas kernels for 2%

profile of v7, /device:TPU:1, one launch (start us, length us, event | category | flops | bytes accessed | tf_op | source)
XLA Modules:
  0.0 137.4 jit_solution(13538431616425921589)
XLA Ops:
  0.6 0.0 copy-start.1
  0.6 1.9 %tell.1 = f32[4,56,384]{2,1,0:T(8,128)} custom-call(bf16[2,8,3,4,384]{4,3,2,1,0:T(4,128)(2,1)} %bitcast.56, f32[2,3,4,384]{3,2,1,0:T(4,128)} %bitcast.48, s32[3,4,384]{2,1,0:T(4,128)} %bitcast.53), custom_call_target="tpu_custom_call" | custom-call | tf_op jit(solution)/shard_map/tell/pallas_call | solution.py:374
  2.5 4.9 %all-to-all-start = ((f32[4,56,384]{2,1,0:T(8,128)}), f32[4,56,384]{2,1,0:T(8,128)S(1)}, u32[]{:S(2)}, u32[]{:S(2)}) async-start(f32[4,56,384]{2,1,0:T(8,128)} %tell.1), calls=%async_computation | async-start | bytes 688128 | tf_op jit(solution)/shard_map/all_to_all | solution.py:414
  7.4 0.0 copy-done.1
  7.4 0.1 table.1.table_ref
  7.5 5.9 %all-to-all-done.all_ref = f32[4,56,384]{2,1,0:T(8,128)S(1)} async-done(((f32[4,56,384]{2,1,0:T(8,128)}), f32[4,56,384]{2,1,0:T(8,128)S(1)}, u32[]{:S(2)}, u32[]{:S(2)}) %all-to-all-start) | async-done | bytes 344096 | tf_op jit(solution)/shard_map/all_to_all | solution.py:414
  13.4 2.2 %images.1 = f32[2304,128]{1,0:T(8,128)} custom-call(f32[4,56,384]{2,1,0:T(8,128)S(1)} %all-to-all-done.all_ref, bf16[768,384]{1,0:T(8,128)(2,1)S(1)} %table.1.table_ref), custom_call_target="tpu_custom_call" | custom-call | tf_op jit(solution)/shard_map/images/pallas_call | solution.py:359
  15.6 0.0 copy-start.5
  15.6 0.0 copy-start.6
  15.6 0.0 copy-start.7
  15.6 19.6 %all-to-all-start.1 = ((f32[1152,2,128]{2,1,0:T(2,128)}), f32[1152,2,128]{2,1,0:T(2,128)S(1)}, u32[]{:S(2)}, u32[]{:S(2)}) async-start(f32[1152,2,128]{2,1,0:T(2,128)} %bitcast.6), calls=%async_computation.1 | async-start | bytes 2359296 | tf_op jit(solution)/shard_map/all_to_all | solution.py:388
  35.2 0.1 pad_add_fusion.place_ref
  35.2 0.0 copy-done.5
  35.2 0.0 copy-done.6
  35.2 0.0 copy-done.7
  35.3 0.6 later.1
  35.9 2.2 %collective-permute-start.2 = (f32[16,384]{1,0:T(8,128)S(1)}, f32[16,384]{1,0:T(8,128)S(1)}, u32[]{:S(2)}, u32[]{:S(2)}) collective-permute-start(f32[16,384]{1,0:T(8,128)S(1)} %get-tuple-element.24), channel_id=1, source_target_pairs={{0,1},{1,2},{2,3},{3,0},{4,5},{5,6},{6,7},{7,4},{8,9},{9,10},{10,1... | collective-permute-start | bytes 73736 | tf_op jit(solution)/shard_map/ppermute | solution.py:435
  38.1 3.7 %collective-permute-start.3 = (f32[16,384]{1,0:T(8,128)S(1)}, f32[16,384]{1,0:T(8,128)S(1)}, u32[]{:S(2)}, u32[]{:S(2)}) collective-permute-start(f32[16,384]{1,0:T(8,128)S(1)} %get-tuple-element.25), channel_id=1, source_target_pairs={{0,2},{1,3},{2,0},{3,1},{4,6},{5,7},{6,4},{7,5},{8,10},{9,11},{10,... | collective-permute-start | bytes 73736 | tf_op jit(solution)/shard_map/ppermute | solution.py:435
  41.8 2.5 %collective-permute-start.4 = (f32[16,384]{1,0:T(8,128)S(1)}, f32[16,384]{1,0:T(8,128)S(1)}, u32[]{:S(2)}, u32[]{:S(2)}) collective-permute-start(f32[16,384]{1,0:T(8,128)S(1)} %get-tuple-element.26), channel_id=1, source_target_pairs={{0,3},{1,0},{2,1},{3,2},{4,7},{5,4},{6,5},{7,6},{8,11},{9,8},{10,9... | collective-permute-start | bytes 73736 | tf_op jit(solution)/shard_map/ppermute | solution.py:435
  44.3 4.1 %collective-permute-start = (f32[4,3,384]{2,1,0:T(4,128)S(1)}, f32[4,3,384]{2,1,0:T(4,128)S(1)}, u32[]{:S(2)}, u32[]{:S(2)}) collective-permute-start(f32[4,3,384]{2,1,0:T(4,128)S(1)} %get-tuple-element.21), channel_id=1, source_target_pairs={{0,4},{4,8},{8,12},{12,16},{16,20},{20,24},{24,28},{28,32},{32,36}... | collective-permute-start | bytes 55304 | tf_op jit(solution)/shard_map/ppermute | solution.py:422
  48.4 1.9 %collective-permute-start.1 = (f32[4,2,384]{2,1,0:T(2,128)S(1)}, f32[4,2,384]{2,1,0:T(2,128)S(1)}, u32[]{:S(2)}, u32[]{:S(2)}) collective-permute-start(f32[4,2,384]{2,1,0:T(2,128)S(1)} %get-tuple-element.22), channel_id=1, source_target_pairs={{4,0},{8,4},{12,8},{16,12},{20,16},{24,20},{28,24},{32,28},{36,32}... | collective-permute-start | bytes 36872 | tf_op jit(solution)/shard_map/ppermute | solution.py:423
  50.4 0.0 copy-start
  50.4 1.7 %copy-done = s32[4,384,384]{2,1,0:T(8,128)S(1)} copy-done((s32[4,384,384]{2,1,0:T(8,128)S(1)}, s32[4,384,384]{2,1,0:T(8,128)}, u32[]{:S(2)}) %copy-start) | copy-done | bytes 2359320
  52.0 0.0 copy-start.3
  52.0 0.0 copy-start.4
  52.0 1.4 %mask.1.mask_ref = f32[3,384,128]{2,1,0:T(8,128)S(1)} custom-call(s32[4]{0:T(128)S(1)} %pad_add_fusion.place_ref, s32[4,384,384]{2,1,0:T(8,128)S(1)} %copy-done), custom_call_target="tpu_custom_call" | custom-call | tf_op jit(solution)/shard_map/mask/pallas_call | solution.py:359
  53.5 0.0 collective-permute-done.2.refs_1_
  53.5 0.0 collective-permute-done.3.refs_2_
  53.5 0.0 collective-permute-done.4.refs_3_
  53.5 9.0 %collective-permute-done.1.after_ref = f32[4,2,384]{2,1,0:T(2,128)S(1)} collective-permute-done((f32[4,2,384]{2,1,0:T(2,128)S(1)}, f32[4,2,384]{2,1,0:T(2,128)S(1)}, u32[]{:S(2)}, u32[]{:S(2)}) %collective-permute-start.1) | collective-permute-done | bytes 12320 | tf_op jit(solution)/shard_map/ppermute | solution.py:423
  62.5 0.0 collective-permute-done.before_ref
  62.5 0.8 smooth.1
  63.4 5.7 %all-to-all-done.1 = f32[1152,2,128]{2,1,0:T(2,128)S(1)} async-done(((f32[1152,2,128]{2,1,0:T(2,128)}), f32[1152,2,128]{2,1,0:T(2,128)S(1)}, u32[]{:S(2)}, u32[]{:S(2)}) %all-to-all-start.1) | async-done | bytes 1179680 | tf_op jit(solution)/shard_map/all_to_all | solution.py:388
  69.1 0.0 copy-done.3
  69.1 0.0 copy-done.4
  69.1 2.1 %middle.1 = f32[2304,128]{1,0:T(8,128)S(1)} custom-call(f32[2304,128]{1,0:T(8,128)S(1)} %bitcast.46, f32[3,384,128]{2,1,0:T(8,128)S(1)} %mask.1.mask_ref, bf16[768,384]{1,0:T(8,128)(2,1)S(1)} %copy-done.3, bf16[768,384]{1,0:T(8,128)(2,1)S(1)} %copy-done.4), custom_call_target="tpu_custom_call" | custom-call | tf_op jit(solution)/shard_map/middle/pallas_call | solution.py:359
  71.2 0.0 copy-start.2
  71.2 40.6 %all_to_all.25 = f32[1152,2,128]{2,1,0:T(2,128)S(1)} all-to-all(f32[1152,2,128]{2,1,0:T(2,128)S(1)} %bitcast.47), channel_id=1, replica_groups=mesh['z'=8,'y'=8,'core'=2,'coil'=4] {'z','core','y'}, dimensions={0} | all-to-all | bytes 2359296 | tf_op jit(solution)/shard_map/all_to_all | solution.py:388
  111.8 0.0 copy-done.2
  111.8 0.0 copy-start.8
  111.8 1.6 %combine.1 = (f32[4,8,384]{2,1,0:T(8,128)S(1)}, f32[128,1,128]{2,1,0:T(1,128)S(1)}) custom-call(f32[2304,128]{1,0:T(8,128)S(1)} %bitcast.45, f32[4,56,384]{2,1,0:T(8,128)S(1)} %all-to-all-done.all_ref, f32[4,6,384]{2,1,0:T(8,128)S(1)} %get-tuple-element.30.smooth_ref, f32[4,6,384]{2,1,0:T(8,128)S(1)} %get-tuple-element.31.residual_ref, ...), custom_call_target="tpu_custom_call" | custom-call | tf_op jit(solution)/shard_map/combine/pallas_call | solution.py:359
  113.4 15.9 %all_to_all.26.parts_ref = f32[128,1,128]{2,1,0:T(1,128)S(1)} all-to-all(f32[128,1,128]{2,1,0:T(1,128)S(1)} %get-tuple-element.32), channel_id=1, replica_groups={{288,292,296,300,304,308,312,316,256,260,264,268,272,276,280,284,352,35..., dimensions={0} | all-to-all | bytes 131072 | tf_op jit(solution)/shard_map/all_to_all | solution.py:458
  129.3 0.3 join.1
  129.6 6.7 %all_to_all.27.all_ref = f32[4,8,384]{2,1,0:T(8,128)S(1)} all-to-all(f32[4,8,384]{2,1,0:T(8,128)S(1)} %join.1), channel_id=1, replica_groups=mesh['z'=8,'y'=8,'core'=2,'coil'=4] {'coil'}, dimensions={0} | all-to-all | bytes 98304 | tf_op jit(solution)/shard_map/all_to_all | solution.py:460
  136.4 0.0 copy-done.8
  136.4 1.0 finish.1
  (1 shorter events, 0.0 us)
Async XLA Ops:
  0.6 6.8 %copy-start.1 = (bf16[768,384]{1,0:T(8,128)(2,1)S(1)}, bf16[768,384]{1,0:T(8,128)(2,1)}, u32[]{:S(2)}) copy-start(bf16[768,384]{1,0:T(8,128)(2,1)} %constant.33.clone.table_ref) | copy-start | bytes 1769476
  2.5 10.8 %all-to-all-start = ((f32[4,56,384]{2,1,0:T(8,128)}), f32[4,56,384]{2,1,0:T(8,128)S(1)}, u32[]{:S(2)}, u32[]{:S(2)}) async-start(f32[4,56,384]{2,1,0:T(8,128)} %tell.1), calls=%async_computation | async-start | bytes 688128 | tf_op jit(solution)/shard_map/all_to_all | solution.py:414
  15.6 19.7 %copy-start.5 = (f32[2,1,4,3,384]{4,2,3,1,0:T(4,128)S(1)}, f32[2,1,4,3,384]{4,2,3,1,0:T(4,128)}, u32[]{:S(2)}) copy-start(f32[2,1,4,3,384]{4,2,3,1,0:T(4,128)} %param.12) | copy-start | bytes 110596
  15.6 19.7 %copy-start.6 = (f32[2,1,4,3,384]{4,2,3,1,0:T(4,128)S(1)}, f32[2,1,4,3,384]{4,2,3,1,0:T(4,128)}, u32[]{:S(2)}) copy-start(f32[2,1,4,3,384]{4,2,3,1,0:T(4,128)} %param.11) | copy-start | bytes 110596
  15.6 19.7 %copy-start.7 = (s32[1,4,3,384]{3,1,2,0:T(4,128)S(1)}, s32[1,4,3,384]{3,1,2,0:T(4,128)}, u32[]{:S(2)}) copy-start(s32[1,4,3,384]{3,1,2,0:T(4,128)} %param.15) | copy-start | bytes 55300
  15.6 53.5 %all-to-all-start.1 = ((f32[1152,2,128]{2,1,0:T(2,128)}), f32[1152,2,128]{2,1,0:T(2,128)S(1)}, u32[]{:S(2)}, u32[]{:S(2)}) async-start(f32[1152,2,128]{2,1,0:T(2,128)} %bitcast.6), calls=%async_computation.1 | async-start | bytes 2359296 | tf_op jit(solution)/shard_map/all_to_all | solution.py:388
  35.9 17.6 %collective-permute-start.2 = (f32[16,384]{1,0:T(8,128)S(1)}, f32[16,384]{1,0:T(8,128)S(1)}, u32[]{:S(2)}, u32[]{:S(2)}) collective-permute-start(f32[16,384]{1,0:T(8,128)S(1)} %get-tuple-element.24), channel_id=1, source_target_pairs={{0,1},{1,2},{2,3},{3,0},{4,5},{5,6},{6,7},{7,4},{8,9},{9,10},{10,1... | collective-permute-start | bytes 73736 | tf_op jit(solution)/shard_map/ppermute | solution.py:435
  38.1 15.4 %collective-permute-start.3 = (f32[16,384]{1,0:T(8,128)S(1)}, f32[16,384]{1,0:T(8,128)S(1)}, u32[]{:S(2)}, u32[]{:S(2)}) collective-permute-start(f32[16,384]{1,0:T(8,128)S(1)} %get-tuple-element.25), channel_id=1, source_target_pairs={{0,2},{1,3},{2,0},{3,1},{4,6},{5,7},{6,4},{7,5},{8,10},{9,11},{10,... | collective-permute-start | bytes 73736 | tf_op jit(solution)/shard_map/ppermute | solution.py:435
  41.8 11.7 %collective-permute-start.4 = (f32[16,384]{1,0:T(8,128)S(1)}, f32[16,384]{1,0:T(8,128)S(1)}, u32[]{:S(2)}, u32[]{:S(2)}) collective-permute-start(f32[16,384]{1,0:T(8,128)S(1)} %get-tuple-element.26), channel_id=1, source_target_pairs={{0,3},{1,0},{2,1},{3,2},{4,7},{5,4},{6,5},{7,6},{8,11},{9,8},{10,9... | collective-permute-start | bytes 73736 | tf_op jit(solution)/shard_map/ppermute | solution.py:435
  44.3 18.2 %collective-permute-start = (f32[4,3,384]{2,1,0:T(4,128)S(1)}, f32[4,3,384]{2,1,0:T(4,128)S(1)}, u32[]{:S(2)}, u32[]{:S(2)}) collective-permute-start(f32[4,3,384]{2,1,0:T(4,128)S(1)} %get-tuple-element.21), channel_id=1, source_target_pairs={{0,4},{4,8},{8,12},{12,16},{16,20},{20,24},{24,28},{28,32},{32,36}... | collective-permute-start | bytes 55304 | tf_op jit(solution)/shard_map/ppermute | solution.py:422
  48.4 14.1 %collective-permute-start.1 = (f32[4,2,384]{2,1,0:T(2,128)S(1)}, f32[4,2,384]{2,1,0:T(2,128)S(1)}, u32[]{:S(2)}, u32[]{:S(2)}) collective-permute-start(f32[4,2,384]{2,1,0:T(2,128)S(1)} %get-tuple-element.22), channel_id=1, source_target_pairs={{4,0},{8,4},{12,8},{16,12},{20,16},{24,20},{28,24},{32,28},{36,32}... | collective-permute-start | bytes 36872 | tf_op jit(solution)/shard_map/ppermute | solution.py:423
  50.4 1.7 %copy-start = (s32[4,384,384]{2,1,0:T(8,128)S(1)}, s32[4,384,384]{2,1,0:T(8,128)}, u32[]{:S(2)}) copy-start(s32[4,384,384]{2,1,0:T(8,128)} %sampling_ref.1) | copy-start | bytes 7077892
  52.0 17.1 %copy-start.3 = (bf16[768,384]{1,0:T(8,128)(2,1)S(1)}, bf16[768,384]{1,0:T(8,128)(2,1)}, u32[]{:S(2)}) copy-start(bf16[768,384]{1,0:T(8,128)(2,1)} %constant.34.clone.forward_ref) | copy-start | bytes 1769476
  52.0 17.1 %copy-start.4 = (bf16[768,384]{1,0:T(8,128)(2,1)S(1)}, bf16[768,384]{1,0:T(8,128)(2,1)}, u32[]{:S(2)}) copy-start(bf16[768,384]{1,0:T(8,128)(2,1)} %constant.35.clone.inverse_ref) | copy-start | bytes 1769476
  71.2 40.6 %copy-start.2 = (bf16[384,768]{1,0:T(8,128)(2,1)S(1)}, bf16[384,768]{1,0:T(8,128)(2,1)}, u32[]{:S(2)}) copy-start(bf16[384,768]{1,0:T(8,128)(2,1)} %constant.36.clone.table_ref) | copy-start | bytes 1769476
  111.8 24.5 %copy-start.8 = (f32[2,1,4,3,384]{4,2,3,1,0:T(4,128)S(1)}, f32[2,1,4,3,384]{4,2,3,1,0:T(4,128)}, u32[]{:S(2)}) copy-start(f32[2,1,4,3,384]{4,2,3,1,0:T(4,128)} %param.10) | copy-start | bytes 110596

commit v8 on v7

--- a/solution.py
+++ b/solution.py
@@ -454,7 +454,7 @@
         "combine",
     )
     turned = np.roll(np.arange(slabs).reshape(sizes), [n // 2 for n in sizes[:2]], (0, 1))
-    turned = [int(v) for v in turned.reshape(-1)]
+    turned = [int(v) for v in turned[:, :, ::-1].reshape(-1)]
     parts = lax.all_to_all(parts, slab_axes, 0, 0, axis_index_groups=[turned], tiled=True)
     (applied,) = call(join_kernel, (parts, applied), [applied], "join")
     applied = lax.all_to_all(applied, "coil", 0, 0, tiled=True)

time: 138 us -> 138 us (level)
  no operation moved by 1% of the time
where the time goes in v8:
time: 138 us; the launch traced here: 137 us
  blocking collectives  62.9 us (46%)
  starting transfers between devices  38.9 us (28%)
  waiting for transfers between devices  20.7 us (15%)
  Pallas kernels  12 us (9%)
  local copies, waits for them, and re-layouts  1.7 us (1%)
    all_to_all x1, blocking collectives, swap(): return lax.all_to_all(pairs, axis, 0, 0, tiled=True).reshape(values.shape)  40.6 us
    all_to_all x1, starting transfers between devices, swap(): return lax.all_to_all(pairs, axis, 0, 0, tiled=True).reshape(values.shape)  19.6 us
    all_to_all x1, blocking collectives, body(): lax.all_to_all(parts, slab_axes, 0, 0, axis_index_groups=[turned], tiled=...  15.5 us
    pallas_call x10, Pallas kernels, call(): pl.pallas_call(kernel, out_shape=[jax.ShapeDtypeStruct(s, f32) if isinsta...  10.2 us
    ppermute x1, waiting for transfers between devices, body(): after = lax.ppermute(first, slab_axes, [(j, i) for i, j in up])  9.03 us
    ppermute x3, starting transfers between devices, body(): lax.ppermute(other, 'coil', [(i, (i + k) % frames) for i in range(frames)])  8.42 us
    all_to_all x1, blocking collectives, body(): applied = lax.all_to_all(applied, 'coil', 0, 0, tiled=True)  6.74 us
    all_to_all x1, waiting for transfers between devices, body(): lax.all_to_all(tell((sens, d, w), zdim, cols), 'coil', 0, 0, tiled=True)  5.91 us
  transfers between devices with their start and end apart: 7, of which 3 were waited for; matrix products, arithmetic and copies ran while one was open for 0% of the time, Pallas kernels for 2%

profile of v8, /device:TPU:1, one launch (start us, length us, event | category | flops | bytes accessed | tf_op | source)
XLA Modules:
  0.0 137.0 jit_solution(3027894696811482646)
XLA Ops:
  0.6 0.0 copy-start.1
  0.6 1.9 %tell.1 = f32[4,56,384]{2,1,0:T(8,128)} custom-call(bf16[2,8,3,4,384]{4,3,2,1,0:T(4,128)(2,1)} %bitcast.56, f32[2,3,4,384]{3,2,1,0:T(4,128)} %bitcast.48, s32[3,4,384]{2,1,0:T(4,128)} %bitcast.53), custom_call_target="tpu_custom_call" | custom-call | tf_op jit(solution)/shard_map/tell/pallas_call | solution.py:374
  2.5 4.9 %all-to-all-start = ((f32[4,56,384]{2,1,0:T(8,128)}), f32[4,56,384]{2,1,0:T(8,128)S(1)}, u32[]{:S(2)}, u32[]{:S(2)}) async-start(f32[4,56,384]{2,1,0:T(8,128)} %tell.1), calls=%async_computation | async-start | bytes 688128 | tf_op jit(solution)/shard_map/all_to_all | solution.py:414
  7.4 0.0 copy-done.1
  7.4 0.1 table.1.table_ref
  7.5 5.9 %all-to-all-done.all_ref = f32[4,56,384]{2,1,0:T(8,128)S(1)} async-done(((f32[4,56,384]{2,1,0:T(8,128)}), f32[4,56,384]{2,1,0:T(8,128)S(1)}, u32[]{:S(2)}, u32[]{:S(2)}) %all-to-all-start) | async-done | bytes 344096 | tf_op jit(solution)/shard_map/all_to_all | solution.py:414
  13.4 2.2 %images.1 = f32[2304,128]{1,0:T(8,128)} custom-call(f32[4,56,384]{2,1,0:T(8,128)S(1)} %all-to-all-done.all_ref, bf16[768,384]{1,0:T(8,128)(2,1)S(1)} %table.1.table_ref), custom_call_target="tpu_custom_call" | custom-call | tf_op jit(solution)/shard_map/images/pallas_call | solution.py:359
  15.6 0.0 copy-start.5
  15.6 0.0 copy-start.6
  15.6 0.0 copy-start.7
  15.6 19.6 %all-to-all-start.1 = ((f32[1152,2,128]{2,1,0:T(2,128)}), f32[1152,2,128]{2,1,0:T(2,128)S(1)}, u32[]{:S(2)}, u32[]{:S(2)}) async-start(f32[1152,2,128]{2,1,0:T(2,128)} %bitcast.6), calls=%async_computation.1 | async-start | bytes 2359296 | tf_op jit(solution)/shard_map/all_to_all | solution.py:388
  35.2 0.1 pad_add_fusion.place_ref
  35.2 0.0 copy-done.5
  35.2 0.0 copy-done.6
  35.2 0.0 copy-done.7
  35.3 0.6 later.1
  35.9 2.2 %collective-permute-start.2 = (f32[16,384]{1,0:T(8,128)S(1)}, f32[16,384]{1,0:T(8,128)S(1)}, u32[]{:S(2)}, u32[]{:S(2)}) collective-permute-start(f32[16,384]{1,0:T(8,128)S(1)} %get-tuple-element.24), channel_id=1, source_target_pairs={{0,1},{1,2},{2,3},{3,0},{4,5},{5,6},{6,7},{7,4},{8,9},{9,10},{10,1... | collective-permute-start | bytes 73736 | tf_op jit(solution)/shard_map/ppermute | solution.py:435
  38.1 3.7 %collective-permute-start.3 = (f32[16,384]{1,0:T(8,128)S(1)}, f32[16,384]{1,0:T(8,128)S(1)}, u32[]{:S(2)}, u32[]{:S(2)}) collective-permute-start(f32[16,384]{1,0:T(8,128)S(1)} %get-tuple-element.25), channel_id=1, source_target_pairs={{0,2},{1,3},{2,0},{3,1},{4,6},{5,7},{6,4},{7,5},{8,10},{9,11},{10,... | collective-permute-start | bytes 73736 | tf_op jit(solution)/shard_map/ppermute | solution.py:435
  41.8 2.5 %collective-permute-start.4 = (f32[16,384]{1,0:T(8,128)S(1)}, f32[16,384]{1,0:T(8,128)S(1)}, u32[]{:S(2)}, u32[]{:S(2)}) collective-permute-start(f32[16,384]{1,0:T(8,128)S(1)} %get-tuple-element.26), channel_id=1, source_target_pairs={{0,3},{1,0},{2,1},{3,2},{4,7},{5,4},{6,5},{7,6},{8,11},{9,8},{10,9... | collective-permute-start | bytes 73736 | tf_op jit(solution)/shard_map/ppermute | solution.py:435
  44.3 4.1 %collective-permute-start = (f32[4,3,384]{2,1,0:T(4,128)S(1)}, f32[4,3,384]{2,1,0:T(4,128)S(1)}, u32[]{:S(2)}, u32[]{:S(2)}) collective-permute-start(f32[4,3,384]{2,1,0:T(4,128)S(1)} %get-tuple-element.21), channel_id=1, source_target_pairs={{0,4},{4,8},{8,12},{12,16},{16,20},{20,24},{24,28},{28,32},{32,36}... | collective-permute-start | bytes 55304 | tf_op jit(solution)/shard_map/ppermute | solution.py:422
  48.4 1.9 %collective-permute-start.1 = (f32[4,2,384]{2,1,0:T(2,128)S(1)}, f32[4,2,384]{2,1,0:T(2,128)S(1)}, u32[]{:S(2)}, u32[]{:S(2)}) collective-permute-start(f32[4,2,384]{2,1,0:T(2,128)S(1)} %get-tuple-element.22), channel_id=1, source_target_pairs={{4,0},{8,4},{12,8},{16,12},{20,16},{24,20},{28,24},{32,28},{36,32}... | collective-permute-start | bytes 36872 | tf_op jit(solution)/shard_map/ppermute | solution.py:423
  50.4 0.0 copy-start
  50.4 1.7 %copy-done = s32[4,384,384]{2,1,0:T(8,128)S(1)} copy-done((s32[4,384,384]{2,1,0:T(8,128)S(1)}, s32[4,384,384]{2,1,0:T(8,128)}, u32[]{:S(2)}) %copy-start) | copy-done | bytes 2359320
  52.0 0.0 copy-start.3
  52.0 0.0 copy-start.4
  52.0 1.4 %mask.1.mask_ref = f32[3,384,128]{2,1,0:T(8,128)S(1)} custom-call(s32[4]{0:T(128)S(1)} %pad_add_fusion.place_ref, s32[4,384,384]{2,1,0:T(8,128)S(1)} %copy-done), custom_call_target="tpu_custom_call" | custom-call | tf_op jit(solution)/shard_map/mask/pallas_call | solution.py:359
  53.5 0.0 collective-permute-done.2.refs_1_
  53.5 0.0 collective-permute-done.3.refs_2_
  53.5 0.0 collective-permute-done.4.refs_3_
  53.5 9.0 %collective-permute-done.1.after_ref = f32[4,2,384]{2,1,0:T(2,128)S(1)} collective-permute-done((f32[4,2,384]{2,1,0:T(2,128)S(1)}, f32[4,2,384]{2,1,0:T(2,128)S(1)}, u32[]{:S(2)}, u32[]{:S(2)}) %collective-permute-start.1) | collective-permute-done | bytes 12320 | tf_op jit(solution)/shard_map/ppermute | solution.py:423
  62.5 0.0 collective-permute-done.before_ref
  62.5 0.8 smooth.1
  63.4 5.7 %all-to-all-done.1 = f32[1152,2,128]{2,1,0:T(2,128)S(1)} async-done(((f32[1152,2,128]{2,1,0:T(2,128)}), f32[1152,2,128]{2,1,0:T(2,128)S(1)}, u32[]{:S(2)}, u32[]{:S(2)}) %all-to-all-start.1) | async-done | bytes 1179680 | tf_op jit(solution)/shard_map/all_to_all | solution.py:388
  69.1 0.0 copy-done.3
  69.1 0.0 copy-done.4
  69.1 2.1 %middle.1 = f32[2304,128]{1,0:T(8,128)S(1)} custom-call(f32[2304,128]{1,0:T(8,128)S(1)} %bitcast.46, f32[3,384,128]{2,1,0:T(8,128)S(1)} %mask.1.mask_ref, bf16[768,384]{1,0:T(8,128)(2,1)S(1)} %copy-done.3, bf16[768,384]{1,0:T(8,128)(2,1)S(1)} %copy-done.4), custom_call_target="tpu_custom_call" | custom-call | tf_op jit(solution)/shard_map/middle/pallas_call | solution.py:359
  71.2 0.0 copy-start.2
  71.2 40.6 %all_to_all.25 = f32[1152,2,128]{2,1,0:T(2,128)S(1)} all-to-all(f32[1152,2,128]{2,1,0:T(2,128)S(1)} %bitcast.47), channel_id=1, replica_groups=mesh['z'=8,'y'=8,'core'=2,'coil'=4] {'z','core','y'}, dimensions={0} | all-to-all | bytes 2359296 | tf_op jit(solution)/shard_map/all_to_all | solution.py:388
  111.8 0.0 copy-done.2
  111.8 0.0 copy-start.8
  111.8 1.6 %combine.1 = (f32[4,8,384]{2,1,0:T(8,128)S(1)}, f32[128,1,128]{2,1,0:T(1,128)S(1)}) custom-call(f32[2304,128]{1,0:T(8,128)S(1)} %bitcast.45, f32[4,56,384]{2,1,0:T(8,128)S(1)} %all-to-all-done.all_ref, f32[4,6,384]{2,1,0:T(8,128)S(1)} %get-tuple-element.30.smooth_ref, f32[4,6,384]{2,1,0:T(8,128)S(1)} %get-tuple-element.31.residual_ref, ...), custom_call_target="tpu_custom_call" | custom-call | tf_op jit(solution)/shard_map/combine/pallas_call | solution.py:359
  113.4 15.5 %all_to_all.26.parts_ref = f32[128,1,128]{2,1,0:T(1,128)S(1)} all-to-all(f32[128,1,128]{2,1,0:T(1,128)S(1)} %get-tuple-element.32), channel_id=1, replica_groups={{292,288,300,296,308,304,316,312,260,256,268,264,276,272,284,280,356,35..., dimensions={0} | all-to-all | bytes 131072 | tf_op jit(solution)/shard_map/all_to_all | solution.py:458
  128.9 0.3 join.1
  129.2 6.7 %all_to_all.27.all_ref = f32[4,8,384]{2,1,0:T(8,128)S(1)} all-to-all(f32[4,8,384]{2,1,0:T(8,128)S(1)} %join.1), channel_id=1, replica_groups=mesh['z'=8,'y'=8,'core'=2,'coil'=4] {'coil'}, dimensions={0} | all-to-all | bytes 98304 | tf_op jit(solution)/shard_map/all_to_all | solution.py:460
  136.0 0.0 copy-done.8
  136.0 1.0 finish.1
  (1 shorter events, 0.0 us)
Async XLA Ops:
  0.6 6.8 %copy-start.1 = (bf16[768,384]{1,0:T(8,128)(2,1)S(1)}, bf16[768,384]{1,0:T(8,128)(2,1)}, u32[]{:S(2)}) copy-start(bf16[768,384]{1,0:T(8,128)(2,1)} %constant.33.clone.table_ref) | copy-start | bytes 1769476
  2.5 10.8 %all-to-all-start = ((f32[4,56,384]{2,1,0:T(8,128)}), f32[4,56,384]{2,1,0:T(8,128)S(1)}, u32[]{:S(2)}, u32[]{:S(2)}) async-start(f32[4,56,384]{2,1,0:T(8,128)} %tell.1), calls=%async_computation | async-start | bytes 688128 | tf_op jit(solution)/shard_map/all_to_all | solution.py:414
  15.6 19.7 %copy-start.5 = (f32[2,1,4,3,384]{4,2,3,1,0:T(4,128)S(1)}, f32[2,1,4,3,384]{4,2,3,1,0:T(4,128)}, u32[]{:S(2)}) copy-start(f32[2,1,4,3,384]{4,2,3,1,0:T(4,128)} %param.12) | copy-start | bytes 110596
  15.6 19.7 %copy-start.6 = (f32[2,1,4,3,384]{4,2,3,1,0:T(4,128)S(1)}, f32[2,1,4,3,384]{4,2,3,1,0:T(4,128)}, u32[]{:S(2)}) copy-start(f32[2,1,4,3,384]{4,2,3,1,0:T(4,128)} %param.11) | copy-start | bytes 110596
  15.6 19.7 %copy-start.7 = (s32[1,4,3,384]{3,1,2,0:T(4,128)S(1)}, s32[1,4,3,384]{3,1,2,0:T(4,128)}, u32[]{:S(2)}) copy-start(s32[1,4,3,384]{3,1,2,0:T(4,128)} %param.15) | copy-start | bytes 55300
  15.6 53.5 %all-to-all-start.1 = ((f32[1152,2,128]{2,1,0:T(2,128)}), f32[1152,2,128]{2,1,0:T(2,128)S(1)}, u32[]{:S(2)}, u32[]{:S(2)}) async-start(f32[1152,2,128]{2,1,0:T(2,128)} %bitcast.6), calls=%async_computation.1 | async-start | bytes 2359296 | tf_op jit(solution)/shard_map/all_to_all | solution.py:388
  35.9 17.6 %collective-permute-start.2 = (f32[16,384]{1,0:T(8,128)S(1)}, f32[16,384]{1,0:T(8,128)S(1)}, u32[]{:S(2)}, u32[]{:S(2)}) collective-permute-start(f32[16,384]{1,0:T(8,128)S(1)} %get-tuple-element.24), channel_id=1, source_target_pairs={{0,1},{1,2},{2,3},{3,0},{4,5},{5,6},{6,7},{7,4},{8,9},{9,10},{10,1... | collective-permute-start | bytes 73736 | tf_op jit(solution)/shard_map/ppermute | solution.py:435
  38.1 15.4 %collective-permute-start.3 = (f32[16,384]{1,0:T(8,128)S(1)}, f32[16,384]{1,0:T(8,128)S(1)}, u32[]{:S(2)}, u32[]{:S(2)}) collective-permute-start(f32[16,384]{1,0:T(8,128)S(1)} %get-tuple-element.25), channel_id=1, source_target_pairs={{0,2},{1,3},{2,0},{3,1},{4,6},{5,7},{6,4},{7,5},{8,10},{9,11},{10,... | collective-permute-start | bytes 73736 | tf_op jit(solution)/shard_map/ppermute | solution.py:435
  41.8 11.7 %collective-permute-start.4 = (f32[16,384]{1,0:T(8,128)S(1)}, f32[16,384]{1,0:T(8,128)S(1)}, u32[]{:S(2)}, u32[]{:S(2)}) collective-permute-start(f32[16,384]{1,0:T(8,128)S(1)} %get-tuple-element.26), channel_id=1, source_target_pairs={{0,3},{1,0},{2,1},{3,2},{4,7},{5,4},{6,5},{7,6},{8,11},{9,8},{10,9... | collective-permute-start | bytes 73736 | tf_op jit(solution)/shard_map/ppermute | solution.py:435
  44.3 18.2 %collective-permute-start = (f32[4,3,384]{2,1,0:T(4,128)S(1)}, f32[4,3,384]{2,1,0:T(4,128)S(1)}, u32[]{:S(2)}, u32[]{:S(2)}) collective-permute-start(f32[4,3,384]{2,1,0:T(4,128)S(1)} %get-tuple-element.21), channel_id=1, source_target_pairs={{0,4},{4,8},{8,12},{12,16},{16,20},{20,24},{24,28},{28,32},{32,36}... | collective-permute-start | bytes 55304 | tf_op jit(solution)/shard_map/ppermute | solution.py:422
  48.4 14.1 %collective-permute-start.1 = (f32[4,2,384]{2,1,0:T(2,128)S(1)}, f32[4,2,384]{2,1,0:T(2,128)S(1)}, u32[]{:S(2)}, u32[]{:S(2)}) collective-permute-start(f32[4,2,384]{2,1,0:T(2,128)S(1)} %get-tuple-element.22), channel_id=1, source_target_pairs={{4,0},{8,4},{12,8},{16,12},{20,16},{24,20},{28,24},{32,28},{36,32}... | collective-permute-start | bytes 36872 | tf_op jit(solution)/shard_map/ppermute | solution.py:423
  50.4 1.7 %copy-start = (s32[4,384,384]{2,1,0:T(8,128)S(1)}, s32[4,384,384]{2,1,0:T(8,128)}, u32[]{:S(2)}) copy-start(s32[4,384,384]{2,1,0:T(8,128)} %sampling_ref.1) | copy-start | bytes 7077892
  52.0 17.1 %copy-start.3 = (bf16[768,384]{1,0:T(8,128)(2,1)S(1)}, bf16[768,384]{1,0:T(8,128)(2,1)}, u32[]{:S(2)}) copy-start(bf16[768,384]{1,0:T(8,128)(2,1)} %constant.34.clone.forward_ref) | copy-start | bytes 1769476
  52.0 17.1 %copy-start.4 = (bf16[768,384]{1,0:T(8,128)(2,1)S(1)}, bf16[768,384]{1,0:T(8,128)(2,1)}, u32[]{:S(2)}) copy-start(bf16[768,384]{1,0:T(8,128)(2,1)} %constant.35.clone.inverse_ref) | copy-start | bytes 1769476
  71.2 40.6 %copy-start.2 = (bf16[384,768]{1,0:T(8,128)(2,1)S(1)}, bf16[384,768]{1,0:T(8,128)(2,1)}, u32[]{:S(2)}) copy-start(bf16[384,768]{1,0:T(8,128)(2,1)} %constant.36.clone.table_ref) | copy-start | bytes 1769476
  111.8 24.2 %copy-start.8 = (f32[2,1,4,3,384]{4,2,3,1,0:T(4,128)S(1)}, f32[2,1,4,3,384]{4,2,3,1,0:T(4,128)}, u32[]{:S(2)}) copy-start(f32[2,1,4,3,384]{4,2,3,1,0:T(4,128)} %param.10) | copy-start | bytes 110596
